TPU v7x, 512 devices: a whole 4x8x8 slice. The times are simulated.
512 devices in a mesh: vtx: 64 (over y, z_lo, core), col: 8 (over z_hi, x).
Axes of the slice: x: 4, y: 8, z: 8 (z_hi: 2, z_lo: 4; z = z_hi * 4 + z_lo), core: 2. Of those that a mesh axis runs over, the one named last changes fastest.
Arguments:
- features: bfloat16 [128, 65536], P('col', 'vtx'), may hold values from -6 to 6
- tile_values: bfloat16 [4096, 128, 128], P('vtx'), may hold values from 0 to 1
- tile_source: int32 [4096], P('vtx'), may hold values from 0 to 7
- tile_dest: int32 [4096], P('vtx'), may hold values from 0 to 511, as said below
- tile_count: int32 [64], P('vtx'), may hold values from 8 to 64, as said below
- degree: int32 [65536], P('vtx'), may hold values from 8 to 64
- w_self: bfloat16 [128, 256], replicated, may hold values from -0.5 to 0.5
- w_neigh: bfloat16 [128, 256], replicated, may hold values from -0.5 to 0.5
- bias: float32 [256], replicated, may hold values from -3 to 3
- cotangent: bfloat16 [256, 65536], P(None, ('vtx', 'col')), may hold values from -6 to 6
Outputs:
- hidden: bfloat16 [256, 65536], P(None, ('vtx', 'col'))
- grad_x: bfloat16 [128, 65536], P('col', 'vtx')
- grad_self: float32 [128, 256], replicated
- grad_neigh: float32 [128, 256], replicated
- grad_bias: float32 [256], replicated
Inputs may be any that keep to these rules, and one draw needn't show every extreme that they name: Index v of vtx uses its first tile_count[v] slots; the others are ignored. Some index uses all 64 slots in every draw. `tile_dest`: among the first 32 slots of one index of vtx, and likewise among its last 32, at most 2 have destination blocks at any one index j of vtx (blocks j * 8 to (j + 1) * 8 - 1); this most is reached.
All inputs are finite; a program needn't handle non-finite values.
Results may differ from a plain program's by a relative error of at most 0.007.
Values may be sent and summed in bfloat16 or wider, within the bound.
No kernel may reach another device: no remote copies, remote signals or barrier semaphores. Data moves between devices by JAX's collectives and lax.ppermute only.
A program may use at most 64 MiB of HBM per device.

v0:
```python
import jax
import jax.numpy as jnp
from jax import lax
from jax.sharding import PartitionSpec as P

TB = 128
TILES_DEV = 64


epsilon = 1e-06
tile_batch = 8


def normalized(summed):
    return summed / jnp.sqrt(jnp.mean(summed * summed) + epsilon)


def silu_slope(preact):
    sigma = jax.nn.sigmoid(preact)
    return sigma * (1.0 + preact * (1.0 - sigma))


def tile_terms(values, sources, live_count, feat_blocks):
    slot_total = values.shape[0]
    feature_rows = feat_blocks.shape[0]
    side = values.shape[1]

    def advance(group, running):
        first = group * tile_batch
        group_values = lax.dynamic_slice_in_dim(values, first, tile_batch, 0)
        group_sources = lax.dynamic_slice_in_dim(sources, first, tile_batch, 0)
        group_feats = jnp.take(feat_blocks, group_sources, axis=1)
        product = jnp.einsum(
            "fgj,gij->gfi", group_feats, group_values, preferred_element_type=jnp.float32
        )
        inside_mask = first + jnp.arange(tile_batch, dtype=jnp.int32) < live_count
        product = jnp.where(inside_mask[:, None, None], product, 0.0)
        return lax.dynamic_update_slice_in_dim(running, product, first, 0)

    group_turns = (live_count + tile_batch - 1) // tile_batch
    initial = jnp.zeros((slot_total, feature_rows, side), jnp.float32)
    return lax.fori_loop(0, group_turns, advance, initial)


def tile_back(values, picked_part, live_count):

    def advance(group, running):
        first = group * tile_batch
        group_values = lax.dynamic_slice_in_dim(values, first, tile_batch, 0)
        group_grads = lax.dynamic_slice_in_dim(picked_part, first, tile_batch, 0)
        product = jnp.einsum(
            "gfi,gij->gfj", group_grads, group_values, preferred_element_type=jnp.float32
        )
        inside_mask = first + jnp.arange(tile_batch, dtype=jnp.int32) < live_count
        product = jnp.where(inside_mask[:, None, None], product, 0.0)
        return lax.dynamic_update_slice_in_dim(running, product, first, 0)

    group_turns = (live_count + tile_batch - 1) // tile_batch
    initial = jnp.zeros(picked_part.shape, jnp.float32)
    return lax.fori_loop(0, group_turns, advance, initial)


def to_sources(grads, sources, blocks_here):
    hit_table = (sources[:, None] == jnp.arange(blocks_here, dtype=jnp.int32)[None, :]).astype(
        jnp.float32
    )
    return jnp.einsum("tb,tfj->bfj", hit_table, grads, precision=lax.Precision.HIGHEST)


def local(
    features,
    tile_values,
    tile_source,
    tile_dest,
    tile_count,
    degree,
    w_self,
    w_neigh,
    bias,
    cotangent,
):
    feature_rows = features.shape[0]
    node_count = features.shape[1]
    blocks_here = node_count // TB
    tile_live = tile_count[0]
    own_blocks = features.reshape(feature_rows, blocks_here, TB)
    block_terms = tile_terms(tile_values, tile_source, tile_live, own_blocks)
    live_mask = jnp.arange(TILES_DEV, dtype=jnp.int32) < tile_live
    span = lax.axis_size("vtx") * blocks_here
    relative = tile_dest
    inside = (relative >= 0) & (relative < span) & live_mask
    segment_ids = jnp.where(inside, relative, span)
    summed = lax.psum_scatter(
        jax.ops.segment_sum(block_terms, segment_ids, num_segments=span + 1)[:span],
        "vtx",
        scatter_dimension=0,
        tiled=True,
    )
    deg_float = degree.astype(jnp.float32)
    agg_blocks = (summed / deg_float.reshape(blocks_here, TB)[:, None, :]).astype(jnp.bfloat16)
    agg = agg_blocks.transpose(1, 0, 2).reshape(feature_rows, node_count)
    full_feats, full_agg = (
        lax.all_to_all(features, "col", split_axis=1, concat_axis=0, tiled=True),
        lax.all_to_all(agg, "col", split_axis=1, concat_axis=0, tiled=True),
    )
    preact = jnp.dot(w_self.T, full_feats, preferred_element_type=jnp.float32)
    preact = (
        preact + jnp.dot(w_neigh.T, full_agg, preferred_element_type=jnp.float32) + bias[:, None]
    )
    hidden = jax.nn.silu(preact).astype(jnp.bfloat16)
    grad_pre = (cotangent.astype(jnp.float32) * silu_slope(preact)).astype(jnp.bfloat16)
    part_self = jnp.dot(full_feats, grad_pre.T, preferred_element_type=jnp.float32)
    part_neigh = jnp.dot(full_agg, grad_pre.T, preferred_element_type=jnp.float32)
    part_bias = jnp.sum(grad_pre.astype(jnp.float32), axis=1)
    sum_self, sum_neigh, sum_bias = lax.psum((part_self, part_neigh, part_bias), ("vtx", "col"))
    dx_self = jnp.dot(w_self, grad_pre, preferred_element_type=jnp.float32).astype(jnp.bfloat16)
    dagg = jnp.dot(w_neigh, grad_pre, preferred_element_type=jnp.float32).astype(jnp.bfloat16)
    back_self, back_agg = (
        lax.all_to_all(dx_self, "col", split_axis=0, concat_axis=1, tiled=True),
        lax.all_to_all(dagg, "col", split_axis=0, concat_axis=1, tiled=True),
    )
    dsum = (back_agg.astype(jnp.float32) / deg_float[None, :]).astype(jnp.bfloat16)
    slot_total = tile_dest.shape[0]
    wanted = tile_dest[:, None] * TB + jnp.arange(TB, dtype=jnp.int32)[None, :]
    portion = lax.all_gather(dsum, "vtx", axis=1, tiled=True)
    width_here = portion.shape[1]
    relative = wanted
    inside = (relative >= 0) & (relative < width_here)
    fetched = jnp.take(portion, jnp.clip(relative, 0, width_here - 1), axis=1)
    fetched = fetched.transpose(1, 0, 2)
    picked = jnp.where(
        inside[:, None, :], fetched, jnp.zeros((slot_total, feature_rows, TB), jnp.bfloat16)
    )
    own_grads = tile_back(tile_values, picked, tile_live)
    dx_blocks = to_sources(own_grads, tile_source, blocks_here)
    dx_neigh = dx_blocks.transpose(1, 0, 2).reshape(feature_rows, node_count)
    grad_x = (back_self.astype(jnp.float32) + dx_neigh).astype(jnp.bfloat16)
    return (hidden, grad_x, normalized(sum_self), normalized(sum_neigh), normalized(sum_bias))


def solution(mesh):
    placed = (
        P("col", "vtx"),
        P("vtx", None, None),
        P("vtx"),
        P("vtx"),
        P("vtx"),
        P("vtx"),
        P(),
        P(),
        P(),
        P(None, ("vtx", "col")),
    )
    return jax.shard_map(
        local,
        mesh=mesh,
        in_specs=placed,
        out_specs=(P(None, ("vtx", "col")), P("col", "vtx"), P(), P(), P()),
        check_vma=False,
    )
```

profile of v0, /device:TPU:1, one launch (start us, length us, event | category | flops | bytes accessed | tf_op | source)
XLA Modules:
  0.0 834.2 jit_solution(11644572005708799928)
XLA Ops:
  7.9 1.4 copy_bitcast_fusion.1
  9.3 31.7 %while.20 = (s32[]{:T(128)}, f32[64,16,128]{2,1,0:T(8,128)S(1)}, s32[]{:T(128)}, s32[]{:T(128)}, s32[64]{0:T(128)}, /*index=5*/bf16[16,8,128]{2,0,1:T(8,128)(2,1...) while((s32[]{:T(128)}, f32[64,16,128]{2,1,0:T(8,128)S(1)}, ...), condition=%wide.region_1.2_spmd, body=%wide.region_0.1_spmd.sunk | while | flops 4228166 | bytes 432439 | solution.py:42
  9.3 1.4 compare_and_fusion.2
  10.7 1.3 gather_fusion
  12.1 1.2 fusion.51
  13.3 1.4 compare_and_fusion.2
  14.7 1.3 gather_fusion
  16.0 1.2 fusion.51
  17.3 1.4 compare_and_fusion.2
  18.7 1.3 gather_fusion
  20.0 1.2 fusion.51
  21.2 1.4 compare_and_fusion.2
  22.6 1.3 gather_fusion
  24.0 1.2 fusion.51
  25.2 1.4 compare_and_fusion.2
  26.6 1.3 gather_fusion
  27.9 1.2 fusion.51
  29.2 1.4 compare_and_fusion.2
  30.6 1.3 gather_fusion
  31.9 1.2 fusion.51
  33.1 1.4 compare_and_fusion.2
  34.5 1.3 gather_fusion
  35.8 1.2 fusion.51
  37.1 1.4 compare_and_fusion.2
  38.5 1.3 gather_fusion
  39.8 1.2 fusion.51
  41.1 2.2 broadcast_in_dim.70
  43.3 7.5 scatter_fusion
  50.8 4.4 slice.8
  55.3 13.4 %all-to-all-start = ((bf16[16,8,128]{2,0,1:T(8,128)(2,1)}), bf16[16,8,128]{2,0,1:T(8,128)(2,1)S(1)}, u32[]{:S(2)}, u32[]{:S(2)}) async-start(bf16[16,8,128]{2,0,1:T(8,128)(2,1)} %copy_bitcast_fusion.1), calls=%async_computation | async-start | bytes 65536 | tf_op jit(solution)/shard_map/all_to_all | solution.py:103
  68.8 274.1 %reduce-scatter.2.cloned.1.call-done = f32[8,16,128]{2,1,0:T(8,128)} async-done(((f32[512,16,128]{2,1,0:T(8,128)}), f32[8,16,128]{2,1,0:T(8,128)}) %reduce-scatter.2.cloned.1.call-update) | async-done | bytes 65552 | tf_op jit(solution)/shard_map/reduce_scatter | solution.py:93
  342.9 1.5 fusion.21
  344.4 8.5 %all-to-all-start.1 = ((bf16[16,8,128]{2,0,1:T(8,128)(2,1)}), bf16[16,8,128]{2,0,1:T(8,128)(2,1)S(1)}, u32[]{:S(2)}, u32[]{:S(2)}) async-start(bf16[16,8,128]{2,0,1:T(8,128)(2,1)} %fusion.21), calls=%async_computation.2 | async-start | bytes 65536 | tf_op jit(solution)/shard_map/all_to_all | solution.py:104
  353.1 8.8 %all-to-all-done.1 = bf16[16,8,128]{2,0,1:T(8,128)(2,1)S(1)} async-done(((bf16[16,8,128]{2,0,1:T(8,128)(2,1)}), bf16[16,8,128]{2,0,1:T(8,128)(2,1)S(1)}, u32[]{:S(2)}, u32[]{:S(2)}) %all-to-all-start.1) | async-done | bytes 32800 | tf_op jit(solution)/shard_map/all_to_all | solution.py:104
  363.8 3.3 all-to-all-start.3
  368.1 8.0 all-to-all-done.3
  377.4 99.1 %psum.23 = f32[256]{0:T(256)S(1)} all-reduce(f32[256]{0:T(256)S(1)} %get-tuple-element.142), channel_id=1, replica_groups=mesh['vtx'=64,'col'=8] {'vtx','col'}, use_global_device_ids=true, to_apply=%region_11.12 | all-reduce | flops 256 | bytes 2048 | tf_op jit(solution)/shard_map/psum | solution.py:115
  478.7 5.8 all-to-all-start.2
  485.8 160.3 %all-reduce.3.cloned.1.call-done = (f32[128,256]{0,1:T(8,128)}, f32[128,256]{1,0:T(8,128)}) async-done(((f32[128,256]{0,1:T(8,128)}, f32[128,256]{1,0:T(8,128)}), (f32[128,256]{0,1:T(8,128)}, f32[128,256]{1,0:T(8,128)})) %all-reduce.3.cloned.1.call-update) | async-done | bytes 262160 | tf_op jit(solution)/shard_map/psum | solution.py:115
  646.0 1.5 multiply_reduce_fusion
  648.3 1.5 multiply_reduce_fusion.1
  652.2 1.6 broadcast_divide_fusion
  653.8 127.4 %all-gather.2.cloned.1.call-done = bf16[16,65536]{0,1:T(8,128)(2,1)} async-done(((bf16[16,1024]{0,1:T(8,128)(2,1)}), bf16[16,65536]{0,1:T(8,128)(2,1)}) %all-gather.2.cloned.1.call-update) | async-done | bytes 2097168 | tf_op jit(solution)/shard_map/all_gather | solution.py:125
  781.2 29.8 %gather_fusion.1 = bf16[8192,16]{1,0:T(8,128)(2,1)S(1)} fusion(bf16[16,65536]{0,1:T(8,128)(2,1)} %all-gather.2.cloned.1.call-done, s32[8192]{0:T(1024)S(1)} %fusion.16), kind=kCustom, calls=%fused_computation.1 | custom fusion | bytes 557056 | tf_op jit(solution)/shard_map/jit(_take)/gather | solution.py:129
  811.9 14.8 %while.21 = (s32[]{:T(128)}, f32[64,16,128]{2,0,1:T(8,128)S(1)}, s32[]{:T(128)}, s32[]{:T(128)}, bf16[64,16,128]{2,1,0:T(8,128)(2,1)S(1)}, /*index=5*/bf16[64,12...) while((s32[]{:T(128)}, f32[64,16,128]{2,0,1:T(8,128)S(1)}, s32[]{:T(128)}, s32[]{:T(128)}, ...), condition=%wide.region_5.6_spmd, body=%wide.region_4.5_spmd.sunk | while | flops 4210710 | bytes 493223 | solution.py:60
  814.4 1.1 convolution_select_fusion.3
  816.3 1.1 convolution_select_fusion.3
  820.0 1.1 convolution_select_fusion.3
  (76 shorter events, 21.9 us)
Async XLA Ops:
  7.2 354.8 %copy-start = (bf16[128,256]{1,0:T(8,128)(2,1)S(1)}, bf16[128,256]{1,0:T(8,128)(2,1)}, u32[]{:S(2)}) copy-start(bf16[128,256]{1,0:T(8,128)(2,1)} %param.21) | copy-start | bytes 196612
  7.2 33.9 %copy-start.5 = (s32[64]{0:T(128)S(1)}, s32[64]{0:T(128)}, u32[]{:S(2)}) copy-start(s32[64]{0:T(128)} %param.17) | copy-start | bytes 772
  7.2 335.8 %reduce-scatter.2.cloned.1.call-start = ((), (), s32[]{:S(2)}) async-start(), calls=%async_computation.5 | async-start | bytes 4259840 | tf_op jit(solution)/shard_map/reduce_scatter | solution.py:93
  55.2 13.5 %copy-start.2 = (bf16[256,128]{1,0:T(8,128)(2,1)S(1)}, bf16[256,128]{1,0:T(8,128)(2,1)}, u32[]{:S(2)}) copy-start(bf16[256,128]{1,0:T(8,128)(2,1)} %param.23) | copy-start | bytes 196612
  55.2 13.6 %copy-start.4 = (s32[1024]{0:T(1024)S(1)}, s32[1024]{0:T(1024)}, u32[]{:S(2)}) copy-start(s32[1024]{0:T(1024)} %param.19) | copy-start | bytes 12292
  55.2 297.7 %copy-start.1 = (bf16[128,256]{1,0:T(8,128)(2,1)S(1)}, bf16[128,256]{1,0:T(8,128)(2,1)}, u32[]{:S(2)}) copy-start(bf16[128,256]{1,0:T(8,128)(2,1)} %param.20) | copy-start | bytes 196612
  55.2 306.7 %copy-start.6 = (f32[256]{0:T(256)S(1)}, f32[256]{0:T(256)}, u32[]{:S(2)}) copy-start(f32[256]{0:T(256)} %param.22) | copy-start | bytes 3076
  55.3 289.1 %all-to-all-start = ((bf16[16,8,128]{2,0,1:T(8,128)(2,1)}), bf16[16,8,128]{2,0,1:T(8,128)(2,1)S(1)}, u32[]{:S(2)}, u32[]{:S(2)}) async-start(bf16[16,8,128]{2,0,1:T(8,128)(2,1)} %copy_bitcast_fusion.1), calls=%async_computation | async-start | bytes 65536 | tf_op jit(solution)/shard_map/all_to_all | solution.py:103
  344.4 17.5 %all-to-all-start.1 = ((bf16[16,8,128]{2,0,1:T(8,128)(2,1)}), bf16[16,8,128]{2,0,1:T(8,128)(2,1)S(1)}, u32[]{:S(2)}, u32[]{:S(2)}) async-start(bf16[16,8,128]{2,0,1:T(8,128)(2,1)} %fusion.21), calls=%async_computation.2 | async-start | bytes 65536 | tf_op jit(solution)/shard_map/all_to_all | solution.py:104
  363.8 12.3 %all-to-all-start.3 = ((bf16[8,16,128]{2,1,0:T(8,128)(2,1)}), bf16[8,16,128]{2,1,0:T(8,128)(2,1)S(1)}, u32[]{:S(2)}, u32[]{:S(2)}) async-start(bf16[8,16,128]{2,1,0:T(8,128)(2,1)} %bitcast.13), calls=%async_computation.4 | async-start | bytes 65536 | tf_op jit(solution)/shard_map/all_to_all | solution.py:120
  367.1 278.9 %all-reduce.3.cloned.1.call-start = ((), (), s32[]{:S(2)}) async-start(), calls=%async_computation.7 | async-start | bytes 524288 | tf_op jit(solution)/shard_map/psum | solution.py:115
  368.1 413.1 %all-gather.2.cloned.1.call-start = ((), (), s32[]{:S(2)}) async-start(), calls=%async_computation.6 | async-start | bytes 17039360 | tf_op jit(solution)/shard_map/all_gather | solution.py:125
  478.7 348.1 %all-to-all-start.2 = ((bf16[8,16,128]{2,1,0:T(8,128)(2,1)}), bf16[8,16,128]{2,1,0:T(8,128)(2,1)S(1)}, u32[]{:S(2)}, u32[]{:S(2)}) async-start(bf16[8,16,128]{2,1,0:T(8,128)(2,1)} %bitcast.10), calls=%async_computation.3 | async-start | bytes 65536 | tf_op jit(solution)/shard_map/all_to_all | solution.py:119
  811.7 15.0 %copy-start.3 = (s32[64]{0:T(128)S(1)}, s32[64]{0:T(128)}, u32[]{:S(2)}) copy-start(s32[64]{0:T(128)} %get-tuple-element.326) | copy-start | bytes 772
Sparse Core Ops, SparseCore 0:
  55.4 287.5 reduce-scatter.1
  374.6 271.4 all-reduce.2
  648.2 132.9 all-gather.1
where the time goes:
time: 835 us; the launch traced here: 834 us
  waiting for transfers between devices  579 us (69%)
  blocking collectives  99.1 us (12%)
  local copies, waits for them, and re-layouts  52 us (6%)
  other arithmetic  33.3 us (4%)
  starting transfers between devices  31.2 us (4%)
  matrix products  22.9 us (3%)
  between operations  16.7 us (2%)
    reduce_scatter x1, waiting for transfers between devices, local(): lax.psum_scatter(jax.ops.segment_sum(block_terms, segment_ids, num_segmen...  274 us
    psum x1, waiting for transfers between devices, local(): lax.psum((part_self, part_neigh, part_bias), ('vtx', 'col'))  160 us
    all_gather x1, waiting for transfers between devices, local(): portion = lax.all_gather(dsum, 'vtx', axis=1, tiled=True)  127 us
    psum x1, blocking collectives, local(): lax.psum((part_self, part_neigh, part_bias), ('vtx', 'col'))  99.1 us
    gather x2, local copies, waits for them, and re-layouts, local(): fetched = jnp.take(portion, jnp.clip(relative, 0, width_here - 1), axis=1)  30.6 us
  transfers between devices with their start and end apart: 7, of which 5 were waited for; matrix products, arithmetic and copies ran while one was open for 7% of the time, Pallas kernels for 0%

commit v1 on v0

v1 whole, which is shorter than its diff:
```python
import jax
import jax.numpy as jnp
from jax import lax
from jax.experimental import pallas as pl
from jax.experimental.pallas import tpu as pltpu
from jax.sharding import Mesh
from jax.sharding import PartitionSpec as P

TB = 128
TILES_DEV = 64
RB = 8
F_LOC = 16
Y = 8
STEP = 16

EPS = 1e-06
BF = jnp.bfloat16
F32 = jnp.float32

AXES = ("y", "zl", "k", "col")
VTX = ("y", "zl", "k")
YZ = ("y", "zl")

VMEM = pl.BlockSpec(memory_space=pltpu.VMEM)
SMEM = pl.BlockSpec(memory_space=pltpu.SMEM)
PARAMS = pltpu.CompilerParams(vmem_limit_bytes=32 * 1024 * 1024)


def whole(kernel, out_shape, in_specs, scratch=()):
    many = isinstance(out_shape, (tuple, list))
    return pl.pallas_call(
        kernel,
        out_shape=out_shape,
        in_specs=in_specs,
        out_specs=[VMEM] * len(out_shape) if many else VMEM,
        scratch_shapes=list(scratch),
        compiler_params=PARAMS,
    )


def sds(shape, dtype):
    return jax.ShapeDtypeStruct(shape, dtype)


def terms_kernel(src, feats, vals, out):
    first = pl.program_id(0) * STEP
    for t in range(STEP):
        start = pl.multiple_of(src[first + t] * TB, TB)
        block = feats[:, pl.ds(start, TB)]
        term = lax.dot_general(
            block, vals[t], (((1,), (1,)), ((), ())), preferred_element_type=F32
        )
        out[t] = term.astype(BF)


def tile_terms(src, feats, vals):
    return pl.pallas_call(
        terms_kernel,
        out_shape=sds((TILES_DEV, F_LOC, TB), BF),
        grid_spec=pltpu.PrefetchScalarGridSpec(
            num_scalar_prefetch=1,
            grid=(TILES_DEV // STEP,),
            in_specs=[
                pl.BlockSpec((F_LOC, RB * TB), lambda g, s: (0, 0)),
                pl.BlockSpec((STEP, TB, TB), lambda g, s: (g, 0, 0)),
            ],
            out_specs=pl.BlockSpec((STEP, F_LOC, TB), lambda g, s: (g, 0, 0)),
        ),
        compiler_params=PARAMS,
    )(src, feats, vals)


def dense_kernel(dest_own, dest_other, own, other, out, acc):
    k = lax.axis_index("k")
    dump = acc.shape[0] - 1
    acc[...] = jnp.zeros_like(acc)
    for dests, terms in ((dest_own, own), (dest_other, other)):

        def add(s, carry, dests=dests, terms=terms):
            d = dests[s]
            mine = jnp.logical_and(d >= 0, ((d >> 3) & 1) == k)
            at = jnp.where(mine, (d >> 4) * RB + (d & 7), dump)
            acc[at] = acc[at] + terms[s].astype(F32)
            return carry

        lax.fori_loop(0, TILES_DEV, add, 0, unroll=8)
    out[...] = acc[0:dump].astype(BF)


def agg_kernel(recv, degree, feats, out):
    for b in range(RB):
        total = jnp.sum(recv[:, b].astype(F32), axis=0)
        deg = degree[b : b + 1, :].astype(F32)
        out[b, 0:F_LOC] = (total / deg).astype(BF)
        out[b, F_LOC : 2 * F_LOC] = feats[:, b * TB : (b + 1) * TB]


def dense_layer_kernel(recv, w_self, w_neigh, bias, cot, degree, hidden, out):
    agg = recv[:, 0:F_LOC].reshape(RB * F_LOC, TB)
    feats = recv[:, F_LOC : 2 * F_LOC].reshape(RB * F_LOC, TB)
    ws = w_self[...]
    wn = w_neigh[...]
    first = (((0,), (0,)), ((), ()))
    last = (((1,), (1,)), ((), ()))
    preact = lax.dot_general(ws, feats, first, preferred_element_type=F32)
    preact = preact + lax.dot_general(wn, agg, first, preferred_element_type=F32)
    preact = preact + bias[...]
    sigma = 1.0 / (1.0 + jnp.exp(-preact))
    hidden[...] = (preact * sigma).astype(BF)
    slope = sigma * (1.0 + preact * (1.0 - sigma))
    grad_pre = (cot[...].astype(F32) * slope).astype(BF)
    part_self = lax.dot_general(feats, grad_pre, last, preferred_element_type=F32)
    part_neigh = lax.dot_general(agg, grad_pre, last, preferred_element_type=F32)
    ones = jnp.ones((8, TB), BF)
    part_bias = lax.dot_general(ones, grad_pre, last, preferred_element_type=F32)[0:1]
    dx_self = jnp.dot(ws, grad_pre, preferred_element_type=F32).astype(BF)
    dagg = jnp.dot(wn, grad_pre, preferred_element_type=F32).astype(BF)
    deg = degree[pl.ds(lax.axis_index("col"), 1), :].astype(F32)
    dsum = (dagg.astype(F32) / deg).astype(BF)
    two = jnp.concatenate([part_bias[:, 0:TB], part_bias[:, TB:]], axis=0)
    high = two.astype(BF).astype(F32)
    tail = jnp.concatenate([high, two - high, jnp.zeros((12, TB), F32)], axis=0).astype(BF)
    for c in range(RB):
        rows = slice(c * F_LOC, (c + 1) * F_LOC)
        out[c, 0:16] = dsum[rows]
        out[c, 16:32] = dx_self[rows]
        out[c, 32:48] = part_self[rows, 0:TB].astype(BF)
        out[c, 48:64] = part_self[rows, TB:].astype(BF)
        out[c, 64:80] = part_neigh[rows, 0:TB].astype(BF)
        out[c, 80:96] = part_neigh[rows, TB:].astype(BF)
        out[c, 96:112] = tail


def spread_kernel(recv, out):
    places = out.shape[0]
    chunk = jnp.sum(recv[:, 32:96].astype(F32), axis=0)
    tail = jnp.sum(recv[:, 96:112].astype(F32), axis=0)
    two = tail[0:2] + tail[2:4]
    high = two.astype(BF).astype(F32)
    low_half = jnp.concatenate([high, two - high, jnp.zeros((4, TB), F32)], axis=0)
    blocks = recv[:, 0:16]
    for p in range(places):
        g = p // (places // Y)
        out[p, 0:RB] = blocks
        out[p, RB] = jnp.concatenate([chunk[8 * g : 8 * g + 8], low_half], axis=0).astype(BF)


def pick_kernel(dest_own, dest_other, recv, own, other, sums):
    k = lax.axis_index("k")
    for dests, picked in ((dest_own, own), (dest_other, other)):

        def pick(s, carry, dests=dests, picked=picked):
            d = dests[s]
            mine = jnp.logical_and(d >= 0, ((d >> 3) & 1) == k)
            at = jnp.where(mine, d, 0)
            tile = recv[at >> 4, at & 7]
            picked[s] = jnp.where(mine, tile, jnp.zeros_like(tile))
            return carry

        lax.fori_loop(0, TILES_DEV, pick, 0, unroll=8)
    total = jnp.sum(recv[:, RB].astype(F32), axis=0)
    high = total.astype(BF)
    low = (total - high.astype(F32)).astype(BF)
    other[TILES_DEV] = high
    other[TILES_DEV + 1] = low
    sums[...] = high.astype(F32) + low.astype(F32)


def joined_kernel(sums, other, out, bias_out):
    given = other[TILES_DEV].astype(F32) + other[TILES_DEV + 1].astype(F32)
    total = sums[...] + given
    for p in range(out.shape[0]):
        out[p] = total[0:8]
    two = total[8:10] + total[10:12]
    bias_out[...] = two / jnp.sqrt(jnp.mean(two * two) + EPS)


def back_kernel(src, own, other, vals, recv, out, acc):
    g = pl.program_id(0)

    @pl.when(g == 0)
    def _():
        acc[...] = recv[:, 16:32].astype(F32)

    first = g * STEP
    for t in range(STEP):
        grad = own[t] + other[t]
        at = src[first + t]
        acc[at] = acc[at] + jnp.dot(grad, vals[t], preferred_element_type=F32)

    @pl.when(g == pl.num_programs(0) - 1)
    def _():
        for b in range(RB):
            out[:, b * TB : (b + 1) * TB] = acc[b].astype(BF)


def tile_back(src, own, other, vals, recv):
    return pl.pallas_call(
        back_kernel,
        out_shape=sds((F_LOC, RB * TB), BF),
        grid_spec=pltpu.PrefetchScalarGridSpec(
            num_scalar_prefetch=1,
            grid=(TILES_DEV // STEP,),
            in_specs=[
                pl.BlockSpec((STEP, F_LOC, TB), lambda g, s: (g, 0, 0)),
                pl.BlockSpec((STEP, F_LOC, TB), lambda g, s: (g, 0, 0)),
                pl.BlockSpec((STEP, TB, TB), lambda g, s: (g, 0, 0)),
                pl.BlockSpec(recv.shape, lambda g, s: (0, 0, 0)),
            ],
            out_specs=pl.BlockSpec((F_LOC, RB * TB), lambda g, s: (0, 0)),
            scratch_shapes=[pltpu.VMEM((RB, F_LOC, TB), F32)],
        ),
        compiler_params=PARAMS,
    )(src, own, other, vals, recv)


def normal_kernel(x, grad_self, grad_neigh):
    for first, out in ((0, grad_self), (32, grad_neigh)):
        part = x[:, first : first + 32]
        scale = jnp.sqrt(jnp.sum(part * part) / (RB * 32 * TB) + EPS)
        scaled = part / scale
        for c in range(RB):
            rows = slice(c * F_LOC, (c + 1) * F_LOC)
            out[rows, 0:TB] = scaled[c, 0:16]
            out[rows, TB:] = scaled[c, 16:32]


def local(
    features,
    tile_values,
    tile_source,
    tile_dest,
    tile_count,
    degree,
    w_self,
    w_neigh,
    bias,
    cotangent,
):
    places = lax.axis_size(YZ)
    swap = [(0, 1), (1, 0)]
    live = jnp.arange(TILES_DEV, dtype=jnp.int32) < tile_count[0]
    dest = jnp.where(live, tile_dest, -1)
    dest_other = lax.ppermute(dest, "k", swap)
    degree2 = degree.reshape(RB, TB)

    terms = tile_terms(tile_source, features, tile_values)
    terms_other = lax.ppermute(terms, "k", swap)
    dense = whole(
        dense_kernel,
        sds((places * RB, F_LOC, TB), BF),
        [SMEM, SMEM, VMEM, VMEM],
        [pltpu.VMEM((places * RB + 1, F_LOC, TB), F32)],
    )(dest, dest_other, terms, terms_other)
    summed = lax.all_to_all(
        dense.reshape(places, RB, F_LOC, TB), YZ, split_axis=0, concat_axis=0, tiled=True
    )
    packed = whole(agg_kernel, sds((RB, 2 * F_LOC, TB), BF), [VMEM] * 3)(
        summed, degree2, features
    )
    full = lax.all_to_all(packed, "col", split_axis=0, concat_axis=0, tiled=True)
    hidden, back = whole(
        dense_layer_kernel,
        (sds(cotangent.shape, BF), sds((RB, 112, TB), BF)),
        [VMEM] * 6,
    )(full, w_self, w_neigh, bias[:, None], cotangent, degree2)
    back = lax.all_to_all(back, "col", split_axis=0, concat_axis=0, tiled=True)
    spread = whole(spread_kernel, sds((places, RB + 1, F_LOC, TB), BF), [VMEM])(back)
    portion = lax.all_to_all(spread, YZ, split_axis=0, concat_axis=0, tiled=True)
    own, other, sums = whole(
        pick_kernel,
        (
            sds((TILES_DEV, F_LOC, TB), BF),
            sds((TILES_DEV + 2, F_LOC, TB), BF),
            sds((16, TB), F32),
        ),
        [SMEM, SMEM, VMEM],
    )(dest, dest_other, portion)
    given = lax.ppermute(other, "k", swap)
    joined, grad_bias = whole(
        joined_kernel, (sds((RB * Y, 8, TB), F32), sds((2, TB), F32)), [VMEM] * 2
    )(sums, given)
    chunks = lax.all_to_all(joined, ("col", "y"), split_axis=0, concat_axis=0, tiled=True)
    grad_x = tile_back(tile_source, own, given, tile_values, back)
    grad_self, grad_neigh = whole(
        normal_kernel, (sds(w_self.shape, F32), sds(w_self.shape, F32)), [VMEM]
    )(chunks.reshape(RB, 8 * Y, TB))
    return hidden, grad_x, grad_self, grad_neigh, grad_bias.reshape(-1)


def solution(mesh):
    vtx, col = mesh.shape["vtx"], mesh.shape["col"]
    fine = Mesh(mesh.devices.reshape(Y, vtx // (2 * Y), 2, col), AXES)
    placed = (
        P("col", VTX),
        P(VTX, None, None),
        P(VTX),
        P(VTX),
        P(VTX),
        P(VTX),
        P(),
        P(),
        P(),
        P(None, AXES),
    )
    return jax.shard_map(
        local,
        mesh=fine,
        in_specs=placed,
        out_specs=(P(None, AXES), P("col", VTX), P(), P(), P()),
        check_vma=False,
    )
```

time: 835 us -> 156 us (0.19)
  waiting for transfers between devices: 579 us -> 25.3 us
  local copies, waits for them, and re-layouts: 52 us -> 3.18 us
  other arithmetic: 33.3 us -> 0.01 us
  matrix products: 22.9 us -> 0 us
  blocking collectives: 99.1 us -> 81.9 us
  between operations: 16.7 us -> 1.43 us
  Pallas kernels: 0 us -> 10.7 us
    reduce_scatter x1 -> x0, waiting for transfers between devices: 274 us -> none  [local(): lax.psum_scatter(jax.ops.segment_sum(block_terms, segment_ids, num_segmen...]
    psum x1 -> x0, waiting for transfers between devices: 160 us -> none  [local(): lax.psum((part_self, part_neigh, part_bias), ('vtx', 'col'))]
    all_gather x1 -> x0, waiting for transfers between devices: 127 us -> none  [local(): portion = lax.all_gather(dsum, 'vtx', axis=1, tiled=True)]
    psum x1 -> x0, blocking collectives: 99.1 us -> none  [local(): lax.psum((part_self, part_neigh, part_bias), ('vtx', 'col'))]
    all_to_all x0 -> x3, blocking collectives: none -> 81.9 us  [the longest x1 35.1 us: local(): lax.all_to_all(spread, YZ, split_axis=0, concat_axis=0, tiled=True)]
    gather x10 -> x0, local copies, waits for them, and re-layouts: 41.2 us -> none  [the longest x2 30.6 us: local(): fetched = jnp.take(portion, jnp.clip(relative, 0, width_here - 1), axis=1)]
    dot_general x23 -> x0, matrix products: 22.9 us -> none  [the longest x8 9.92 us: advance(): jnp.einsum('fgj,gij->gfi', group_feats, group_values, preferred_element_t...]
    ppermute x0 -> x3, starting transfers between devices: none -> 18.2 us  [the longest x1 8.8 us: local(): terms_other = lax.ppermute(terms, 'k', swap)]
  transfers between devices with their start and end apart: 7 -> 5, of which waited for: 5 -> 4; matrix products, arithmetic and copies ran while one was open for 7% -> 0% of each run, Pallas kernels for 0% -> 1%
where the time goes in v1:
time: 156 us; the launch traced here: 155 us
  blocking collectives  81.9 us (53%)
  starting transfers between devices  32.6 us (21%)
  waiting for transfers between devices  25.3 us (16%)
  Pallas kernels  10.7 us (7%)
  local copies, waits for them, and re-layouts  3.18 us (2%)
    all_to_all x1, blocking collectives, local(): lax.all_to_all(spread, YZ, split_axis=0, concat_axis=0, tiled=True)  35.1 us
    all_to_all x1, blocking collectives, local(): lax.all_to_all(dense.reshape(places, RB, F_LOC, TB), YZ, split_axis=0, co...  34.5 us
    all_to_all x1, waiting for transfers between devices, local(): lax.all_to_all(joined, ('col', 'y'), split_axis=0, concat_axis=0, tiled=T...  14.1 us
    all_to_all x1, blocking collectives, local(): back = lax.all_to_all(back, 'col', split_axis=0, concat_axis=0, tiled=True)  12.3 us
    all_to_all x1, starting transfers between devices, local(): lax.all_to_all(packed, 'col', split_axis=0, concat_axis=0, tiled=True)  9.77 us
    all_to_all x1, waiting for transfers between devices, local(): lax.all_to_all(packed, 'col', split_axis=0, concat_axis=0, tiled=True)  8.96 us
    ppermute x1, starting transfers between devices, local(): terms_other = lax.ppermute(terms, 'k', swap)  8.8 us
    ppermute x1, starting transfers between devices, local(): given = lax.ppermute(other, 'k', swap)  7.47 us
  transfers between devices with their start and end apart: 5, of which 4 were waited for; matrix products, arithmetic and copies ran while one was open for 0% of the time, Pallas kernels for 1%

profile of v1, /device:TPU:1, one launch (start us, length us, event | category | flops | bytes accessed | tf_op | source)
XLA Modules:
  0.0 155.1 jit_solution(4623928349843209327)
XLA Ops:
  0.6 0.0 copy-start
  0.6 1.6 %copy-done = bf16[64,128,128]{2,1,0:T(8,128)(2,1)S(1)} copy-done((bf16[64,128,128]{2,1,0:T(8,128)(2,1)S(1)}, bf16[64,128,128]{2,1,0:T(8,128)(2,1)}, u32[]{:S(2)}) %copy-start) | copy-done | bytes 2097176
  2.2 0.0 copy-start.2
  2.2 0.8 copy-done.2
  3.0 0.0 copy-start.8
  3.0 0.7 copy-done.8
  3.6 0.0 copy-start.11
  3.6 2.1 %shard_map.137.own = bf16[64,16,128]{2,1,0:T(8,128)(2,1)S(1)} custom-call(s32[64]{0:T(128)S(1)} %copy-done.8, bf16[16,1024]{1,0:T(8,128)(2,1)S(1)} %copy-done.2, bf16[64,128,128]{2,1,0:T(8,128)(2,1)S(1)} %copy-done), custom_call_target="tpu_custom_call" | custom-call | tf_op jit(solution)/shard_map/pallas_call | solution.py:57
  5.7 8.8 %collective-permute-start.1 = (bf16[64,16,128]{2,1,0:T(8,128)(2,1)S(1)}, bf16[64,16,128]{2,1,0:T(8,128)(2,1)S(1)}, u32[]{:S(2)}, u32[]{:S(2)}) collective-permute-start(bf16[64,16,128]{2,1,0:T(8,128)(2,1)S(1)} %shard_map.137.own), channel_id=1, source_target_pairs={{0,8},{8,0},{1,9},{9,1},{2,10},{10,2},{3,11},{11,3},{4,12},{12,4},... | collective-permute-start | bytes 786440 | tf_op jit(solution)/shard_map/ppermute | solution.py:248
  15.2 0.0 copy-done.11
  15.2 1.9 %collective-permute-start = (s32[64]{0:T(128)S(1)}, s32[64]{0:T(128)S(1)}, u32[]{:S(2)}, u32[]{:S(2)}) collective-permute-start(s32[64]{0:T(128)S(1)} %compare_select_fusion.dest_own), channel_id=1, source_target_pairs={{0,8},{8,0},{1,9},{9,1},{2,10},{10,2},{3,11},{11,3},{4,12},{12,4},... | collective-permute-start | bytes 776 | tf_op jit(solution)/shard_map/ppermute | solution.py:244
  17.1 1.1 collective-permute-done.dest_other
  18.2 0.0 collective-permute-done.1.other
  18.2 1.6 %shard_map.138 = bf16[256,16,128]{2,1,0:T(8,128)(2,1)S(1)} custom-call(s32[64]{0:T(128)S(1)} %compare_select_fusion.dest_own, s32[64]{0:T(128)S(1)} %collective-permute-done.dest_other, bf16[64,16,128]{2,1,0:T(8,128)(2,1)S(1)} %shard_map.137.own, bf16[64,16,128]{2,1,0:T(8,128)(2,1)S(1)} %collective-permute-done.1.other), custom_call_target="tpu_custom_call" | custom-call | tf_op jit(solution)/shard_map/pallas_call | solution.py:249
  19.8 0.0 copy-start.3
  19.9 0.0 copy-start.7
  19.9 0.0 copy-start.10
  19.9 34.5 %all_to_all.25.recv = bf16[32,8,16,128]{3,2,1,0:T(8,128)(2,1)S(1)} all-to-all(bf16[32,8,16,128]{3,2,1,0:T(8,128)(2,1)S(1)} %bitcast.7), channel_id=1, replica_groups=mesh['y'=8,'zl'=4,'k'=2,'col'=8] {'y','zl'}, dimensions={0} | all-to-all | bytes 2097152 | tf_op jit(solution)/shard_map/all_to_all | solution.py:255
  54.4 0.0 copy-start.4
  54.4 0.0 copy-start.5
  54.4 0.0 copy-start.6
  54.4 0.0 copy-done.3
  54.4 0.0 copy-done.7
  54.4 0.8 shard_map.139
  55.2 9.8 %all-to-all-start.1 = ((bf16[8,32,128]{2,1,0:T(8,128)(2,1)}), bf16[8,32,128]{2,1,0:T(8,128)(2,1)S(1)}, u32[]{:S(2)}, u32[]{:S(2)}) async-start(bf16[8,32,128]{2,1,0:T(8,128)(2,1)} %shard_map.139), calls=%async_computation.1 | async-start | bytes 131072 | tf_op jit(solution)/shard_map/all_to_all | solution.py:261
  65.0 0.0 copy-done.10
  65.0 0.1 copy.15.bias
  65.1 9.0 %all-to-all-done.1.recv = bf16[8,32,128]{2,1,0:T(8,128)(2,1)S(1)} async-done(((bf16[8,32,128]{2,1,0:T(8,128)(2,1)}), bf16[8,32,128]{2,1,0:T(8,128)(2,1)S(1)}, u32[]{:S(2)}, u32[]{:S(2)}) %all-to-all-start.1) | async-done | bytes 65568 | tf_op jit(solution)/shard_map/all_to_all | solution.py:261
  74.1 0.0 copy-done.4
  74.1 0.0 copy-done.5
  74.1 0.0 copy-done.6
  74.1 1.0 shard_map.140
  75.1 12.3 %all_to_all.26.recv = bf16[8,112,128]{2,1,0:T(8,128)(2,1)S(1)} all-to-all(bf16[8,112,128]{2,1,0:T(8,128)(2,1)S(1)} %get-tuple-element.15), channel_id=1, replica_groups=mesh['y'=8,'zl'=4,'k'=2,'col'=8] {'col'}, dimensions={0} | all-to-all | bytes 458752 | tf_op jit(solution)/shard_map/all_to_all | solution.py:267
  87.3 0.2 shard_map.141
  87.5 0.0 copy-start.1
  87.5 35.1 %all_to_all.27.recv = bf16[32,9,16,128]{3,2,1,0:T(8,128)(2,1)S(1)} all-to-all(bf16[32,9,16,128]{3,2,1,0:T(8,128)(2,1)S(1)} %shard_map.141), channel_id=1, replica_groups=mesh['y'=8,'zl'=4,'k'=2,'col'=8] {'y','zl'}, dimensions={0} | all-to-all | bytes 2359296 | tf_op jit(solution)/shard_map/all_to_all | solution.py:269
  122.6 0.0 copy-start.9
  122.6 1.2 shard_map.142
  123.9 7.5 %collective-permute-start.2 = (bf16[66,16,128]{2,1,0:T(8,128)(2,1)S(1)}, bf16[66,16,128]{2,1,0:T(8,128)(2,1)S(1)}, u32[]{:S(2)}, u32[]{:S(2)}) collective-permute-start(bf16[66,16,128]{2,1,0:T(8,128)(2,1)S(1)} %get-tuple-element.17), channel_id=1, source_target_pairs={{0,8},{8,0},{1,9},{9,1},{2,10},{10,2},{3,11},{11,3},{4,12},{12,4},... | collective-permute-start | bytes 811016 | tf_op jit(solution)/shard_map/ppermute | solution.py:279
  131.3 1.2 collective-permute-done.2.other
  132.5 0.7 shard_map.144
  133.2 4.6 %all-to-all-start.4 = ((f32[64,8,128]{2,1,0:T(8,128)}), f32[64,8,128]{2,1,0:T(8,128)S(1)}, u32[]{:S(2)}, u32[]{:S(2)}) async-start(f32[64,8,128]{2,1,0:T(8,128)} %get-tuple-element.19), calls=%async_computation.4 | async-start | bytes 524288 | tf_op jit(solution)/shard_map/all_to_all | solution.py:283
  137.8 0.0 copy-done.1
  137.9 0.0 copy-done.9
  137.9 2.2 %shard_map.143 = bf16[16,1024]{1,0:T(8,128)(2,1)} custom-call(s32[64]{0:T(128)S(1)} %copy-done.9, bf16[64,16,128]{2,1,0:T(8,128)(2,1)S(1)} %get-tuple-element.16.own, bf16[66,16,128]{2,1,0:T(8,128)(2,1)S(1)} %collective-permute-done.2.other, bf16[64,128,128]{2,1,0:T(8,128)(2,1)S(1)} %copy-done.1, bf16[8,112,128]{2,1,0:T(8,128)(2,1)S(1)} %all_to_all.26.recv), custom_call_target="tpu_custom_call" | custom-call | tf_op jit(solution)/shard_map/pallas_call | solution.py:198
  140.1 14.1 %all-to-all-done.4 = f32[64,8,128]{2,1,0:T(8,128)S(1)} async-done(((f32[64,8,128]{2,1,0:T(8,128)}), f32[64,8,128]{2,1,0:T(8,128)S(1)}, u32[]{:S(2)}, u32[]{:S(2)}) %all-to-all-start.4) | async-done | bytes 262176 | tf_op jit(solution)/shard_map/all_to_all | solution.py:283
  154.2 0.9 shard_map.145
  (1 shorter events, 0.0 us)
Async XLA Ops:
  0.6 1.6 %copy-start = (bf16[64,128,128]{2,1,0:T(8,128)(2,1)S(1)}, bf16[64,128,128]{2,1,0:T(8,128)(2,1)}, u32[]{:S(2)}) copy-start(bf16[64,128,128]{2,1,0:T(8,128)(2,1)} %vals.3) | copy-start | bytes 6291460
  2.2 0.8 copy-start.2
  3.0 0.7 copy-start.8
  3.6 11.6 %copy-start.11 = (s32[64]{0:T(128)S(1)}, s32[64]{0:T(128)}, u32[]{:S(2)}) copy-start(s32[64]{0:T(128)} %param.13) | copy-start | bytes 772
  5.7 12.5 %collective-permute-start.1 = (bf16[64,16,128]{2,1,0:T(8,128)(2,1)S(1)}, bf16[64,16,128]{2,1,0:T(8,128)(2,1)S(1)}, u32[]{:S(2)}, u32[]{:S(2)}) collective-permute-start(bf16[64,16,128]{2,1,0:T(8,128)(2,1)S(1)} %shard_map.137.own), channel_id=1, source_target_pairs={{0,8},{8,0},{1,9},{9,1},{2,10},{10,2},{3,11},{11,3},{4,12},{12,4},... | collective-permute-start | bytes 786440 | tf_op jit(solution)/shard_map/ppermute | solution.py:248
  15.2 3.0 %collective-permute-start = (s32[64]{0:T(128)S(1)}, s32[64]{0:T(128)S(1)}, u32[]{:S(2)}, u32[]{:S(2)}) collective-permute-start(s32[64]{0:T(128)S(1)} %compare_select_fusion.dest_own), channel_id=1, source_target_pairs={{0,8},{8,0},{1,9},{9,1},{2,10},{10,2},{3,11},{11,3},{4,12},{12,4},... | collective-permute-start | bytes 776 | tf_op jit(solution)/shard_map/ppermute | solution.py:244
  19.8 34.5 %copy-start.3 = (bf16[16,1024]{1,0:T(8,128)(2,1)S(1)}, bf16[16,1024]{1,0:T(8,128)(2,1)}, u32[]{:S(2)}) copy-start(bf16[16,1024]{1,0:T(8,128)(2,1)} %feats.3) | copy-start | bytes 98308
  19.9 34.5 %copy-start.7 = (s32[1024]{0:T(1024)S(1)}, s32[1024]{0:T(1024)}, u32[]{:S(2)}) copy-start(s32[1024]{0:T(1024)} %param.15) | copy-start | bytes 12292
  19.9 45.1 %copy-start.10 = (f32[256]{0:T(256)S(1)}, f32[256]{0:T(256)}, u32[]{:S(2)}) copy-start(f32[256]{0:T(256)} %param.18) | copy-start | bytes 3076
  54.4 19.7 %copy-start.4 = (bf16[128,256]{1,0:T(8,128)(2,1)S(1)}, bf16[128,256]{1,0:T(8,128)(2,1)}, u32[]{:S(2)}) copy-start(bf16[128,256]{1,0:T(8,128)(2,1)} %w_self.1) | copy-start | bytes 196612
  54.4 19.7 %copy-start.5 = (bf16[128,256]{1,0:T(8,128)(2,1)S(1)}, bf16[128,256]{1,0:T(8,128)(2,1)}, u32[]{:S(2)}) copy-start(bf16[128,256]{1,0:T(8,128)(2,1)} %w_neigh.1) | copy-start | bytes 196612
  54.4 19.7 %copy-start.6 = (bf16[256,128]{1,0:T(8,128)(2,1)S(1)}, bf16[256,128]{1,0:T(8,128)(2,1)}, u32[]{:S(2)}) copy-start(bf16[256,128]{1,0:T(8,128)(2,1)} %cot.1) | copy-start | bytes 196612
  55.2 18.9 %all-to-all-start.1 = ((bf16[8,32,128]{2,1,0:T(8,128)(2,1)}), bf16[8,32,128]{2,1,0:T(8,128)(2,1)S(1)}, u32[]{:S(2)}, u32[]{:S(2)}) async-start(bf16[8,32,128]{2,1,0:T(8,128)(2,1)} %shard_map.139), calls=%async_computation.1 | async-start | bytes 131072 | tf_op jit(solution)/shard_map/all_to_all | solution.py:261
  87.5 50.4 %copy-start.1 = (bf16[64,128,128]{2,1,0:T(8,128)(2,1)S(1)}, bf16[64,128,128]{2,1,0:T(8,128)(2,1)}, u32[]{:S(2)}) copy-start(bf16[64,128,128]{2,1,0:T(8,128)(2,1)} %vals.3) | copy-start | bytes 6291460
  122.6 15.2 %copy-start.9 = (s32[64]{0:T(128)S(1)}, s32[64]{0:T(128)}, u32[]{:S(2)}) copy-start(s32[64]{0:T(128)} %src.3) | copy-start | bytes 772
  123.9 8.6 %collective-permute-start.2 = (bf16[66,16,128]{2,1,0:T(8,128)(2,1)S(1)}, bf16[66,16,128]{2,1,0:T(8,128)(2,1)S(1)}, u32[]{:S(2)}, u32[]{:S(2)}) collective-permute-start(bf16[66,16,128]{2,1,0:T(8,128)(2,1)S(1)} %get-tuple-element.17), channel_id=1, source_target_pairs={{0,8},{8,0},{1,9},{9,1},{2,10},{10,2},{3,11},{11,3},{4,12},{12,4},... | collective-permute-start | bytes 811016 | tf_op jit(solution)/shard_map/ppermute | solution.py:279
  133.2 21.0 %all-to-all-start.4 = ((f32[64,8,128]{2,1,0:T(8,128)}), f32[64,8,128]{2,1,0:T(8,128)S(1)}, u32[]{:S(2)}, u32[]{:S(2)}) async-start(f32[64,8,128]{2,1,0:T(8,128)} %get-tuple-element.19), calls=%async_computation.4 | async-start | bytes 524288 | tf_op jit(solution)/shard_map/all_to_all | solution.py:283

commit v2 on v1

v2 whole, which is shorter than its diff:
```python
import functools

import jax
import jax.numpy as jnp
from jax import lax
from jax.experimental import pallas as pl
from jax.experimental.pallas import tpu as pltpu
from jax.sharding import Mesh
from jax.sharding import PartitionSpec as P

TB = 128
TILES_DEV = 64
RB = 8
F_LOC = 16
Y = 8
STEP = 16
EXTRA = 5

EPS = 1e-06
BF = jnp.bfloat16
F32 = jnp.float32

AXES = ("y", "zl", "k", "col")
VTX = ("y", "zl", "k")
YZ = ("y", "zl")

VMEM = pl.BlockSpec(memory_space=pltpu.VMEM)
SMEM = pl.BlockSpec(memory_space=pltpu.SMEM)
HBM = pl.BlockSpec(memory_space=pltpu.HBM)
PARAMS = pltpu.CompilerParams(vmem_limit_bytes=32 * 1024 * 1024)
FULL_PARAMS = pltpu.CompilerParams(vmem_limit_bytes=59 * 1024 * 1024)


def whole(kernel, out_shape, in_specs, scratch=(), out_specs=None, cost=None):
    many = isinstance(out_shape, (tuple, list))
    return pl.pallas_call(
        kernel,
        out_shape=out_shape,
        in_specs=in_specs,
        out_specs=out_specs or ([VMEM] * len(out_shape) if many else VMEM),
        scratch_shapes=list(scratch),
        compiler_params=PARAMS,
        cost_estimate=cost,
    )


def lasting(us):
    return pl.CostEstimate(flops=0, transcendentals=0, bytes_accessed=int(us * 3.6e6))


def sds(shape, dtype):
    return jax.ShapeDtypeStruct(shape, dtype)


def terms_kernel(
    src_h, dest_h, count_h, feats_h, vals_h, out, src, dest, count, feats, vals, sems, val_sems
):
    small = [
        pltpu.make_async_copy(a, b, sems.at[n])
        for n, (a, b) in enumerate(
            ((src_h, src), (feats_h, feats), (dest_h, dest), (count_h, count))
        )
    ]
    parts = TILES_DEV // STEP
    large = [
        pltpu.make_async_copy(
            vals_h.at[pl.ds(g * STEP, STEP)], vals.at[pl.ds(g * STEP, STEP)], val_sems.at[g]
        )
        for g in range(parts)
    ]
    for copy in small + large:
        copy.start()
    for copy in small:
        copy.wait()
    slot = lax.broadcasted_iota(jnp.int32, (16, TB), 1)
    row = lax.broadcasted_iota(jnp.int32, (16, TB), 0)
    d = jnp.concatenate([dest[...], dest[...]], axis=1)
    d = jnp.where(slot < count[0], jnp.broadcast_to(d, (16, TB)), -1)
    coded = jnp.where(row == 0, d >> 3, d & 7)
    out[TILES_DEV] = coded.astype(F32).astype(BF)
    for g in range(parts):
        large[g].wait()
        for t in range(g * STEP, (g + 1) * STEP):
            start = pl.multiple_of(src[t] * TB, TB)
            block = feats[:, pl.ds(start, TB)]
            term = lax.dot_general(
                block, vals[t], (((1,), (1,)), ((), ())), preferred_element_type=F32
            )
            out[t] = term.astype(BF)


def tile_terms(src, dest, count, feats, vals):
    return pl.pallas_call(
        terms_kernel,
        out_shape=sds((TILES_DEV + 1, F_LOC, TB), BF),
        in_specs=[HBM] * 5,
        out_specs=VMEM,
        scratch_shapes=[
            pltpu.SMEM((TILES_DEV,), jnp.int32),
            pltpu.VMEM((1, TILES_DEV), jnp.int32),
            pltpu.SMEM((1,), jnp.int32),
            pltpu.VMEM(feats.shape, BF),
            pltpu.VMEM(vals.shape, BF),
            pltpu.SemaphoreType.DMA((4,)),
            pltpu.SemaphoreType.DMA((TILES_DEV // STEP,)),
        ],
        compiler_params=FULL_PARAMS,
    )(src, dest, count, feats, vals)


def dense_kernel(dest_own, count, own, other, out, dest_other, acc, coded, sem):
    k = lax.axis_index("k")
    dump = acc.shape[0] - 1
    given = other[TILES_DEV].astype(F32)
    coded[...] = (given[0:1] * 8.0 + given[1:2]).astype(jnp.int32)
    copy = pltpu.make_async_copy(coded, dest_other, sem)
    copy.start()
    acc[...] = jnp.zeros_like(acc)

    def add_to(d, used, term):
        mine = jnp.logical_and(used, ((d >> 3) & 1) == k)
        at = jnp.where(mine, (d >> 4) * RB + (d & 7), dump)
        acc[at] = acc[at] + term.astype(F32)

    def add_own(s, carry):
        add_to(dest_own[s], s < count[0], own[s])
        return carry

    lax.fori_loop(0, TILES_DEV, add_own, 0, unroll=8)
    copy.wait()

    def add_other(s, carry):
        d = dest_other[0, s]
        add_to(d, d >= 0, other[s])
        return carry

    lax.fori_loop(0, TILES_DEV, add_other, 0, unroll=8)
    out[...] = acc[0:dump].astype(BF)


def agg_kernel(recv, degree, feats, out):
    for b in range(RB):
        total = jnp.sum(recv[:, b].astype(F32), axis=0)
        deg = degree[b : b + 1, :].astype(F32)
        out[b, 0:F_LOC] = (total / deg).astype(BF)
        out[b, F_LOC : 2 * F_LOC] = feats[:, b * TB : (b + 1) * TB]


def dense_layer_kernel(recv, w_self, w_neigh, bias, cot, degree, hidden, out):
    agg = recv[:, 0:F_LOC].reshape(RB * F_LOC, TB)
    feats = recv[:, F_LOC : 2 * F_LOC].reshape(RB * F_LOC, TB)
    ws = w_self[...]
    wn = w_neigh[...]
    first = (((0,), (0,)), ((), ()))
    last = (((1,), (1,)), ((), ()))
    preact = lax.dot_general(ws, feats, first, preferred_element_type=F32)
    preact = preact + lax.dot_general(wn, agg, first, preferred_element_type=F32)
    preact = preact + jnp.broadcast_to(bias[...], (TB, bias.shape[1])).T
    sigma = 1.0 / (1.0 + jnp.exp(-preact))
    hidden[...] = (preact * sigma).astype(BF)
    slope = sigma * (1.0 + preact * (1.0 - sigma))
    grad_pre = (cot[...].astype(F32) * slope).astype(BF)
    part_self = lax.dot_general(feats, grad_pre, last, preferred_element_type=F32)
    part_neigh = lax.dot_general(agg, grad_pre, last, preferred_element_type=F32)
    ones = jnp.ones((8, TB), BF)
    part_bias = lax.dot_general(ones, grad_pre, last, preferred_element_type=F32)[0:1]
    dx_self = jnp.dot(ws, grad_pre, preferred_element_type=F32).astype(BF)
    dagg = jnp.dot(wn, grad_pre, preferred_element_type=F32).astype(BF)
    deg = degree[pl.ds(lax.axis_index("col"), 1), :].astype(F32)
    dsum = (dagg.astype(F32) / deg).astype(BF)
    two = jnp.concatenate([part_bias[:, 0:TB], part_bias[:, TB:]], axis=0)
    high = two.astype(BF).astype(F32)
    tail = jnp.concatenate([high, two - high, jnp.zeros((12, TB), F32)], axis=0).astype(BF)
    for c in range(RB):
        rows = slice(c * F_LOC, (c + 1) * F_LOC)
        out[c, 0:16] = dsum[rows]
        out[c, 16:32] = dx_self[rows]
        out[c, 32:48] = part_self[rows, 0:TB].astype(BF)
        out[c, 48:64] = part_self[rows, TB:].astype(BF)
        out[c, 64:80] = part_neigh[rows, 0:TB].astype(BF)
        out[c, 80:96] = part_neigh[rows, TB:].astype(BF)
        out[c, 96:112] = tail


def parted(tail):
    two = tail[0:2] + tail[2:4]
    high = two.astype(BF).astype(F32)
    return jnp.concatenate([high, two - high, jnp.zeros((12, TB), F32)], axis=0).astype(BF)


def first_step_kernel(recv, out):
    blocks = recv[:, 0:F_LOC]
    sums = jnp.sum(recv[:, 32:96].astype(F32), axis=0).astype(BF)
    tail = parted(jnp.sum(recv[:, 96:112].astype(F32), axis=0))
    for p in range(out.shape[0]):
        out[p, 0:RB] = blocks
        for n in range(4):
            out[p, RB + n] = sums[n * F_LOC : (n + 1) * F_LOC]
        out[p, RB + 4] = tail


def second_step_kernel(recv, out):
    came = recv.shape[0]
    sums = [jnp.sum(recv[:, RB + n].astype(F32), axis=0) for n in range(EXTRA)]
    sums = [x.astype(BF) for x in sums[:4]] + [parted(sums[4])]
    for p in range(out.shape[0]):
        for q in range(came):
            out[p, q * RB : (q + 1) * RB] = recv[q, 0:RB]
        for n in range(EXTRA):
            out[p, came * RB + n] = sums[n]


def share_kernel(first, recv, out, bias_out):
    sums = [jnp.sum(recv[:, first + n].astype(F32), axis=0) for n in range(EXTRA)]
    for p in range(out.shape[0]):
        for n in range(4):
            out[p, n * F_LOC : (n + 1) * F_LOC] = sums[n].astype(BF)
    bias_out[...] = parted(sums[4])


def pick_kernel(ny, nz, dest_own, count, dest_other, recv, bias_sum, own, other):
    k = lax.axis_index("k")
    of_y = jnp.where(k == 0, nz * RB + EXTRA, RB)
    of_z = jnp.where(k == 0, RB, ny * (nz * RB + EXTRA) // nz)

    def pick(d, used):
        mine = jnp.logical_and(used, ((d >> 3) & 1) == k)
        d = jnp.where(mine, d, 0)
        place = d >> 4
        at = (place // nz) * of_y + (place % nz) * of_z + (d & 7)
        tile = recv[at]
        return jnp.where(mine, tile, jnp.zeros_like(tile))

    def step(s, carry):
        own[s] = pick(dest_own[s], s < count[0])
        d = dest_other[0, s]
        other[s] = pick(d, d >= 0)
        return carry

    lax.fori_loop(0, TILES_DEV, step, 0, unroll=8)
    other[TILES_DEV] = bias_sum[...]


def back_kernel(src, own, given, recv, vals, out, acc):
    g = pl.program_id(0)

    @pl.when(g == 0)
    def _():
        acc[...] = recv[:, F_LOC : 2 * F_LOC].astype(F32)

    first = g * STEP
    for t in range(STEP):
        grad = own[t] + given[t]
        at = src[first + t]
        acc[at] = acc[at] + jnp.dot(grad, vals[t], preferred_element_type=F32)

    @pl.when(g == pl.num_programs(0) - 1)
    def _():
        for b in range(RB):
            out[:, b * TB : (b + 1) * TB] = acc[b].astype(BF)


def tile_back(src, own, given, recv, vals):
    tiles = pl.BlockSpec((STEP, F_LOC, TB), lambda g, s: (g, 0, 0))
    return pl.pallas_call(
        back_kernel,
        out_shape=sds((F_LOC, RB * TB), BF),
        grid_spec=pltpu.PrefetchScalarGridSpec(
            num_scalar_prefetch=1,
            grid=(TILES_DEV // STEP,),
            in_specs=[
                tiles,
                tiles,
                pl.BlockSpec(recv.shape, lambda g, s: (0, 0, 0)),
                pl.BlockSpec((STEP, TB, TB), lambda g, s: (g, 0, 0)),
            ],
            out_specs=pl.BlockSpec((F_LOC, RB * TB), lambda g, s: (0, 0)),
            scratch_shapes=[pltpu.VMEM((RB, F_LOC, TB), F32)],
        ),
        compiler_params=PARAMS,
        cost_estimate=lasting(2.2),
    )(src, own, given, recv, vals)


def normal_kernel(x, bias_sum, given, grad_self, grad_neigh, grad_bias):
    for first, out in ((0, grad_self), (32, grad_neigh)):
        rows = slice(first, first + 32)
        part = x[0:RB, rows].astype(F32) + x[RB : 2 * RB, rows].astype(F32)
        scale = jnp.sqrt(jnp.sum(part * part) / (RB * 32 * TB) + EPS)
        scaled = part / scale
        for c in range(RB):
            at = slice(c * F_LOC, (c + 1) * F_LOC)
            out[at, 0:TB] = scaled[c, 0:16]
            out[at, TB:] = scaled[c, 16:32]
    mine = bias_sum[...].astype(F32)
    theirs = given[TILES_DEV].astype(F32)
    two = (mine[0:2] + mine[2:4]) + (theirs[0:2] + theirs[2:4])
    grad_bias[...] = two / jnp.sqrt(jnp.mean(two * two) + EPS)


def local(
    features,
    tile_values,
    tile_source,
    tile_dest,
    tile_count,
    degree,
    w_self,
    w_neigh,
    bias,
    cotangent,
):
    places = lax.axis_size(YZ)
    swap = [(0, 1), (1, 0)]
    degree2 = degree.reshape(RB, TB)

    terms = tile_terms(
        tile_source, tile_dest.reshape(1, -1), tile_count, features, tile_values
    )
    terms_other = lax.ppermute(terms, "k", swap)
    dense, dest_other = whole(
        dense_kernel,
        (sds((places * RB, F_LOC, TB), BF), sds((1, TB), jnp.int32)),
        [SMEM, SMEM, VMEM, VMEM],
        [
            pltpu.VMEM((places * RB + 1, F_LOC, TB), F32),
            pltpu.VMEM((1, TB), jnp.int32),
            pltpu.SemaphoreType.DMA,
        ],
        [VMEM, SMEM],
    )(tile_dest, tile_count, terms, terms_other)
    summed = lax.all_to_all(
        dense.reshape(places, RB, F_LOC, TB), YZ, split_axis=0, concat_axis=0, tiled=True
    )
    packed = whole(agg_kernel, sds((RB, 2 * F_LOC, TB), BF), [VMEM] * 3)(
        summed, degree2, features
    )
    full = lax.all_to_all(packed, "col", split_axis=0, concat_axis=0, tiled=True)
    hidden, back = whole(
        dense_layer_kernel,
        (sds(cotangent.shape, BF), sds((RB, 112, TB), BF)),
        [VMEM] * 6,
    )(full, w_self, w_neigh, bias.reshape(1, -1), cotangent, degree2)
    back = lax.all_to_all(back, "col", split_axis=0, concat_axis=0, tiled=True)

    ny, nz = lax.axis_size("y"), lax.axis_size("zl")
    tiles = ny * (nz * RB + EXTRA)

    def in_two_steps(first, second):
        def run(back):
            n1, n2 = lax.axis_size(first), lax.axis_size(second)
            one = whole(first_step_kernel, sds((n1, RB + EXTRA, F_LOC, TB), BF), [VMEM])(back)
            one = lax.all_to_all(one, first, split_axis=0, concat_axis=0, tiled=True)
            two = whole(second_step_kernel, sds((n2, tiles // n2, F_LOC, TB), BF), [VMEM])(one)
            two = lax.all_to_all(two, second, split_axis=0, concat_axis=0, tiled=True)
            share, bias_sum = whole(
                functools.partial(share_kernel, n1 * RB),
                (sds((2 * RB, 64, TB), BF), sds((F_LOC, TB), BF)),
                [VMEM],
            )(two)
            return two.reshape(tiles, F_LOC, TB), share, bias_sum

        return run

    portion, share, bias_sum = lax.cond(
        lax.axis_index("k") == 0, in_two_steps("zl", "y"), in_two_steps("y", "zl"), back
    )
    chunks = lax.all_to_all(share, ("k", "col"), split_axis=0, concat_axis=0, tiled=True)
    own, other = whole(
        functools.partial(pick_kernel, ny, nz),
        (sds((TILES_DEV, F_LOC, TB), BF), sds((TILES_DEV + 1, F_LOC, TB), BF)),
        [SMEM, SMEM, SMEM, VMEM, VMEM],
        cost=lasting(1.2),
    )(tile_dest, tile_count, dest_other, portion, bias_sum)
    given = lax.ppermute(other, "k", swap)
    grad_x = tile_back(tile_source, own, given, back, tile_values)
    grad_self, grad_neigh, grad_bias = whole(
        normal_kernel,
        (sds(w_self.shape, F32), sds(w_self.shape, F32), sds((2, TB), F32)),
        [VMEM] * 3,
    )(chunks, bias_sum, given)
    return hidden, grad_x, grad_self, grad_neigh, grad_bias.reshape(-1)


def solution(mesh):
    vtx, col = mesh.shape["vtx"], mesh.shape["col"]
    fine = Mesh(mesh.devices.reshape(Y, vtx // (2 * Y), 2, col), AXES)
    placed = (
        P("col", VTX),
        P(VTX, None, None),
        P(VTX),
        P(VTX),
        P(VTX),
        P(VTX),
        P(),
        P(),
        P(),
        P(None, AXES),
    )
    return jax.shard_map(
        local,
        mesh=fine,
        in_specs=placed,
        out_specs=(P(None, AXES), P("col", VTX), P(), P(), P()),
        check_vma=False,
    )
```

time: 156 us -> 145 us (0.929)
  starting transfers between devices: 32.6 us -> 22.3 us
  waiting for transfers between devices: 25.3 us -> 16.1 us
  blocking collectives: 81.9 us -> 88.3 us
  Pallas kernels: 10.7 us -> 15.2 us
  local copies, waits for them, and re-layouts: 3.18 us -> 1 us
    all_to_all x2, waiting for transfers between devices: 23.1 us -> 13.4 us  [the longest x1 9.78 us: local(): back = lax.all_to_all(back, 'col', split_axis=0, concat_axis=0, tiled=True)]
    all_to_all x2 -> x3, blocking collectives: 47.4 us -> 54.1 us  [the longest x1 20.5 us: run(): two = lax.all_to_all(two, second, split_axis=0, concat_axis=0, tiled=True)]
    ppermute x1, starting transfers between devices: 7.47 us -> 2.09 us  [local(): given = lax.ppermute(other, 'k', swap)]
    pallas_call x6 -> x7, Pallas kernels: 6.72 us -> 11.6 us  [the longest x1 3.64 us: tile_terms(): pl.pallas_call(terms_kernel, out_shape=sds((TILES_DEV + 1, F_LOC, TB), BF...]
    all_to_all x2, starting transfers between devices: 14.4 us -> 11.4 us  [the longest x1 8.02 us: local(): lax.all_to_all(share, ('k', 'col'), split_axis=0, concat_axis=0, tiled=True)]
    unnamed x24 -> x20, local copies, waits for them, and re-layouts: 3.04 us -> 1 us
    ppermute x1 -> x0, starting transfers between devices: 1.92 us -> none  [local(): dest_other = lax.ppermute(dest, 'k', swap)]
  transfers between devices with their start and end apart: 5 -> 4, of which waited for: 4 -> 4; matrix products, arithmetic and copies ran while one was open for 0% -> 0% of each run, Pallas kernels for 1% -> 3%
where the time goes in v2:
time: 145 us; the launch traced here: 144 us
  blocking collectives  88.3 us (61%)
  starting transfers between devices  22.3 us (15%)
  waiting for transfers between devices  16.1 us (11%)
  Pallas kernels  15.2 us (10%)
    all_to_all x1, blocking collectives, local(): lax.all_to_all(dense.reshape(places, RB, F_LOC, TB), YZ, split_axis=0, co...  34.2 us
    all_to_all x1, blocking collectives, run(): two = lax.all_to_all(two, second, split_axis=0, concat_axis=0, tiled=True)  20.5 us
    all_to_all x1, blocking collectives, local(): lax.all_to_all(packed, 'col', split_axis=0, concat_axis=0, tiled=True)  18.7 us
    all_to_all x1, blocking collectives, run(): one = lax.all_to_all(one, first, split_axis=0, concat_axis=0, tiled=True)  15 us
    all_to_all x1, waiting for transfers between devices, local(): back = lax.all_to_all(back, 'col', split_axis=0, concat_axis=0, tiled=True)  9.78 us
    ppermute x1, starting transfers between devices, local(): terms_other = lax.ppermute(terms, 'k', swap)  8.79 us
    all_to_all x1, starting transfers between devices, local(): lax.all_to_all(share, ('k', 'col'), split_axis=0, concat_axis=0, tiled=True)  8.02 us
    pallas_call x1, Pallas kernels, tile_terms(): pl.pallas_call(terms_kernel, out_shape=sds((TILES_DEV + 1, F_LOC, TB), BF...  3.64 us
  transfers between devices with their start and end apart: 4, of which 4 were waited for; matrix products, arithmetic and copies ran while one was open for 0% of the time, Pallas kernels for 3%

profile of v2, /device:TPU:1, one launch (start us, length us, event | category | flops | bytes accessed | tf_op | source)
XLA Modules:
  0.0 144.3 jit_solution(3970443572354112940)
XLA Ops:
  0.6 0.0 copy-start.7
  1.3 0.0 copy-start.2
  1.3 0.0 copy-start.6
  1.3 3.6 %shard_map.137.own = bf16[65,16,128]{2,1,0:T(8,128)(2,1)} custom-call(s32[64]{0:T(128)} %src.1, s32[1,64]{1,0:T(1,128)} %bitcast.10, s32[1]{0:T(128)S(6)} %copy.21.count_h.count, bf16[16,1024]{1,0:T(8,128)(2,1)} %feats.1, bf16[64,128,128]{2,1,0:T(8,128)(2,1)} %vals.1), custom_call_target="tpu_custom_call" | custom-call | tf_op jit(solution)/shard_map/pallas_call | solution.py:93
  5.0 8.8 %collective-permute-start = (bf16[65,16,128]{2,1,0:T(8,128)(2,1)}, bf16[65,16,128]{2,1,0:T(8,128)(2,1)S(1)}, u32[]{:S(2)}, u32[]{:S(2)}) collective-permute-start(bf16[65,16,128]{2,1,0:T(8,128)(2,1)} %shard_map.137.own), channel_id=1, source_target_pairs={{0,8},{8,0},{1,9},{9,1},{2,10},{10,2},{3,11},{11,3},{4,12},{12,4},... | collective-permute-start | bytes 798728 | tf_op jit(solution)/shard_map/ppermute | solution.py:320
  13.8 1.4 collective-permute-done.other
  15.1 0.0 copy-done.7
  15.1 0.0 copy-start.1
  15.1 0.9 copy-done.1
  16.1 2.2 %shard_map.138 = (bf16[256,16,128]{2,1,0:T(8,128)(2,1)S(1)}, s32[1,128]{1,0:T(1,128)S(1)}) custom-call(s32[64]{0:T(128)S(1)} %copy-done.7, s32[1]{0:T(128)S(6)} %copy.21.count_h.count, bf16[65,16,128]{2,1,0:T(8,128)(2,1)S(1)} %copy-done.1, bf16[65,16,128]{2,1,0:T(8,128)(2,1)S(1)} %collective-permute-done.other), custom_call_target="tpu_custom_call" | custom-call | tf_op jit(solution)/shard_map/pallas_call | solution.py:321
  18.3 0.0 copy-start.3
  18.3 0.0 copy-start.4
  18.3 0.0 copy-start.5
  18.3 0.0 copy-start.9
  18.4 34.2 %all_to_all.46.recv = bf16[32,8,16,128]{3,2,1,0:T(8,128)(2,1)S(1)} all-to-all(bf16[32,8,16,128]{3,2,1,0:T(8,128)(2,1)S(1)} %bitcast.7), channel_id=1, replica_groups=mesh['y'=8,'zl'=4,'k'=2,'col'=8] {'y','zl'}, dimensions={0} | all-to-all | bytes 2097152 | tf_op jit(solution)/shard_map/all_to_all | solution.py:332
  52.6 0.0 copy-done.2
  52.6 0.0 copy-done.6
  52.6 0.2 shard_map.139
  52.7 18.7 %all_to_all.47.recv = bf16[8,32,128]{2,1,0:T(8,128)(2,1)S(1)} all-to-all(bf16[8,32,128]{2,1,0:T(8,128)(2,1)S(1)} %shard_map.139), channel_id=1, replica_groups=mesh['y'=8,'zl'=4,'k'=2,'col'=8] {'col'}, dimensions={0} | all-to-all | bytes 131072 | tf_op jit(solution)/shard_map/all_to_all | solution.py:338
  71.4 0.0 copy-done.3
  71.4 0.0 copy-done.4
  71.4 0.0 copy-done.5
  71.4 0.0 copy-done.9
  71.4 1.2 shard_map.140
  72.6 3.4 %all-to-all-start.6 = ((bf16[8,112,128]{2,1,0:T(8,128)(2,1)}), bf16[8,112,128]{2,1,0:T(8,128)(2,1)S(1)}, u32[]{:S(2)}, u32[]{:S(2)}) async-start(bf16[8,112,128]{2,1,0:T(8,128)(2,1)} %get-tuple-element.26), calls=%async_computation.6 | async-start | bytes 458752 | tf_op jit(solution)/shard_map/all_to_all | solution.py:344
  76.1 9.8 %all-to-all-done.6.recv = bf16[8,112,128]{2,1,0:T(8,128)(2,1)S(1)} async-done(((bf16[8,112,128]{2,1,0:T(8,128)(2,1)}), bf16[8,112,128]{2,1,0:T(8,128)(2,1)S(1)}, u32[]{:S(2)}, u32[]{:S(2)}) %all-to-all-start.6) | async-done | bytes 229408 | tf_op jit(solution)/shard_map/all_to_all | solution.py:344
  85.8 0.0 copy-start
  85.8 37.7 %conditional.1 = (bf16[296,16,128]{2,1,0:T(8,128)(2,1)}, bf16[16,64,128]{2,1,0:T(8,128)(2,1)}, bf16[16,128]{1,0:T(8,128)(2,1)S(1)}) conditional(s32[]{:T(128)} %convert_element_type.3, bf16[8,112,128]{2,1,0:T(8,128)(2,1)S(1)} %all-to-all-done.6.recv, bf16[8,112,128]{2,1,0:T(8,128)(2,1)S(1)} %all-to-all-done.6.recv), branch_computations={%region_0.0_spmd, %region_1.0_spmd} | conditional | bytes 3276824 | solution.py:365
  85.8 0.1 branch_0_fun.3
  85.9 15.0 %all_to_all.42.recv = bf16[8,13,16,128]{3,2,1,0:T(8,128)(2,1)S(1)} all-to-all(bf16[8,13,16,128]{3,2,1,0:T(8,128)(2,1)S(1)} %branch_0_fun.3), channel_id=1, replica_groups=mesh['y'=8,'zl'=4,'k'=2,'col'=8] {'y'}, dimensions={0} | all-to-all | bytes 851968 | tf_op jit(solution)/shard_map/cond/branch_0_fun/all_to_all | solution.py:353
  100.9 0.1 branch_0_fun.4
  101.1 20.5 %all_to_all.43.recv = bf16[4,74,16,128]{3,2,1,0:T(8,128)(2,1)} all-to-all(bf16[4,74,16,128]{3,2,1,0:T(8,128)(2,1)S(1)} %branch_0_fun.4), channel_id=1, replica_groups=mesh['y'=8,'zl'=4,'k'=2,'col'=8] {'zl'}, dimensions={0} | all-to-all | bytes 2424832 | tf_op jit(solution)/shard_map/cond/branch_0_fun/all_to_all | solution.py:355
  121.5 2.0 %branch_0_fun.5 = (bf16[16,64,128]{2,1,0:T(8,128)(2,1)}, bf16[16,128]{1,0:T(8,128)(2,1)S(1)}) custom-call(bf16[4,74,16,128]{3,2,1,0:T(8,128)(2,1)} %all_to_all.43.recv), custom_call_target="tpu_custom_call" | custom-call | tf_op jit(solution)/shard_map/cond/branch_0_fun/pallas_call | solution.py:356
  123.5 0.0 copy-start.8
  123.5 8.0 %all-to-all-start.7 = ((bf16[16,64,128]{2,1,0:T(8,128)(2,1)}), bf16[16,64,128]{2,1,0:T(8,128)(2,1)S(1)}, u32[]{:S(2)}, u32[]{:S(2)}) async-start(bf16[16,64,128]{2,1,0:T(8,128)(2,1)} %get-tuple-element.31), calls=%async_computation.7 | async-start | bytes 524288 | tf_op jit(solution)/shard_map/all_to_all | solution.py:368
  131.5 2.6 %shard_map.141 = (bf16[64,16,128]{2,1,0:T(8,128)(2,1)S(1)}, bf16[65,16,128]{2,1,0:T(8,128)(2,1)S(1)}) custom-call(s32[64]{0:T(128)S(1)} %copy-done.7, s32[1]{0:T(128)S(6)} %copy.21.count_h.count, s32[1,128]{1,0:T(1,128)S(1)} %get-tuple-element.25.dest_other, bf16[296,16,128]{2,1,0:T(8,128)(2,1)} %get-tuple-element.27.recv, ...), custom_call_target="tpu_custom_call" | custom-call | bytes 4320000 | tf_op jit(solution)/shard_map/pallas_call | solution.py:369
  134.1 2.1 %collective-permute-start.1 = (bf16[65,16,128]{2,1,0:T(8,128)(2,1)S(1)}, bf16[65,16,128]{2,1,0:T(8,128)(2,1)S(1)}, u32[]{:S(2)}, u32[]{:S(2)}) collective-permute-start(bf16[65,16,128]{2,1,0:T(8,128)(2,1)S(1)} %get-tuple-element.30), channel_id=1, source_target_pairs={{0,8},{8,0},{1,9},{9,1},{2,10},{10,2},{3,11},{11,3},{4,12},{12,4},... | collective-permute-start | bytes 798728 | tf_op jit(solution)/shard_map/ppermute | solution.py:375
  136.2 1.3 collective-permute-done.1.given
  137.6 0.0 copy-done
  137.6 0.0 copy-done.8
  137.6 2.2 %shard_map.142 = bf16[16,1024]{1,0:T(8,128)(2,1)} custom-call(s32[64]{0:T(128)S(1)} %copy-done.8, bf16[64,16,128]{2,1,0:T(8,128)(2,1)S(1)} %get-tuple-element.29.own, bf16[65,16,128]{2,1,0:T(8,128)(2,1)S(1)} %collective-permute-done.1.given, bf16[8,112,128]{2,1,0:T(8,128)(2,1)S(1)} %all-to-all-done.6.recv, bf16[64,128,128]{2,1,0:T(8,128)(2,1)S(1)} %copy-done), custom_call_target="tpu_custom_call" | custom-call | bytes 7920000 | tf_op jit(solution)/shard_map/pallas_call | solution.py:265
  139.8 3.6 %all-to-all-done.7.x = bf16[16,64,128]{2,1,0:T(8,128)(2,1)S(1)} async-done(((bf16[16,64,128]{2,1,0:T(8,128)(2,1)}), bf16[16,64,128]{2,1,0:T(8,128)(2,1)S(1)}, u32[]{:S(2)}, u32[]{:S(2)}) %all-to-all-start.7) | async-done | bytes 262176 | tf_op jit(solution)/shard_map/all_to_all | solution.py:368
  143.4 0.9 shard_map.143
Async XLA Ops:
  0.6 14.5 %copy-start.7 = (s32[64]{0:T(128)S(1)}, s32[64]{0:T(128)}, u32[]{:S(2)}) copy-start(s32[64]{0:T(128)} %dest_own.3) | copy-start | bytes 772
  1.3 51.3 %copy-start.2 = (bf16[16,1024]{1,0:T(8,128)(2,1)S(1)}, bf16[16,1024]{1,0:T(8,128)(2,1)}, u32[]{:S(2)}) copy-start(bf16[16,1024]{1,0:T(8,128)(2,1)} %feats.1) | copy-start | bytes 98308
  1.3 51.3 %copy-start.6 = (s32[1024]{0:T(1024)S(1)}, s32[1024]{0:T(1024)}, u32[]{:S(2)}) copy-start(s32[1024]{0:T(1024)} %param.17) | copy-start | bytes 12292
  5.0 10.2 %collective-permute-start = (bf16[65,16,128]{2,1,0:T(8,128)(2,1)}, bf16[65,16,128]{2,1,0:T(8,128)(2,1)S(1)}, u32[]{:S(2)}, u32[]{:S(2)}) collective-permute-start(bf16[65,16,128]{2,1,0:T(8,128)(2,1)} %shard_map.137.own), channel_id=1, source_target_pairs={{0,8},{8,0},{1,9},{9,1},{2,10},{10,2},{3,11},{11,3},{4,12},{12,4},... | collective-permute-start | bytes 798728 | tf_op jit(solution)/shard_map/ppermute | solution.py:320
  15.1 1.0 copy-start.1
  18.3 53.1 %copy-start.3 = (bf16[128,256]{1,0:T(8,128)(2,1)S(1)}, bf16[128,256]{1,0:T(8,128)(2,1)}, u32[]{:S(2)}) copy-start(bf16[128,256]{1,0:T(8,128)(2,1)} %w_self.1) | copy-start | bytes 196612
  18.3 53.1 %copy-start.4 = (bf16[128,256]{1,0:T(8,128)(2,1)S(1)}, bf16[128,256]{1,0:T(8,128)(2,1)}, u32[]{:S(2)}) copy-start(bf16[128,256]{1,0:T(8,128)(2,1)} %w_neigh.1) | copy-start | bytes 196612
  18.3 53.1 %copy-start.5 = (bf16[256,128]{1,0:T(8,128)(2,1)S(1)}, bf16[256,128]{1,0:T(8,128)(2,1)}, u32[]{:S(2)}) copy-start(bf16[256,128]{1,0:T(8,128)(2,1)} %cot.1) | copy-start | bytes 196612
  18.3 53.1 %copy-start.9 = (f32[256]{0:T(256)S(1)}, f32[256]{0:T(256)}, u32[]{:S(2)}) copy-start(f32[256]{0:T(256)} %param.20) | copy-start | bytes 3076
  72.6 13.2 %all-to-all-start.6 = ((bf16[8,112,128]{2,1,0:T(8,128)(2,1)}), bf16[8,112,128]{2,1,0:T(8,128)(2,1)S(1)}, u32[]{:S(2)}, u32[]{:S(2)}) async-start(bf16[8,112,128]{2,1,0:T(8,128)(2,1)} %get-tuple-element.26), calls=%async_computation.6 | async-start | bytes 458752 | tf_op jit(solution)/shard_map/all_to_all | solution.py:344
  85.8 51.7 %copy-start = (bf16[64,128,128]{2,1,0:T(8,128)(2,1)S(1)}, bf16[64,128,128]{2,1,0:T(8,128)(2,1)}, u32[]{:S(2)}) copy-start(bf16[64,128,128]{2,1,0:T(8,128)(2,1)} %vals.1) | copy-start | bytes 6291460
  123.5 14.1 %copy-start.8 = (s32[64]{0:T(128)S(1)}, s32[64]{0:T(128)}, u32[]{:S(2)}) copy-start(s32[64]{0:T(128)} %src.1) | copy-start | bytes 772
  123.5 19.9 %all-to-all-start.7 = ((bf16[16,64,128]{2,1,0:T(8,128)(2,1)}), bf16[16,64,128]{2,1,0:T(8,128)(2,1)S(1)}, u32[]{:S(2)}, u32[]{:S(2)}) async-start(bf16[16,64,128]{2,1,0:T(8,128)(2,1)} %get-tuple-element.31), calls=%async_computation.7 | async-start | bytes 524288 | tf_op jit(solution)/shard_map/all_to_all | solution.py:368
  134.1 3.4 %collective-permute-start.1 = (bf16[65,16,128]{2,1,0:T(8,128)(2,1)S(1)}, bf16[65,16,128]{2,1,0:T(8,128)(2,1)S(1)}, u32[]{:S(2)}, u32[]{:S(2)}) collective-permute-start(bf16[65,16,128]{2,1,0:T(8,128)(2,1)S(1)} %get-tuple-element.30), channel_id=1, source_target_pairs={{0,8},{8,0},{1,9},{9,1},{2,10},{10,2},{3,11},{11,3},{4,12},{12,4},... | collective-permute-start | bytes 798728 | tf_op jit(solution)/shard_map/ppermute | solution.py:375

commit v3 on v2

--- a/solution.py
+++ b/solution.py
@@ -13,6 +13,7 @@
 RB = 8
 F_LOC = 16
 Y = 8
+NX = 4
 STEP = 16
 EXTRA = 5
 
@@ -20,13 +21,14 @@
 BF = jnp.bfloat16
 F32 = jnp.float32
 
-AXES = ("y", "zl", "k", "col")
+AXES = ("y", "zl", "k", "zh", "x")
+COL = ("zh", "x")
 VTX = ("y", "zl", "k")
-YZ = ("y", "zl")
 
 VMEM = pl.BlockSpec(memory_space=pltpu.VMEM)
 SMEM = pl.BlockSpec(memory_space=pltpu.SMEM)
 HBM = pl.BlockSpec(memory_space=pltpu.HBM)
+ANY = pl.BlockSpec(memory_space=pl.ANY)
 PARAMS = pltpu.CompilerParams(vmem_limit_bytes=32 * 1024 * 1024)
 FULL_PARAMS = pltpu.CompilerParams(vmem_limit_bytes=59 * 1024 * 1024)
 
@@ -108,8 +110,12 @@
     )(src, dest, count, feats, vals)
 
 
-def dense_kernel(dest_own, count, own, other, out, dest_other, acc, coded, sem):
+def dense_kernel(ny, nz, dest_own, count, own, other, feats, out, dest_other, acc, coded, sem):
     k = lax.axis_index("k")
+    size = ny * NX + NX
+    of_y = jnp.where(k == 0, NX, 2 * nz * size // ny)
+    of_z = jnp.where(k == 0, size, RB)
+    of_zh = jnp.where(k == 0, nz * size, NX)
     dump = acc.shape[0] - 1
     given = other[TILES_DEV].astype(F32)
     coded[...] = (given[0:1] * 8.0 + given[1:2]).astype(jnp.int32)
@@ -119,7 +125,10 @@
 
     def add_to(d, used, term):
         mine = jnp.logical_and(used, ((d >> 3) & 1) == k)
-        at = jnp.where(mine, (d >> 4) * RB + (d & 7), dump)
+        place = d >> 4
+        at = (place // nz) * of_y + (place % nz) * of_z
+        at = at + ((d & 7) // NX) * of_zh + (d & 7) % NX
+        at = jnp.where(mine, at, dump)
         acc[at] = acc[at] + term.astype(F32)
 
     def add_own(s, carry):
@@ -137,13 +146,54 @@
     lax.fori_loop(0, TILES_DEV, add_other, 0, unroll=8)
     out[...] = acc[0:dump].astype(BF)
 
-
-def agg_kernel(recv, degree, feats, out):
+    @pl.when(k == 0)
+    def _():
+        for m in range(2 * nz):
+            for x in range(NX):
+                b = (m // nz) * NX + x
+                out[m * size + ny * NX + x] = feats[:, b * TB : (b + 1) * TB]
+
+
+def middle_first_kernel(nz, recv, out):
+    ny = out.shape[0] // NX
+    here = lax.axis_index("zl")
+    for h in range(2):
+        for n in range(ny * NX):
+            total = recv[h * nz, n].astype(F32)
+            for z in range(1, nz):
+                total = total + recv[h * nz + z, n].astype(F32)
+            out[n, h * F_LOC : (h + 1) * F_LOC] = total.astype(BF)
+        for x in range(NX):
+            tile = recv[h * nz + here, ny * NX + x]
+            for y in range(ny):
+                out[y * NX + x, (2 + h) * F_LOC : (3 + h) * F_LOC] = tile
+
+
+def middle_second_kernel(recv, feats, out):
+    places = out.shape[0] // RB
     for b in range(RB):
-        total = jnp.sum(recv[:, b].astype(F32), axis=0)
-        deg = degree[b : b + 1, :].astype(F32)
-        out[b, 0:F_LOC] = (total / deg).astype(BF)
-        out[b, F_LOC : 2 * F_LOC] = feats[:, b * TB : (b + 1) * TB]
+        own = feats[:, b * TB : (b + 1) * TB]
+        for p in range(places):
+            total = jnp.sum(recv[:, p * RB + b].astype(F32), axis=0)
+            out[p * RB + b, 0:F_LOC] = total.astype(BF)
+            out[p * RB + b, F_LOC : 2 * F_LOC] = own
+
+
+def agg_kernel(first_core, recv, degree, out):
+    halves = 2 if first_core else 1
+    size = RB // halves
+    places = recv.shape[0] // size
+    here = lax.axis_index("y" if first_core else "zl") * size
+    deg = degree[pl.ds(lax.axis_index(COL), 1), :].astype(F32)
+    for c in range(RB):
+        h, n = c // size, c % size
+        rows = slice(h * F_LOC, (h + 1) * F_LOC)
+        total = recv[n, rows].astype(F32)
+        for p in range(1, places):
+            total = total + recv[p * size + n, rows].astype(F32)
+        out[c, 0:F_LOC] = (total / deg).astype(BF)
+        rows = slice((halves + h) * F_LOC, (halves + h + 1) * F_LOC)
+        out[c, F_LOC : 2 * F_LOC] = recv[here + n, rows]
 
 
 def dense_layer_kernel(recv, w_self, w_neigh, bias, cot, degree, hidden, out):
@@ -166,7 +216,7 @@
     part_bias = lax.dot_general(ones, grad_pre, last, preferred_element_type=F32)[0:1]
     dx_self = jnp.dot(ws, grad_pre, preferred_element_type=F32).astype(BF)
     dagg = jnp.dot(wn, grad_pre, preferred_element_type=F32).astype(BF)
-    deg = degree[pl.ds(lax.axis_index("col"), 1), :].astype(F32)
+    deg = degree[pl.ds(lax.axis_index(COL), 1), :].astype(F32)
     dsum = (dagg.astype(F32) / deg).astype(BF)
     two = jnp.concatenate([part_bias[:, 0:TB], part_bias[:, TB:]], axis=0)
     high = two.astype(BF).astype(F32)
@@ -210,11 +260,20 @@
             out[p, came * RB + n] = sums[n]
 
 
-def share_kernel(first, recv, out, bias_out):
-    sums = [jnp.sum(recv[:, first + n].astype(F32), axis=0) for n in range(EXTRA)]
+def share_kernel(first, recv_h, out, bias_out, recv, sems):
+    copies = [
+        pltpu.make_async_copy(recv_h.at[p, pl.ds(first, EXTRA)], recv.at[p], sems.at[p])
+        for p in range(recv.shape[0])
+    ]
+    for copy in copies:
+        copy.start()
+    for copy in copies:
+        copy.wait()
+    sums = [jnp.sum(recv[:, n].astype(F32), axis=0) for n in range(EXTRA)]
+    rows = [x.astype(BF) for x in sums[:4]]
     for p in range(out.shape[0]):
         for n in range(4):
-            out[p, n * F_LOC : (n + 1) * F_LOC] = sums[n].astype(BF)
+            out[p, n * F_LOC : (n + 1) * F_LOC] = rows[n]
     bias_out[...] = parted(sums[4])
 
 
@@ -310,7 +369,7 @@
     bias,
     cotangent,
 ):
-    places = lax.axis_size(YZ)
+    ny, nz = lax.axis_size("y"), lax.axis_size("zl")
     swap = [(0, 1), (1, 0)]
     degree2 = degree.reshape(RB, TB)
 
@@ -318,45 +377,68 @@
         tile_source, tile_dest.reshape(1, -1), tile_count, features, tile_values
     )
     terms_other = lax.ppermute(terms, "k", swap)
+    sent = 2 * nz * (ny + 1) * NX
     dense, dest_other = whole(
-        dense_kernel,
-        (sds((places * RB, F_LOC, TB), BF), sds((1, TB), jnp.int32)),
-        [SMEM, SMEM, VMEM, VMEM],
+        functools.partial(dense_kernel, ny, nz),
+        (sds((sent, F_LOC, TB), BF), sds((1, TB), jnp.int32)),
+        [SMEM, SMEM, VMEM, VMEM, VMEM],
         [
-            pltpu.VMEM((places * RB + 1, F_LOC, TB), F32),
+            pltpu.VMEM((sent + 1, F_LOC, TB), F32),
             pltpu.VMEM((1, TB), jnp.int32),
             pltpu.SemaphoreType.DMA,
         ],
         [VMEM, SMEM],
-    )(tile_dest, tile_count, terms, terms_other)
-    summed = lax.all_to_all(
-        dense.reshape(places, RB, F_LOC, TB), YZ, split_axis=0, concat_axis=0, tiled=True
-    )
-    packed = whole(agg_kernel, sds((RB, 2 * F_LOC, TB), BF), [VMEM] * 3)(
-        summed, degree2, features
-    )
-    full = lax.all_to_all(packed, "col", split_axis=0, concat_axis=0, tiled=True)
+    )(tile_dest, tile_count, terms, terms_other, features)
+
+    def exchange(array, axes):
+        return lax.all_to_all(array, axes, split_axis=0, concat_axis=0, tiled=True)
+
+    def first_collect(dense, features, degree2):
+        one = exchange(dense.reshape(2 * nz, (ny + 1) * NX, F_LOC, TB), ("zh", "zl"))
+        two = whole(
+            functools.partial(middle_first_kernel, nz),
+            sds((ny * NX, 4 * F_LOC, TB), BF),
+            [VMEM],
+        )(one)
+        two = exchange(two, ("y", "x"))
+        return whole(
+            functools.partial(agg_kernel, True), sds((RB, 2 * F_LOC, TB), BF), [VMEM] * 2
+        )(two, degree2)
+
+    def second_collect(dense, features, degree2):
+        one = exchange(dense.reshape(ny, sent // ny, F_LOC, TB), "y")
+        two = whole(middle_second_kernel, sds((nz * RB, 2 * F_LOC, TB), BF), [VMEM] * 2)(
+            one, features
+        )
+        two = exchange(two, ("zl",) + COL)
+        return whole(
+            functools.partial(agg_kernel, False), sds((RB, 2 * F_LOC, TB), BF), [VMEM] * 2
+        )(two, degree2)
+
+    full = lax.cond(
+        lax.axis_index("k") == 0, first_collect, second_collect, dense, features, degree2
+    )
     hidden, back = whole(
         dense_layer_kernel,
         (sds(cotangent.shape, BF), sds((RB, 112, TB), BF)),
         [VMEM] * 6,
     )(full, w_self, w_neigh, bias.reshape(1, -1), cotangent, degree2)
-    back = lax.all_to_all(back, "col", split_axis=0, concat_axis=0, tiled=True)
-
-    ny, nz = lax.axis_size("y"), lax.axis_size("zl")
+    back = exchange(back, COL)
+
     tiles = ny * (nz * RB + EXTRA)
 
     def in_two_steps(first, second):
         def run(back):
             n1, n2 = lax.axis_size(first), lax.axis_size(second)
             one = whole(first_step_kernel, sds((n1, RB + EXTRA, F_LOC, TB), BF), [VMEM])(back)
-            one = lax.all_to_all(one, first, split_axis=0, concat_axis=0, tiled=True)
+            one = exchange(one, first)
             two = whole(second_step_kernel, sds((n2, tiles // n2, F_LOC, TB), BF), [VMEM])(one)
-            two = lax.all_to_all(two, second, split_axis=0, concat_axis=0, tiled=True)
+            two = exchange(two, second)
             share, bias_sum = whole(
                 functools.partial(share_kernel, n1 * RB),
                 (sds((2 * RB, 64, TB), BF), sds((F_LOC, TB), BF)),
-                [VMEM],
+                [ANY],
+                [pltpu.VMEM((n2, EXTRA, F_LOC, TB), BF), pltpu.SemaphoreType.DMA((n2,))],
             )(two)
             return two.reshape(tiles, F_LOC, TB), share, bias_sum
 
@@ -365,7 +447,7 @@
     portion, share, bias_sum = lax.cond(
         lax.axis_index("k") == 0, in_two_steps("zl", "y"), in_two_steps("y", "zl"), back
     )
-    chunks = lax.all_to_all(share, ("k", "col"), split_axis=0, concat_axis=0, tiled=True)
+    chunks = exchange(share, ("k",) + COL)
     own, other = whole(
         functools.partial(pick_kernel, ny, nz),
         (sds((TILES_DEV, F_LOC, TB), BF), sds((TILES_DEV + 1, F_LOC, TB), BF)),
@@ -384,9 +466,9 @@
 
 def solution(mesh):
     vtx, col = mesh.shape["vtx"], mesh.shape["col"]
-    fine = Mesh(mesh.devices.reshape(Y, vtx // (2 * Y), 2, col), AXES)
+    fine = Mesh(mesh.devices.reshape(Y, vtx // (2 * Y), 2, 2, col // 2), AXES)
     placed = (
-        P("col", VTX),
+        P(COL, VTX),
         P(VTX, None, None),
         P(VTX),
         P(VTX),
@@ -401,6 +483,6 @@
         local,
         mesh=fine,
         in_specs=placed,
-        out_specs=(P(None, AXES), P("col", VTX), P(), P(), P()),
+        out_specs=(P(None, AXES), P(COL, VTX), P(), P(), P()),
         check_vma=False,
     )

time: 145 us -> 137 us (0.945)
  waiting for transfers between devices: 16.1 us -> 6.29 us
  blocking collectives: 88.3 us -> 91.4 us
  starting transfers between devices: 22.3 us -> 20.7 us
    all_to_all x2 -> x1, waiting for transfers between devices: 13.4 us -> 3.6 us  [exchange(): return lax.all_to_all(array, axes, split_axis=0, concat_axis=0, tiled=True)]
    all_to_all x4 -> x5, blocking collectives: 88.3 us -> 91.4 us  [exchange(): return lax.all_to_all(array, axes, split_axis=0, concat_axis=0, tiled=True)]
    all_to_all x2 -> x1, starting transfers between devices: 11.4 us -> 9.86 us  [exchange(): return lax.all_to_all(array, axes, split_axis=0, concat_axis=0, tiled=True)]
    pallas_call x2 -> x3, Pallas kernels: 2.38 us -> 3.34 us  [the longest x1 3.18 us: local(): whole(functools.partial(dense_kernel, ny, nz), (sds((sent, F_LOC, TB), BF...]
  transfers between devices with their start and end apart: 4 -> 3, of which waited for: 4 -> 3; matrix products, arithmetic and copies ran while one was open for 0% -> 0% of each run, Pallas kernels for 3% -> 4%
where the time goes in v3:
time: 137 us; the launch traced here: 136 us
  blocking collectives  91.4 us (67%)
  starting transfers between devices  20.7 us (15%)
  Pallas kernels  15.1 us (11%)
  waiting for transfers between devices  6.29 us (5%)
  between operations  1.47 us (1%)
    all_to_all x5, blocking collectives, exchange(): return lax.all_to_all(array, axes, split_axis=0, concat_axis=0, tiled=True)  91.4 us
    all_to_all x1, starting transfers between devices, exchange(): return lax.all_to_all(array, axes, split_axis=0, concat_axis=0, tiled=True)  9.86 us
    ppermute x1, starting transfers between devices, local(): terms_other = lax.ppermute(terms, 'k', swap)  8.79 us
    all_to_all x1, waiting for transfers between devices, exchange(): return lax.all_to_all(array, axes, split_axis=0, concat_axis=0, tiled=True)  3.6 us
    pallas_call x1, Pallas kernels, tile_terms(): pl.pallas_call(terms_kernel, out_shape=sds((TILES_DEV + 1, F_LOC, TB), BF...  3.41 us
    pallas_call x1, Pallas kernels, local(): whole(functools.partial(dense_kernel, ny, nz), (sds((sent, F_LOC, TB), BF...  3.18 us
  transfers between devices with their start and end apart: 3, of which 3 were waited for; matrix products, arithmetic and copies ran while one was open for 0% of the time, Pallas kernels for 4%

profile of v3, /device:TPU:1, one launch (start us, length us, event | category | flops | bytes accessed | tf_op | source)
XLA Modules:
  0.0 136.1 jit_solution(10354025566170880209)
XLA Ops:
  0.6 0.0 copy-start.8
  0.6 0.0 copy-start.5
  1.3 0.0 copy-start.9
  1.3 3.4 %shard_map.137.own = bf16[65,16,128]{2,1,0:T(8,128)(2,1)} custom-call(s32[64]{0:T(128)} %src.1, s32[1,64]{1,0:T(1,128)} %bitcast.8, s32[1]{0:T(128)S(6)} %copy.23.count_h.count, bf16[16,1024]{1,0:T(8,128)(2,1)} %feats.1, bf16[64,128,128]{2,1,0:T(8,128)(2,1)} %vals.1), custom_call_target="tpu_custom_call" | custom-call | tf_op jit(solution)/shard_map/pallas_call | solution.py:95
  4.7 8.8 %collective-permute-start = (bf16[65,16,128]{2,1,0:T(8,128)(2,1)}, bf16[65,16,128]{2,1,0:T(8,128)(2,1)S(1)}, u32[]{:S(2)}, u32[]{:S(2)}) collective-permute-start(bf16[65,16,128]{2,1,0:T(8,128)(2,1)} %shard_map.137.own), channel_id=1, source_target_pairs={{0,8},{8,0},{1,9},{9,1},{2,10},{10,2},{3,11},{11,3},{4,12},{12,4},... | collective-permute-start | bytes 798728 | tf_op jit(solution)/shard_map/ppermute | solution.py:379
  13.6 1.3 collective-permute-done.other
  14.9 0.0 copy-done.8
  14.9 0.0 copy-done.5
  14.9 0.0 copy-start.1
  14.9 1.0 copy-done.1
  15.9 3.2 %shard_map.138 = (bf16[288,16,128]{2,1,0:T(8,128)(2,1)S(1)}, s32[1,128]{1,0:T(1,128)S(1)}) custom-call(s32[64]{0:T(128)S(1)} %copy-done.5, s32[1]{0:T(128)S(6)} %copy.23.count_h.count, bf16[65,16,128]{2,1,0:T(8,128)(2,1)S(1)} %copy-done.1, bf16[65,16,128]{2,1,0:T(8,128)(2,1)S(1)} %collective-permute-done.other, bf16[16,1024]{1,0:T(8,128)(2,1)S(1)} %copy-done.8), custom_call_target="tpu_custom_call" | custom-call | tf_op jit(solution)/shard_map/pallas_call | solution.py:381
  19.0 0.0 copy-done.9
  19.1 0.0 copy-start.2
  19.1 0.0 copy-start.3
  19.1 0.0 copy-start.4
  19.1 0.0 copy-start.7
  19.1 44.1 %conditional.2 = (bf16[8,32,128]{2,1,0:T(8,128)(2,1)S(1)}) conditional(s32[]{:T(128)} %convert_element_type.4, (bf16[288,16,128]{2,1,0:T(8,128)(2,1)S(1)}, bf16[16,1024]{1,0:T(8,128)(2,1)S(1)}, s32[8,128]{1,0:T(8,128)S(1)}) %tuple.30, (bf16[288,16,128]{2,1,0:T(8,128)(2,1)S(1)}, s32[8,128]{1,0:T(8,128)S(1)}) %tuple.31), branch_computations={%region_0.0_spmd, %region_1.0_spmd} | conditional | bytes 3407880 | solution.py:418
  19.1 21.7 %all_to_all.48.recv = bf16[8,36,16,128]{3,2,1,0:T(8,128)(2,1)S(1)} all-to-all(bf16[8,36,16,128]{3,2,1,0:T(8,128)(2,1)S(1)} %bitcast.10), channel_id=1, replica_groups=mesh['y'=8,'zl'=4,'k'=2,'zh'=2,'x'=4] {'y'}, dimensions={0} | all-to-all | bytes 2359296 | tf_op jit(solution)/shard_map/cond/branch_0_fun/all_to_all | solution.py:394
  40.8 0.1 branch_0_fun.5
  41.0 22.3 %all_to_all.49.recv = bf16[32,32,128]{2,1,0:T(8,128)(2,1)S(1)} all-to-all(bf16[32,32,128]{2,1,0:T(8,128)(2,1)S(1)} %branch_0_fun.5), channel_id=1, replica_groups=mesh['y'=8,'zl'=4,'k'=2,'zh'=2,'x'=4] {'zl','zh','x'}, dimensions={0} | all-to-all | bytes 524288 | tf_op jit(solution)/shard_map/cond/branch_0_fun/all_to_all | solution.py:394
  63.3 0.0 copy-done.2
  63.3 0.0 copy-done.3
  63.3 0.0 copy-done.4
  63.3 0.0 copy-done.7
  63.3 0.9 shard_map.139
  64.2 12.8 %all_to_all.56.recv = bf16[8,112,128]{2,1,0:T(8,128)(2,1)S(1)} all-to-all(bf16[8,112,128]{2,1,0:T(8,128)(2,1)S(1)} %get-tuple-element.44), channel_id=1, replica_groups=mesh['y'=8,'zl'=4,'k'=2,'zh'=2,'x'=4] {'zh','x'}, dimensions={0} | all-to-all | bytes 458752 | tf_op jit(solution)/shard_map/all_to_all | solution.py:394
  77.0 0.0 copy-start
  77.0 36.5 %conditional.3 = (bf16[296,16,128]{2,1,0:T(8,128)(2,1)}, bf16[16,64,128]{2,1,0:T(8,128)(2,1)}, bf16[16,128]{1,0:T(8,128)(2,1)S(1)}) conditional(s32[]{:T(128)} %convert_element_type.4, bf16[8,112,128]{2,1,0:T(8,128)(2,1)S(1)} %all_to_all.56.recv, bf16[8,112,128]{2,1,0:T(8,128)(2,1)S(1)} %all_to_all.56.recv), branch_computations={%region_2.0_spmd, %region_3.0_spmd} | conditional | bytes 3276824 | solution.py:447
  77.0 0.1 branch_0_fun.7
  77.0 13.6 %all_to_all.52.recv = bf16[8,13,16,128]{3,2,1,0:T(8,128)(2,1)S(1)} all-to-all(bf16[8,13,16,128]{3,2,1,0:T(8,128)(2,1)S(1)} %branch_0_fun.7), channel_id=1, replica_groups=mesh['y'=8,'zl'=4,'k'=2,'zh'=2,'x'=4] {'y'}, dimensions={0} | all-to-all | bytes 851968 | tf_op jit(solution)/shard_map/cond/branch_0_fun/all_to_all | solution.py:394
  90.7 0.1 branch_0_fun.8
  90.8 21.1 %all_to_all.53.recv_h = bf16[4,74,16,128]{3,2,1,0:T(8,128)(2,1)} all-to-all(bf16[4,74,16,128]{3,2,1,0:T(8,128)(2,1)S(1)} %branch_0_fun.8), channel_id=1, replica_groups=mesh['y'=8,'zl'=4,'k'=2,'zh'=2,'x'=4] {'zl'}, dimensions={0} | all-to-all | bytes 2424832 | tf_op jit(solution)/shard_map/cond/branch_0_fun/all_to_all | solution.py:394
  111.9 1.5 %branch_0_fun.9 = (bf16[16,64,128]{2,1,0:T(8,128)(2,1)}, bf16[16,128]{1,0:T(8,128)(2,1)S(1)}) custom-call(bf16[4,74,16,128]{3,2,1,0:T(8,128)(2,1)} %all_to_all.53.recv_h), custom_call_target="tpu_custom_call" | custom-call | tf_op jit(solution)/shard_map/cond/branch_0_fun/pallas_call | solution.py:437
  113.5 0.0 copy-start.6
  113.5 9.9 %all-to-all-start.9 = ((bf16[16,64,128]{2,1,0:T(8,128)(2,1)}), bf16[16,64,128]{2,1,0:T(8,128)(2,1)S(1)}, u32[]{:S(2)}, u32[]{:S(2)}) async-start(bf16[16,64,128]{2,1,0:T(8,128)(2,1)} %get-tuple-element.49), calls=%async_computation.9 | async-start | bytes 524288 | tf_op jit(solution)/shard_map/all_to_all | solution.py:394
  123.3 2.6 %shard_map.140 = (bf16[64,16,128]{2,1,0:T(8,128)(2,1)S(1)}, bf16[65,16,128]{2,1,0:T(8,128)(2,1)S(1)}) custom-call(s32[64]{0:T(128)S(1)} %copy-done.5, s32[1]{0:T(128)S(6)} %copy.23.count_h.count, s32[1,128]{1,0:T(1,128)S(1)} %get-tuple-element.43.dest_other, bf16[296,16,128]{2,1,0:T(8,128)(2,1)} %get-tuple-element.45.recv, ...), custom_call_target="tpu_custom_call" | custom-call | bytes 4320000 | tf_op jit(solution)/shard_map/pallas_call | solution.py:451
  125.9 2.1 %collective-permute-start.1 = (bf16[65,16,128]{2,1,0:T(8,128)(2,1)S(1)}, bf16[65,16,128]{2,1,0:T(8,128)(2,1)S(1)}, u32[]{:S(2)}, u32[]{:S(2)}) collective-permute-start(bf16[65,16,128]{2,1,0:T(8,128)(2,1)S(1)} %get-tuple-element.48), channel_id=1, source_target_pairs={{0,8},{8,0},{1,9},{9,1},{2,10},{10,2},{3,11},{11,3},{4,12},{12,4},... | collective-permute-start | bytes 798728 | tf_op jit(solution)/shard_map/ppermute | solution.py:457
  128.0 1.3 collective-permute-done.1.given
  129.4 0.0 copy-done
  129.4 0.0 copy-done.6
  129.4 2.2 %shard_map.141 = bf16[16,1024]{1,0:T(8,128)(2,1)} custom-call(s32[64]{0:T(128)S(1)} %copy-done.6, bf16[64,16,128]{2,1,0:T(8,128)(2,1)S(1)} %get-tuple-element.47.own, bf16[65,16,128]{2,1,0:T(8,128)(2,1)S(1)} %collective-permute-done.1.given, bf16[8,112,128]{2,1,0:T(8,128)(2,1)S(1)} %all_to_all.56.recv, bf16[64,128,128]{2,1,0:T(8,128)(2,1)S(1)} %copy-done), custom_call_target="tpu_custom_call" | custom-call | bytes 7920000 | tf_op jit(solution)/shard_map/pallas_call | solution.py:324
  131.6 3.6 %all-to-all-done.9.x = bf16[16,64,128]{2,1,0:T(8,128)(2,1)S(1)} async-done(((bf16[16,64,128]{2,1,0:T(8,128)(2,1)}), bf16[16,64,128]{2,1,0:T(8,128)(2,1)S(1)}, u32[]{:S(2)}, u32[]{:S(2)}) %all-to-all-start.9) | async-done | bytes 262176 | tf_op jit(solution)/shard_map/all_to_all | solution.py:394
  135.2 0.9 shard_map.142
  (1 shorter events, 0.0 us)
Async XLA Ops:
  0.6 14.3 %copy-start.8 = (bf16[16,1024]{1,0:T(8,128)(2,1)S(1)}, bf16[16,1024]{1,0:T(8,128)(2,1)}, u32[]{:S(2)}) copy-start(bf16[16,1024]{1,0:T(8,128)(2,1)} %feats.1) | copy-start | bytes 98308
  0.6 14.3 %copy-start.5 = (s32[64]{0:T(128)S(1)}, s32[64]{0:T(128)}, u32[]{:S(2)}) copy-start(s32[64]{0:T(128)} %dest_own.3) | copy-start | bytes 772
  1.3 17.7 %copy-start.9 = (s32[1024]{0:T(1024)S(1)}, s32[1024]{0:T(1024)}, u32[]{:S(2)}) copy-start(s32[1024]{0:T(1024)} %param.19) | copy-start | bytes 12292
  4.7 10.2 %collective-permute-start = (bf16[65,16,128]{2,1,0:T(8,128)(2,1)}, bf16[65,16,128]{2,1,0:T(8,128)(2,1)S(1)}, u32[]{:S(2)}, u32[]{:S(2)}) collective-permute-start(bf16[65,16,128]{2,1,0:T(8,128)(2,1)} %shard_map.137.own), channel_id=1, source_target_pairs={{0,8},{8,0},{1,9},{9,1},{2,10},{10,2},{3,11},{11,3},{4,12},{12,4},... | collective-permute-start | bytes 798728 | tf_op jit(solution)/shard_map/ppermute | solution.py:379
  14.9 1.0 copy-start.1
  19.1 44.2 %copy-start.2 = (bf16[128,256]{1,0:T(8,128)(2,1)S(1)}, bf16[128,256]{1,0:T(8,128)(2,1)}, u32[]{:S(2)}) copy-start(bf16[128,256]{1,0:T(8,128)(2,1)} %w_self.1) | copy-start | bytes 196612
  19.1 44.2 %copy-start.3 = (bf16[128,256]{1,0:T(8,128)(2,1)S(1)}, bf16[128,256]{1,0:T(8,128)(2,1)}, u32[]{:S(2)}) copy-start(bf16[128,256]{1,0:T(8,128)(2,1)} %w_neigh.1) | copy-start | bytes 196612
  19.1 44.2 %copy-start.4 = (bf16[256,128]{1,0:T(8,128)(2,1)S(1)}, bf16[256,128]{1,0:T(8,128)(2,1)}, u32[]{:S(2)}) copy-start(bf16[256,128]{1,0:T(8,128)(2,1)} %cot.1) | copy-start | bytes 196612
  19.1 44.2 %copy-start.7 = (f32[256]{0:T(256)S(1)}, f32[256]{0:T(256)}, u32[]{:S(2)}) copy-start(f32[256]{0:T(256)} %param.22) | copy-start | bytes 3076
  77.0 52.4 %copy-start = (bf16[64,128,128]{2,1,0:T(8,128)(2,1)S(1)}, bf16[64,128,128]{2,1,0:T(8,128)(2,1)}, u32[]{:S(2)}) copy-start(bf16[64,128,128]{2,1,0:T(8,128)(2,1)} %vals.1) | copy-start | bytes 6291460
  113.5 15.9 %copy-start.6 = (s32[64]{0:T(128)S(1)}, s32[64]{0:T(128)}, u32[]{:S(2)}) copy-start(s32[64]{0:T(128)} %src.1) | copy-start | bytes 772
  113.5 21.7 %all-to-all-start.9 = ((bf16[16,64,128]{2,1,0:T(8,128)(2,1)}), bf16[16,64,128]{2,1,0:T(8,128)(2,1)S(1)}, u32[]{:S(2)}, u32[]{:S(2)}) async-start(bf16[16,64,128]{2,1,0:T(8,128)(2,1)} %get-tuple-element.49), calls=%async_computation.9 | async-start | bytes 524288 | tf_op jit(solution)/shard_map/all_to_all | solution.py:394
  125.9 3.4 %collective-permute-start.1 = (bf16[65,16,128]{2,1,0:T(8,128)(2,1)S(1)}, bf16[65,16,128]{2,1,0:T(8,128)(2,1)S(1)}, u32[]{:S(2)}, u32[]{:S(2)}) collective-permute-start(bf16[65,16,128]{2,1,0:T(8,128)(2,1)S(1)} %get-tuple-element.48), channel_id=1, source_target_pairs={{0,8},{8,0},{1,9},{9,1},{2,10},{10,2},{3,11},{11,3},{4,12},{12,4},... | collective-permute-start | bytes 798728 | tf_op jit(solution)/shard_map/ppermute | solution.py:457

commit v4 on v3

--- a/solution.py
+++ b/solution.py
@@ -113,9 +113,10 @@
 def dense_kernel(ny, nz, dest_own, count, own, other, feats, out, dest_other, acc, coded, sem):
     k = lax.axis_index("k")
     size = ny * NX + NX
-    of_y = jnp.where(k == 0, NX, 2 * nz * size // ny)
-    of_z = jnp.where(k == 0, size, RB)
-    of_zh = jnp.where(k == 0, nz * size, NX)
+    of_y = jnp.where(k == 1, NX, 2 * nz * size // ny)
+    of_z = jnp.where(k == 1, size, RB)
+    of_zh = jnp.where(k == 1, nz * size, NX)
+    bits = nz.bit_length() - 1
     dump = acc.shape[0] - 1
     given = other[TILES_DEV].astype(F32)
     coded[...] = (given[0:1] * 8.0 + given[1:2]).astype(jnp.int32)
@@ -125,9 +126,8 @@
 
     def add_to(d, used, term):
         mine = jnp.logical_and(used, ((d >> 3) & 1) == k)
-        place = d >> 4
-        at = (place // nz) * of_y + (place % nz) * of_z
-        at = at + ((d & 7) // NX) * of_zh + (d & 7) % NX
+        at = (d >> (4 + bits)) * of_y + ((d >> 4) & (nz - 1)) * of_z
+        at = at + ((d >> 2) & 1) * of_zh + (d & (NX - 1))
         at = jnp.where(mine, at, dump)
         acc[at] = acc[at] + term.astype(F32)
 
@@ -146,7 +146,7 @@
     lax.fori_loop(0, TILES_DEV, add_other, 0, unroll=8)
     out[...] = acc[0:dump].astype(BF)
 
-    @pl.when(k == 0)
+    @pl.when(k == 1)
     def _():
         for m in range(2 * nz):
             for x in range(NX):
@@ -154,7 +154,7 @@
                 out[m * size + ny * NX + x] = feats[:, b * TB : (b + 1) * TB]
 
 
-def middle_first_kernel(nz, recv, out):
+def middle_z_kernel(nz, recv, out):
     ny = out.shape[0] // NX
     here = lax.axis_index("zl")
     for h in range(2):
@@ -169,7 +169,7 @@
                 out[y * NX + x, (2 + h) * F_LOC : (3 + h) * F_LOC] = tile
 
 
-def middle_second_kernel(recv, feats, out):
+def middle_y_kernel(recv, feats, out):
     places = out.shape[0] // RB
     for b in range(RB):
         own = feats[:, b * TB : (b + 1) * TB]
@@ -179,11 +179,11 @@
             out[p * RB + b, F_LOC : 2 * F_LOC] = own
 
 
-def agg_kernel(first_core, recv, degree, out):
-    halves = 2 if first_core else 1
+def agg_kernel(z_first, recv, degree, out):
+    halves = 2 if z_first else 1
     size = RB // halves
     places = recv.shape[0] // size
-    here = lax.axis_index("y" if first_core else "zl") * size
+    here = lax.axis_index("y" if z_first else "zl") * size
     deg = degree[pl.ds(lax.axis_index(COL), 1), :].astype(F32)
     for c in range(RB):
         h, n = c // size, c % size
@@ -281,12 +281,12 @@
     k = lax.axis_index("k")
     of_y = jnp.where(k == 0, nz * RB + EXTRA, RB)
     of_z = jnp.where(k == 0, RB, ny * (nz * RB + EXTRA) // nz)
+    bits = nz.bit_length() - 1
 
     def pick(d, used):
         mine = jnp.logical_and(used, ((d >> 3) & 1) == k)
         d = jnp.where(mine, d, 0)
-        place = d >> 4
-        at = (place // nz) * of_y + (place % nz) * of_z + (d & 7)
+        at = (d >> (4 + bits)) * of_y + ((d >> 4) & (nz - 1)) * of_z + (d & 7)
         tile = recv[at]
         return jnp.where(mine, tile, jnp.zeros_like(tile))
 
@@ -393,10 +393,10 @@
     def exchange(array, axes):
         return lax.all_to_all(array, axes, split_axis=0, concat_axis=0, tiled=True)
 
-    def first_collect(dense, features, degree2):
+    def z_collect(dense, features, degree2):
         one = exchange(dense.reshape(2 * nz, (ny + 1) * NX, F_LOC, TB), ("zh", "zl"))
         two = whole(
-            functools.partial(middle_first_kernel, nz),
+            functools.partial(middle_z_kernel, nz),
             sds((ny * NX, 4 * F_LOC, TB), BF),
             [VMEM],
         )(one)
@@ -405,9 +405,9 @@
             functools.partial(agg_kernel, True), sds((RB, 2 * F_LOC, TB), BF), [VMEM] * 2
         )(two, degree2)
 
-    def second_collect(dense, features, degree2):
+    def y_collect(dense, features, degree2):
         one = exchange(dense.reshape(ny, sent // ny, F_LOC, TB), "y")
-        two = whole(middle_second_kernel, sds((nz * RB, 2 * F_LOC, TB), BF), [VMEM] * 2)(
+        two = whole(middle_y_kernel, sds((nz * RB, 2 * F_LOC, TB), BF), [VMEM] * 2)(
             one, features
         )
         two = exchange(two, ("zl",) + COL)
@@ -416,7 +416,7 @@
         )(two, degree2)
 
     full = lax.cond(
-        lax.axis_index("k") == 0, first_collect, second_collect, dense, features, degree2
+        lax.axis_index("k") == 1, z_collect, y_collect, dense, features, degree2
     )
     hidden, back = whole(
         dense_layer_kernel,

time: 137 us -> 136 us (level)
  waiting for transfers between devices: 6.29 us -> 16.8 us
  blocking collectives: 91.4 us -> 81 us
    all_to_all x1 -> x2, waiting for transfers between devices: 3.6 us -> 14.2 us  [exchange(): return lax.all_to_all(array, axes, split_axis=0, concat_axis=0, tiled=True)]
    all_to_all x5 -> x4, blocking collectives: 91.4 us -> 81 us  [exchange(): return lax.all_to_all(array, axes, split_axis=0, concat_axis=0, tiled=True)]
    all_to_all x1 -> x2, starting transfers between devices: 9.86 us -> 9.64 us  [exchange(): return lax.all_to_all(array, axes, split_axis=0, concat_axis=0, tiled=True)]
  transfers between devices with their start and end apart: 3 -> 4, of which waited for: 3 -> 4; matrix products, arithmetic and copies ran while one was open for 0% -> 0% of each run, Pallas kernels for 4% -> 3%
where the time goes in v4:
time: 136 us; the launch traced here: 135 us
  blocking collectives  81 us (60%)
  starting transfers between devices  20.5 us (15%)
  waiting for transfers between devices  16.8 us (12%)
  Pallas kernels  14.1 us (10%)
  between operations  1.48 us (1%)
    all_to_all x4, blocking collectives, exchange(): return lax.all_to_all(array, axes, split_axis=0, concat_axis=0, tiled=True)  81 us
    all_to_all x2, waiting for transfers between devices, exchange(): return lax.all_to_all(array, axes, split_axis=0, concat_axis=0, tiled=True)  14.2 us
    all_to_all x2, starting transfers between devices, exchange(): return lax.all_to_all(array, axes, split_axis=0, concat_axis=0, tiled=True)  9.64 us
    ppermute x1, starting transfers between devices, local(): terms_other = lax.ppermute(terms, 'k', swap)  8.78 us
    pallas_call x1, Pallas kernels, tile_terms(): pl.pallas_call(terms_kernel, out_shape=sds((TILES_DEV + 1, F_LOC, TB), BF...  3.42 us
  transfers between devices with their start and end apart: 4, of which 4 were waited for; matrix products, arithmetic and copies ran while one was open for 0% of the time, Pallas kernels for 3%

profile of v4, /device:TPU:1, one launch (start us, length us, event | category | flops | bytes accessed | tf_op | source)
XLA Modules:
  0.0 135.0 jit_solution(14333426784413889909)
XLA Ops:
  0.6 0.0 copy-start.8
  0.6 0.0 copy-start.5
  1.3 0.0 copy-start.9
  1.3 3.4 %shard_map.137.own = bf16[65,16,128]{2,1,0:T(8,128)(2,1)} custom-call(s32[64]{0:T(128)} %src.1, s32[1,64]{1,0:T(1,128)} %bitcast.8, s32[1]{0:T(128)S(6)} %copy.23.count_h.count, bf16[16,1024]{1,0:T(8,128)(2,1)} %feats.1, bf16[64,128,128]{2,1,0:T(8,128)(2,1)} %vals.1), custom_call_target="tpu_custom_call" | custom-call | tf_op jit(solution)/shard_map/pallas_call | solution.py:95
  4.8 8.8 %collective-permute-start = (bf16[65,16,128]{2,1,0:T(8,128)(2,1)}, bf16[65,16,128]{2,1,0:T(8,128)(2,1)S(1)}, u32[]{:S(2)}, u32[]{:S(2)}) collective-permute-start(bf16[65,16,128]{2,1,0:T(8,128)(2,1)} %shard_map.137.own), channel_id=1, source_target_pairs={{0,8},{8,0},{1,9},{9,1},{2,10},{10,2},{3,11},{11,3},{4,12},{12,4},... | collective-permute-start | bytes 798728 | tf_op jit(solution)/shard_map/ppermute | solution.py:379
  13.6 1.4 %collective-permute-done.other = bf16[65,16,128]{2,1,0:T(8,128)(2,1)S(1)} collective-permute-done((bf16[65,16,128]{2,1,0:T(8,128)(2,1)}, bf16[65,16,128]{2,1,0:T(8,128)(2,1)S(1)}, u32[]{:S(2)}, u32[]{:S(2)}) %collective-permute-start) | collective-permute-done | bytes 266272 | tf_op jit(solution)/shard_map/ppermute | solution.py:379
  14.9 0.0 copy-done.8
  14.9 0.0 copy-done.5
  14.9 0.0 copy-start.1
  14.9 1.0 copy-done.1
  15.9 2.4 %shard_map.138 = (bf16[288,16,128]{2,1,0:T(8,128)(2,1)S(1)}, s32[1,128]{1,0:T(1,128)S(1)}) custom-call(s32[64]{0:T(128)S(1)} %copy-done.5, s32[1]{0:T(128)S(6)} %copy.23.count_h.count, bf16[65,16,128]{2,1,0:T(8,128)(2,1)S(1)} %copy-done.1, bf16[65,16,128]{2,1,0:T(8,128)(2,1)S(1)} %collective-permute-done.other, bf16[16,1024]{1,0:T(8,128)(2,1)S(1)} %copy-done.8), custom_call_target="tpu_custom_call" | custom-call | tf_op jit(solution)/shard_map/pallas_call | solution.py:381
  18.3 0.0 copy-done.9
  18.3 0.0 copy-start.2
  18.3 0.0 copy-start.3
  18.3 0.0 copy-start.4
  18.3 0.0 copy-start.7
  18.3 46.4 %conditional.2 = (bf16[8,32,128]{2,1,0:T(8,128)(2,1)S(1)}) conditional(s32[]{:T(128)} %convert_element_type.6, (bf16[288,16,128]{2,1,0:T(8,128)(2,1)S(1)}, bf16[16,1024]{1,0:T(8,128)(2,1)S(1)}, s32[8,128]{1,0:T(8,128)S(1)}) %tuple.30, (bf16[288,16,128]{2,1,0:T(8,128)(2,1)S(1)}, s32[8,128]{1,0:T(8,128)S(1)}) %tuple.31), branch_computations={%region_0.0_spmd, %region_1.0_spmd} | conditional | bytes 3407880 | solution.py:418
  18.3 23.8 %all_to_all.50.recv = bf16[8,36,16,128]{3,2,1,0:T(8,128)(2,1)S(1)} all-to-all(bf16[8,36,16,128]{3,2,1,0:T(8,128)(2,1)S(1)} %bitcast.11), channel_id=1, replica_groups=mesh['y'=8,'zl'=4,'k'=2,'zh'=2,'x'=4] {'zh','zl'}, dimensions={0} | all-to-all | bytes 2359296 | tf_op jit(solution)/shard_map/cond/branch_1_fun/all_to_all | solution.py:394
  42.1 0.1 branch_1_fun.5
  42.3 22.5 %all_to_all.51.recv = bf16[32,64,128]{2,1,0:T(8,128)(2,1)S(1)} all-to-all(bf16[32,64,128]{2,1,0:T(8,128)(2,1)S(1)} %branch_1_fun.5), channel_id=1, replica_groups=mesh['y'=8,'zl'=4,'k'=2,'zh'=2,'x'=4] {'y','x'}, dimensions={0} | all-to-all | bytes 1048576 | tf_op jit(solution)/shard_map/cond/branch_1_fun/all_to_all | solution.py:394
  64.8 0.0 copy-done.2
  64.8 0.0 copy-done.3
  64.8 0.0 copy-done.4
  64.8 0.0 copy-done.7
  64.8 1.2 shard_map.139
  66.0 3.4 %all-to-all-start.8 = ((bf16[8,112,128]{2,1,0:T(8,128)(2,1)}), bf16[8,112,128]{2,1,0:T(8,128)(2,1)S(1)}, u32[]{:S(2)}, u32[]{:S(2)}) async-start(bf16[8,112,128]{2,1,0:T(8,128)(2,1)} %get-tuple-element.44), calls=%async_computation.8 | async-start | bytes 458752 | tf_op jit(solution)/shard_map/all_to_all | solution.py:394
  69.4 10.0 %all-to-all-done.8.recv = bf16[8,112,128]{2,1,0:T(8,128)(2,1)S(1)} async-done(((bf16[8,112,128]{2,1,0:T(8,128)(2,1)}), bf16[8,112,128]{2,1,0:T(8,128)(2,1)S(1)}, u32[]{:S(2)}, u32[]{:S(2)}) %all-to-all-start.8) | async-done | bytes 229408 | tf_op jit(solution)/shard_map/all_to_all | solution.py:394
  79.4 0.0 copy-start
  79.4 36.6 %conditional.3 = (bf16[296,16,128]{2,1,0:T(8,128)(2,1)}, bf16[16,64,128]{2,1,0:T(8,128)(2,1)}, bf16[16,128]{1,0:T(8,128)(2,1)S(1)}) conditional(s32[]{:T(128)} %convert_element_type.7, bf16[8,112,128]{2,1,0:T(8,128)(2,1)S(1)} %all-to-all-done.8.recv, bf16[8,112,128]{2,1,0:T(8,128)(2,1)S(1)} %all-to-all-done.8.recv), branch_computations={%region_2.0_spmd, %region_3.0_spmd} | conditional | bytes 3276824 | solution.py:447
  79.4 0.1 branch_0_fun.7
  79.5 13.9 %all_to_all.52.recv = bf16[8,13,16,128]{3,2,1,0:T(8,128)(2,1)S(1)} all-to-all(bf16[8,13,16,128]{3,2,1,0:T(8,128)(2,1)S(1)} %branch_0_fun.7), channel_id=1, replica_groups=mesh['y'=8,'zl'=4,'k'=2,'zh'=2,'x'=4] {'y'}, dimensions={0} | all-to-all | bytes 851968 | tf_op jit(solution)/shard_map/cond/branch_0_fun/all_to_all | solution.py:394
  93.3 0.1 branch_0_fun.8
  93.5 20.9 %all_to_all.53.recv_h = bf16[4,74,16,128]{3,2,1,0:T(8,128)(2,1)} all-to-all(bf16[4,74,16,128]{3,2,1,0:T(8,128)(2,1)S(1)} %branch_0_fun.8), channel_id=1, replica_groups=mesh['y'=8,'zl'=4,'k'=2,'zh'=2,'x'=4] {'zl'}, dimensions={0} | all-to-all | bytes 2424832 | tf_op jit(solution)/shard_map/cond/branch_0_fun/all_to_all | solution.py:394
  114.4 1.5 %branch_0_fun.9 = (bf16[16,64,128]{2,1,0:T(8,128)(2,1)}, bf16[16,128]{1,0:T(8,128)(2,1)S(1)}) custom-call(bf16[4,74,16,128]{3,2,1,0:T(8,128)(2,1)} %all_to_all.53.recv_h), custom_call_target="tpu_custom_call" | custom-call | tf_op jit(solution)/shard_map/cond/branch_0_fun/pallas_call | solution.py:437
  116.0 0.0 copy-start.6
  116.0 6.2 %all-to-all-start.9 = ((bf16[16,64,128]{2,1,0:T(8,128)(2,1)}), bf16[16,64,128]{2,1,0:T(8,128)(2,1)S(1)}, u32[]{:S(2)}, u32[]{:S(2)}) async-start(bf16[16,64,128]{2,1,0:T(8,128)(2,1)} %get-tuple-element.49), calls=%async_computation.9 | async-start | bytes 524288 | tf_op jit(solution)/shard_map/all_to_all | solution.py:394
  122.2 2.0 %shard_map.140 = (bf16[64,16,128]{2,1,0:T(8,128)(2,1)S(1)}, bf16[65,16,128]{2,1,0:T(8,128)(2,1)S(1)}) custom-call(s32[64]{0:T(128)S(1)} %copy-done.5, s32[1]{0:T(128)S(6)} %copy.23.count_h.count, s32[1,128]{1,0:T(1,128)S(1)} %get-tuple-element.43.dest_other, bf16[296,16,128]{2,1,0:T(8,128)(2,1)} %get-tuple-element.45.recv, ...), custom_call_target="tpu_custom_call" | custom-call | bytes 4320000 | tf_op jit(solution)/shard_map/pallas_call | solution.py:451
  124.2 2.1 %collective-permute-start.1 = (bf16[65,16,128]{2,1,0:T(8,128)(2,1)S(1)}, bf16[65,16,128]{2,1,0:T(8,128)(2,1)S(1)}, u32[]{:S(2)}, u32[]{:S(2)}) collective-permute-start(bf16[65,16,128]{2,1,0:T(8,128)(2,1)S(1)} %get-tuple-element.48), channel_id=1, source_target_pairs={{0,8},{8,0},{1,9},{9,1},{2,10},{10,2},{3,11},{11,3},{4,12},{12,4},... | collective-permute-start | bytes 798728 | tf_op jit(solution)/shard_map/ppermute | solution.py:457
  126.3 1.3 collective-permute-done.1.given
  127.7 0.0 copy-done
  127.7 0.0 copy-done.6
  127.7 2.2 %shard_map.141 = bf16[16,1024]{1,0:T(8,128)(2,1)} custom-call(s32[64]{0:T(128)S(1)} %copy-done.6, bf16[64,16,128]{2,1,0:T(8,128)(2,1)S(1)} %get-tuple-element.47.own, bf16[65,16,128]{2,1,0:T(8,128)(2,1)S(1)} %collective-permute-done.1.given, bf16[8,112,128]{2,1,0:T(8,128)(2,1)S(1)} %all-to-all-done.8.recv, bf16[64,128,128]{2,1,0:T(8,128)(2,1)S(1)} %copy-done), custom_call_target="tpu_custom_call" | custom-call | bytes 7920000 | tf_op jit(solution)/shard_map/pallas_call | solution.py:324
  129.9 4.2 %all-to-all-done.9.x = bf16[16,64,128]{2,1,0:T(8,128)(2,1)S(1)} async-done(((bf16[16,64,128]{2,1,0:T(8,128)(2,1)}), bf16[16,64,128]{2,1,0:T(8,128)(2,1)S(1)}, u32[]{:S(2)}, u32[]{:S(2)}) %all-to-all-start.9) | async-done | bytes 262176 | tf_op jit(solution)/shard_map/all_to_all | solution.py:394
  134.1 0.9 shard_map.142
  (1 shorter events, 0.0 us)
Async XLA Ops:
  0.6 14.3 %copy-start.8 = (bf16[16,1024]{1,0:T(8,128)(2,1)S(1)}, bf16[16,1024]{1,0:T(8,128)(2,1)}, u32[]{:S(2)}) copy-start(bf16[16,1024]{1,0:T(8,128)(2,1)} %feats.1) | copy-start | bytes 98308
  0.6 14.3 %copy-start.5 = (s32[64]{0:T(128)S(1)}, s32[64]{0:T(128)}, u32[]{:S(2)}) copy-start(s32[64]{0:T(128)} %dest_own.3) | copy-start | bytes 772
  1.3 17.0 %copy-start.9 = (s32[1024]{0:T(1024)S(1)}, s32[1024]{0:T(1024)}, u32[]{:S(2)}) copy-start(s32[1024]{0:T(1024)} %param.19) | copy-start | bytes 12292
  4.8 10.1 %collective-permute-start = (bf16[65,16,128]{2,1,0:T(8,128)(2,1)}, bf16[65,16,128]{2,1,0:T(8,128)(2,1)S(1)}, u32[]{:S(2)}, u32[]{:S(2)}) collective-permute-start(bf16[65,16,128]{2,1,0:T(8,128)(2,1)} %shard_map.137.own), channel_id=1, source_target_pairs={{0,8},{8,0},{1,9},{9,1},{2,10},{10,2},{3,11},{11,3},{4,12},{12,4},... | collective-permute-start | bytes 798728 | tf_op jit(solution)/shard_map/ppermute | solution.py:379
  14.9 1.0 copy-start.1
  18.3 46.5 %copy-start.2 = (bf16[128,256]{1,0:T(8,128)(2,1)S(1)}, bf16[128,256]{1,0:T(8,128)(2,1)}, u32[]{:S(2)}) copy-start(bf16[128,256]{1,0:T(8,128)(2,1)} %w_self.1) | copy-start | bytes 196612
  18.3 46.5 %copy-start.3 = (bf16[128,256]{1,0:T(8,128)(2,1)S(1)}, bf16[128,256]{1,0:T(8,128)(2,1)}, u32[]{:S(2)}) copy-start(bf16[128,256]{1,0:T(8,128)(2,1)} %w_neigh.1) | copy-start | bytes 196612
  18.3 46.5 %copy-start.4 = (bf16[256,128]{1,0:T(8,128)(2,1)S(1)}, bf16[256,128]{1,0:T(8,128)(2,1)}, u32[]{:S(2)}) copy-start(bf16[256,128]{1,0:T(8,128)(2,1)} %cot.1) | copy-start | bytes 196612
  18.3 46.5 %copy-start.7 = (f32[256]{0:T(256)S(1)}, f32[256]{0:T(256)}, u32[]{:S(2)}) copy-start(f32[256]{0:T(256)} %param.22) | copy-start | bytes 3076
  66.0 13.4 %all-to-all-start.8 = ((bf16[8,112,128]{2,1,0:T(8,128)(2,1)}), bf16[8,112,128]{2,1,0:T(8,128)(2,1)S(1)}, u32[]{:S(2)}, u32[]{:S(2)}) async-start(bf16[8,112,128]{2,1,0:T(8,128)(2,1)} %get-tuple-element.44), calls=%async_computation.8 | async-start | bytes 458752 | tf_op jit(solution)/shard_map/all_to_all | solution.py:394
  79.4 48.3 %copy-start = (bf16[64,128,128]{2,1,0:T(8,128)(2,1)S(1)}, bf16[64,128,128]{2,1,0:T(8,128)(2,1)}, u32[]{:S(2)}) copy-start(bf16[64,128,128]{2,1,0:T(8,128)(2,1)} %vals.1) | copy-start | bytes 6291460
  116.0 11.7 %copy-start.6 = (s32[64]{0:T(128)S(1)}, s32[64]{0:T(128)}, u32[]{:S(2)}) copy-start(s32[64]{0:T(128)} %src.1) | copy-start | bytes 772
  116.0 18.1 %all-to-all-start.9 = ((bf16[16,64,128]{2,1,0:T(8,128)(2,1)}), bf16[16,64,128]{2,1,0:T(8,128)(2,1)S(1)}, u32[]{:S(2)}, u32[]{:S(2)}) async-start(bf16[16,64,128]{2,1,0:T(8,128)(2,1)} %get-tuple-element.49), calls=%async_computation.9 | async-start | bytes 524288 | tf_op jit(solution)/shard_map/all_to_all | solution.py:394
  124.2 3.4 %collective-permute-start.1 = (bf16[65,16,128]{2,1,0:T(8,128)(2,1)S(1)}, bf16[65,16,128]{2,1,0:T(8,128)(2,1)S(1)}, u32[]{:S(2)}, u32[]{:S(2)}) collective-permute-start(bf16[65,16,128]{2,1,0:T(8,128)(2,1)S(1)} %get-tuple-element.48), channel_id=1, source_target_pairs={{0,8},{8,0},{1,9},{9,1},{2,10},{10,2},{3,11},{11,3},{4,12},{12,4},... | collective-permute-start | bytes 798728 | tf_op jit(solution)/shard_map/ppermute | solution.py:457

commit v5 on v4

--- a/solution.py
+++ b/solution.py
@@ -196,7 +196,7 @@
         out[c, F_LOC : 2 * F_LOC] = recv[here + n, rows]
 
 
-def dense_layer_kernel(recv, w_self, w_neigh, bias, cot, degree, hidden, out):
+def dense_layer_kernel(recv, w_self, w_neigh, bias, cot, degree, hidden, out, dx_out):
     agg = recv[:, 0:F_LOC].reshape(RB * F_LOC, TB)
     feats = recv[:, F_LOC : 2 * F_LOC].reshape(RB * F_LOC, TB)
     ws = w_self[...]
@@ -223,13 +223,16 @@
     tail = jnp.concatenate([high, two - high, jnp.zeros((12, TB), F32)], axis=0).astype(BF)
     for c in range(RB):
         rows = slice(c * F_LOC, (c + 1) * F_LOC)
-        out[c, 0:16] = dsum[rows]
-        out[c, 16:32] = dx_self[rows]
-        out[c, 32:48] = part_self[rows, 0:TB].astype(BF)
-        out[c, 48:64] = part_self[rows, TB:].astype(BF)
-        out[c, 64:80] = part_neigh[rows, 0:TB].astype(BF)
-        out[c, 80:96] = part_neigh[rows, TB:].astype(BF)
-        out[c, 96:112] = tail
+        h, x = c // NX, c % NX
+        dx_out[c] = dx_self[rows]
+        out[x, h] = dsum[rows]
+        first = 2 + 4 * h
+        out[x, first] = part_self[rows, 0:TB].astype(BF)
+        out[x, first + 1] = part_self[rows, TB:].astype(BF)
+        out[x, first + 2] = part_neigh[rows, 0:TB].astype(BF)
+        out[x, first + 3] = part_neigh[rows, TB:].astype(BF)
+    for x in range(NX):
+        out[x, 10] = tail
 
 
 def parted(tail):
@@ -238,29 +241,56 @@
     return jnp.concatenate([high, two - high, jnp.zeros((12, TB), F32)], axis=0).astype(BF)
 
 
-def first_step_kernel(recv, out):
-    blocks = recv[:, 0:F_LOC]
-    sums = jnp.sum(recv[:, 32:96].astype(F32), axis=0).astype(BF)
-    tail = parted(jnp.sum(recv[:, 96:112].astype(F32), axis=0))
-    for p in range(out.shape[0]):
-        out[p, 0:RB] = blocks
-        for n in range(4):
-            out[p, RB + n] = sums[n * F_LOC : (n + 1) * F_LOC]
-        out[p, RB + 4] = tail
-
-
-def second_step_kernel(recv, out):
-    came = recv.shape[0]
-    sums = [jnp.sum(recv[:, RB + n].astype(F32), axis=0) for n in range(EXTRA)]
-    sums = [x.astype(BF) for x in sums[:4]] + [parted(sums[4])]
-    for p in range(out.shape[0]):
-        for q in range(came):
-            out[p, q * RB : (q + 1) * RB] = recv[q, 0:RB]
-        for n in range(EXTRA):
-            out[p, came * RB + n] = sums[n]
-
-
-def share_kernel(first, recv_h, out, bias_out, recv, sems):
+def added(recv, n):
+    total = recv[0, n].astype(F32)
+    for p in range(1, recv.shape[0]):
+        total = total + recv[p, n].astype(F32)
+    return total
+
+
+def first_step_kernel(z_first, recv, out):
+    places = out.shape[0]
+    bias = parted(added(recv, 10))
+    for h in range(2):
+        sums = [added(recv, 2 + 4 * h + n).astype(BF) for n in range(4)]
+        at = 0 if z_first else NX * h
+        sums_at = NX if z_first else 2 * NX + 4 * h
+        for p in range(places):
+            if z_first and p // (places // 2) != h:
+                continue
+            for x in range(NX):
+                out[p, at + x] = recv[x, h]
+            for n in range(4):
+                out[p, sums_at + n] = sums[n]
+    for p in range(places):
+        out[p, out.shape[1] - 1] = bias
+
+
+def second_step_kernel(z_first, recv, out):
+    came, places = recv.shape[0], out.shape[0]
+    bias = parted(added(recv, recv.shape[1] - 1))
+    if z_first:
+        nz = came // 2
+        sums = [added(recv, NX + n).astype(BF) for n in range(4)]
+        for p in range(places):
+            for q in range(came):
+                at = (q % nz) * RB + (q // nz) * NX
+                out[p, at : at + NX] = recv[q, 0:NX]
+            for n in range(4):
+                out[p, nz * RB + n] = sums[n]
+            out[p, nz * RB + 4] = bias
+    else:
+        for h in range(2):
+            sums = [added(recv, 2 * NX + 4 * h + n).astype(BF) for n in range(4)]
+            for p in range(places // 2 * h, places // 2 * (h + 1)):
+                for q in range(came):
+                    out[p, q * NX : (q + 1) * NX] = recv[q, h * NX : (h + 1) * NX]
+                for n in range(4):
+                    out[p, came * NX + n] = sums[n]
+                out[p, came * NX + 4] = bias
+
+
+def share_kernel(first, recv_h, dx, out, bias_out, recv, sems):
     copies = [
         pltpu.make_async_copy(recv_h.at[p, pl.ds(first, EXTRA)], recv.at[p], sems.at[p])
         for p in range(recv.shape[0])
@@ -274,19 +304,22 @@
     for p in range(out.shape[0]):
         for n in range(4):
             out[p, n * F_LOC : (n + 1) * F_LOC] = rows[n]
+        out[p, 4 * F_LOC : 5 * F_LOC] = dx[p % RB]
     bias_out[...] = parted(sums[4])
 
 
-def pick_kernel(ny, nz, dest_own, count, dest_other, recv, bias_sum, own, other):
+def pick_kernel(nz, size_0, size_1, dest_own, count, dest_other, recv, bias_sum, own, other):
     k = lax.axis_index("k")
-    of_y = jnp.where(k == 0, nz * RB + EXTRA, RB)
-    of_z = jnp.where(k == 0, RB, ny * (nz * RB + EXTRA) // nz)
+    of_y = jnp.where(k == 0, size_0, NX)
+    of_zl = jnp.where(k == 0, RB, size_1)
+    of_zh = jnp.where(k == 0, NX, nz * size_1)
     bits = nz.bit_length() - 1
 
     def pick(d, used):
         mine = jnp.logical_and(used, ((d >> 3) & 1) == k)
         d = jnp.where(mine, d, 0)
-        at = (d >> (4 + bits)) * of_y + ((d >> 4) & (nz - 1)) * of_z + (d & 7)
+        at = (d >> (4 + bits)) * of_y + ((d >> 4) & (nz - 1)) * of_zl
+        at = at + ((d >> 2) & 1) * of_zh + (d & (NX - 1))
         tile = recv[at]
         return jnp.where(mine, tile, jnp.zeros_like(tile))
 
@@ -300,48 +333,35 @@
     other[TILES_DEV] = bias_sum[...]
 
 
-def back_kernel(src, own, given, recv, vals, out, acc):
-    g = pl.program_id(0)
-
-    @pl.when(g == 0)
+def back_kernel(src, own, given, vals, acc):
+    @pl.when(pl.program_id(0) == 0)
     def _():
-        acc[...] = recv[:, F_LOC : 2 * F_LOC].astype(F32)
-
-    first = g * STEP
+        acc[...] = jnp.zeros_like(acc)
+
+    first = pl.program_id(0) * STEP
     for t in range(STEP):
         grad = own[t] + given[t]
         at = src[first + t]
         acc[at] = acc[at] + jnp.dot(grad, vals[t], preferred_element_type=F32)
 
-    @pl.when(g == pl.num_programs(0) - 1)
-    def _():
-        for b in range(RB):
-            out[:, b * TB : (b + 1) * TB] = acc[b].astype(BF)
-
-
-def tile_back(src, own, given, recv, vals):
+
+def tile_back(src, own, given, vals):
     tiles = pl.BlockSpec((STEP, F_LOC, TB), lambda g, s: (g, 0, 0))
     return pl.pallas_call(
         back_kernel,
-        out_shape=sds((F_LOC, RB * TB), BF),
+        out_shape=sds((RB, F_LOC, TB), F32),
         grid_spec=pltpu.PrefetchScalarGridSpec(
             num_scalar_prefetch=1,
             grid=(TILES_DEV // STEP,),
-            in_specs=[
-                tiles,
-                tiles,
-                pl.BlockSpec(recv.shape, lambda g, s: (0, 0, 0)),
-                pl.BlockSpec((STEP, TB, TB), lambda g, s: (g, 0, 0)),
-            ],
-            out_specs=pl.BlockSpec((F_LOC, RB * TB), lambda g, s: (0, 0)),
-            scratch_shapes=[pltpu.VMEM((RB, F_LOC, TB), F32)],
+            in_specs=[tiles, tiles, pl.BlockSpec((STEP, TB, TB), lambda g, s: (g, 0, 0))],
+            out_specs=pl.BlockSpec((RB, F_LOC, TB), lambda g, s: (0, 0, 0)),
         ),
         compiler_params=PARAMS,
         cost_estimate=lasting(2.2),
-    )(src, own, given, recv, vals)
-
-
-def normal_kernel(x, bias_sum, given, grad_self, grad_neigh, grad_bias):
+    )(src, own, given, vals)
+
+
+def last_kernel(x, bias_sum, given, dx_neigh, grad_x, grad_self, grad_neigh, grad_bias):
     for first, out in ((0, grad_self), (32, grad_neigh)):
         rows = slice(first, first + 32)
         part = x[0:RB, rows].astype(F32) + x[RB : 2 * RB, rows].astype(F32)
@@ -355,6 +375,10 @@
     theirs = given[TILES_DEV].astype(F32)
     two = (mine[0:2] + mine[2:4]) + (theirs[0:2] + theirs[2:4])
     grad_bias[...] = two / jnp.sqrt(jnp.mean(two * two) + EPS)
+    here = lax.axis_index("k") * RB
+    for b in range(RB):
+        dx_self = x[here + b, 4 * F_LOC : 5 * F_LOC].astype(F32)
+        grad_x[:, b * TB : (b + 1) * TB] = (dx_self + dx_neigh[b]).astype(BF)
 
 
 def local(
@@ -418,49 +442,71 @@
     full = lax.cond(
         lax.axis_index("k") == 1, z_collect, y_collect, dense, features, degree2
     )
-    hidden, back = whole(
+    hidden, back, dx_self = whole(
         dense_layer_kernel,
-        (sds(cotangent.shape, BF), sds((RB, 112, TB), BF)),
+        (
+            sds(cotangent.shape, BF),
+            sds((NX, 11, F_LOC, TB), BF),
+            sds((RB, F_LOC, TB), BF),
+        ),
         [VMEM] * 6,
     )(full, w_self, w_neigh, bias.reshape(1, -1), cotangent, degree2)
-    back = exchange(back, COL)
-
-    tiles = ny * (nz * RB + EXTRA)
-
-    def in_two_steps(first, second):
-        def run(back):
-            n1, n2 = lax.axis_size(first), lax.axis_size(second)
-            one = whole(first_step_kernel, sds((n1, RB + EXTRA, F_LOC, TB), BF), [VMEM])(back)
+    back = exchange(back, "x")
+
+    tiles = max(ny * (nz * RB + EXTRA), 2 * nz * (ny * NX + EXTRA))
+
+    def in_two_steps(z_first):
+        zs = ("zh", "zl")
+        first, second = (zs, "y") if z_first else ("y", zs)
+        n1, n2 = lax.axis_size(first), lax.axis_size(second)
+        width = NX + EXTRA if z_first else 2 * NX + 4 + EXTRA
+        sums_at = nz * RB if z_first else ny * NX
+
+        def run(back, dx_self):
+            one = whole(
+                functools.partial(first_step_kernel, z_first),
+                sds((n1, width, F_LOC, TB), BF),
+                [VMEM],
+            )(back)
             one = exchange(one, first)
-            two = whole(second_step_kernel, sds((n2, tiles // n2, F_LOC, TB), BF), [VMEM])(one)
+            two = whole(
+                functools.partial(second_step_kernel, z_first),
+                sds((n2, tiles // n2, F_LOC, TB), BF),
+                [VMEM],
+            )(one)
             two = exchange(two, second)
             share, bias_sum = whole(
-                functools.partial(share_kernel, n1 * RB),
-                (sds((2 * RB, 64, TB), BF), sds((F_LOC, TB), BF)),
-                [ANY],
+                functools.partial(share_kernel, sums_at),
+                (sds((2 * RB, 5 * F_LOC, TB), BF), sds((F_LOC, TB), BF)),
+                [ANY, VMEM],
                 [pltpu.VMEM((n2, EXTRA, F_LOC, TB), BF), pltpu.SemaphoreType.DMA((n2,))],
-            )(two)
+            )(two, dx_self)
             return two.reshape(tiles, F_LOC, TB), share, bias_sum
 
         return run
 
     portion, share, bias_sum = lax.cond(
-        lax.axis_index("k") == 0, in_two_steps("zl", "y"), in_two_steps("y", "zl"), back
+        lax.axis_index("k") == 0, in_two_steps(True), in_two_steps(False), back, dx_self
     )
     chunks = exchange(share, ("k",) + COL)
     own, other = whole(
-        functools.partial(pick_kernel, ny, nz),
+        functools.partial(pick_kernel, nz, tiles // ny, tiles // (2 * nz)),
         (sds((TILES_DEV, F_LOC, TB), BF), sds((TILES_DEV + 1, F_LOC, TB), BF)),
         [SMEM, SMEM, SMEM, VMEM, VMEM],
-        cost=lasting(1.2),
+        cost=lasting(2.0),
     )(tile_dest, tile_count, dest_other, portion, bias_sum)
     given = lax.ppermute(other, "k", swap)
-    grad_x = tile_back(tile_source, own, given, back, tile_values)
-    grad_self, grad_neigh, grad_bias = whole(
-        normal_kernel,
-        (sds(w_self.shape, F32), sds(w_self.shape, F32), sds((2, TB), F32)),
-        [VMEM] * 3,
-    )(chunks, bias_sum, given)
+    dx_neigh = tile_back(tile_source, own, given, tile_values)
+    grad_x, grad_self, grad_neigh, grad_bias = whole(
+        last_kernel,
+        (
+            sds(features.shape, BF),
+            sds(w_self.shape, F32),
+            sds(w_self.shape, F32),
+            sds((2, TB), F32),
+        ),
+        [VMEM] * 4,
+    )(chunks, bias_sum, given, dx_neigh)
     return hidden, grad_x, grad_self, grad_neigh, grad_bias.reshape(-1)
 
 

time: 136 us -> 134 us (0.985)
  blocking collectives: 81 us -> 84.8 us
  waiting for transfers between devices: 16.8 us -> 13.1 us
  starting transfers between devices: 20.5 us -> 18.1 us
    all_to_all x4, blocking collectives: 81 us -> 84.8 us  [exchange(): return lax.all_to_all(array, axes, split_axis=0, concat_axis=0, tiled=True)]
    all_to_all x2, waiting for transfers between devices: 14.2 us -> 10.4 us  [exchange(): return lax.all_to_all(array, axes, split_axis=0, concat_axis=0, tiled=True)]
    all_to_all x2, starting transfers between devices: 9.64 us -> 7.18 us  [exchange(): return lax.all_to_all(array, axes, split_axis=0, concat_axis=0, tiled=True)]
where the time goes in v5:
time: 134 us; the launch traced here: 132 us
  blocking collectives  84.8 us (63%)
  starting transfers between devices  18.1 us (14%)
  Pallas kernels  13.7 us (10%)
  waiting for transfers between devices  13.1 us (10%)
  between operations  1.48 us (1%)
    all_to_all x4, blocking collectives, exchange(): return lax.all_to_all(array, axes, split_axis=0, concat_axis=0, tiled=True)  84.8 us
    all_to_all x2, waiting for transfers between devices, exchange(): return lax.all_to_all(array, axes, split_axis=0, concat_axis=0, tiled=True)  10.4 us
    ppermute x1, starting transfers between devices, local(): terms_other = lax.ppermute(terms, 'k', swap)  8.79 us
    all_to_all x2, starting transfers between devices, exchange(): return lax.all_to_all(array, axes, split_axis=0, concat_axis=0, tiled=True)  7.18 us
    pallas_call x1, Pallas kernels, tile_terms(): pl.pallas_call(terms_kernel, out_shape=sds((TILES_DEV + 1, F_LOC, TB), BF...  3.42 us
  transfers between devices with their start and end apart: 4, of which 4 were waited for; matrix products, arithmetic and copies ran while one was open for 0% of the time, Pallas kernels for 3%

profile of v5, /device:TPU:1, one launch (start us, length us, event | category | flops | bytes accessed | tf_op | source)
XLA Modules:
  0.0 132.2 jit_solution(7495794681690853107)
XLA Ops:
  0.6 0.0 copy-start.8
  0.6 0.0 copy-start.5
  1.3 0.0 copy-start.9
  1.3 3.4 %shard_map.137.own = bf16[65,16,128]{2,1,0:T(8,128)(2,1)} custom-call(s32[64]{0:T(128)} %src.1, s32[1,64]{1,0:T(1,128)} %bitcast.8, s32[1]{0:T(128)S(6)} %copy.23.count_h.count, bf16[16,1024]{1,0:T(8,128)(2,1)} %feats.1, bf16[64,128,128]{2,1,0:T(8,128)(2,1)} %vals.1), custom_call_target="tpu_custom_call" | custom-call | tf_op jit(solution)/shard_map/pallas_call | solution.py:95
  4.8 8.8 %collective-permute-start = (bf16[65,16,128]{2,1,0:T(8,128)(2,1)}, bf16[65,16,128]{2,1,0:T(8,128)(2,1)S(1)}, u32[]{:S(2)}, u32[]{:S(2)}) collective-permute-start(bf16[65,16,128]{2,1,0:T(8,128)(2,1)} %shard_map.137.own), channel_id=1, source_target_pairs={{0,8},{8,0},{1,9},{9,1},{2,10},{10,2},{3,11},{11,3},{4,12},{12,4},... | collective-permute-start | bytes 798728 | tf_op jit(solution)/shard_map/ppermute | solution.py:403
  13.6 1.4 %collective-permute-done.other = bf16[65,16,128]{2,1,0:T(8,128)(2,1)S(1)} collective-permute-done((bf16[65,16,128]{2,1,0:T(8,128)(2,1)}, bf16[65,16,128]{2,1,0:T(8,128)(2,1)S(1)}, u32[]{:S(2)}, u32[]{:S(2)}) %collective-permute-start) | collective-permute-done | bytes 266272 | tf_op jit(solution)/shard_map/ppermute | solution.py:403
  14.9 0.0 copy-done.8
  14.9 0.0 copy-done.5
  14.9 0.0 copy-start.1
  14.9 1.0 copy-done.1
  15.9 2.4 %shard_map.138 = (bf16[288,16,128]{2,1,0:T(8,128)(2,1)S(1)}, s32[1,128]{1,0:T(1,128)S(1)}) custom-call(s32[64]{0:T(128)S(1)} %copy-done.5, s32[1]{0:T(128)S(6)} %copy.23.count_h.count, bf16[65,16,128]{2,1,0:T(8,128)(2,1)S(1)} %copy-done.1, bf16[65,16,128]{2,1,0:T(8,128)(2,1)S(1)} %collective-permute-done.other, bf16[16,1024]{1,0:T(8,128)(2,1)S(1)} %copy-done.8), custom_call_target="tpu_custom_call" | custom-call | tf_op jit(solution)/shard_map/pallas_call | solution.py:405
  18.3 0.0 copy-done.9
  18.3 0.0 copy-start.2
  18.3 0.0 copy-start.3
  18.3 0.0 copy-start.4
  18.3 0.0 copy-start.7
  18.3 46.4 %conditional.2 = (bf16[8,32,128]{2,1,0:T(8,128)(2,1)S(1)}) conditional(s32[]{:T(128)} %convert_element_type.6, (bf16[288,16,128]{2,1,0:T(8,128)(2,1)S(1)}, bf16[16,1024]{1,0:T(8,128)(2,1)S(1)}, s32[8,128]{1,0:T(8,128)S(1)}) %tuple.31, (bf16[288,16,128]{2,1,0:T(8,128)(2,1)S(1)}, s32[8,128]{1,0:T(8,128)S(1)}) %tuple.32), branch_computations={%region_0.0_spmd, %region_1.0_spmd} | conditional | bytes 3407880 | solution.py:442
  18.4 23.7 %all_to_all.44.recv = bf16[8,36,16,128]{3,2,1,0:T(8,128)(2,1)S(1)} all-to-all(bf16[8,36,16,128]{3,2,1,0:T(8,128)(2,1)S(1)} %bitcast.11), channel_id=1, replica_groups=mesh['y'=8,'zl'=4,'k'=2,'zh'=2,'x'=4] {'zh','zl'}, dimensions={0} | all-to-all | bytes 2359296 | tf_op jit(solution)/shard_map/cond/branch_1_fun/all_to_all | solution.py:418
  42.1 0.1 branch_1_fun.5
  42.2 22.5 %all_to_all.45.recv = bf16[32,64,128]{2,1,0:T(8,128)(2,1)S(1)} all-to-all(bf16[32,64,128]{2,1,0:T(8,128)(2,1)S(1)} %branch_1_fun.5), channel_id=1, replica_groups=mesh['y'=8,'zl'=4,'k'=2,'zh'=2,'x'=4] {'y','x'}, dimensions={0} | all-to-all | bytes 1048576 | tf_op jit(solution)/shard_map/cond/branch_1_fun/all_to_all | solution.py:418
  64.8 0.0 copy-done.2
  64.8 0.0 copy-done.3
  64.8 0.0 copy-done.4
  64.8 0.0 copy-done.7
  64.8 1.2 shard_map.139
  66.0 3.4 %all-to-all-start.8 = ((bf16[4,11,16,128]{3,2,1,0:T(8,128)(2,1)}), bf16[4,11,16,128]{3,2,1,0:T(8,128)(2,1)S(1)}, u32[]{:S(2)}, u32[]{:S(2)}) async-start(bf16[4,11,16,128]{3,2,1,0:T(8,128)(2,1)} %get-tuple-element.55), calls=%async_computation.8 | async-start | bytes 360448 | tf_op jit(solution)/shard_map/all_to_all | solution.py:418
  69.4 5.0 %all-to-all-done.8 = bf16[4,11,16,128]{3,2,1,0:T(8,128)(2,1)S(1)} async-done(((bf16[4,11,16,128]{3,2,1,0:T(8,128)(2,1)}), bf16[4,11,16,128]{3,2,1,0:T(8,128)(2,1)S(1)}, u32[]{:S(2)}, u32[]{:S(2)}) %all-to-all-start.8) | async-done | bytes 180256 | tf_op jit(solution)/shard_map/all_to_all | solution.py:418
  74.4 0.0 copy-start
  74.4 40.5 %conditional.3 = (bf16[296,16,128]{2,1,0:T(8,128)(2,1)}, bf16[16,80,128]{2,1,0:T(8,128)(2,1)}, bf16[16,128]{1,0:T(8,128)(2,1)S(1)}) conditional(s32[]{:T(128)} %convert_element_type.7, (bf16[4,11,16,128]{3,2,1,0:T(8,128)(2,1)S(1)}, bf16[8,16,128]{2,1,0:T(8,128)(2,1)S(1)}) %tuple.24, (bf16[4,11,16,128]{3,2,1,0:T(8,128)(2,1)S(1)}, ...), branch_computations={%region_2.0_spmd, %region_3.0_spmd} | conditional | bytes 3538968 | solution.py:488
  74.4 0.1 branch_0_fun.7
  74.5 15.7 %all_to_all.46.recv = bf16[8,17,16,128]{3,2,1,0:T(8,128)(2,1)S(1)} all-to-all(bf16[8,17,16,128]{3,2,1,0:T(8,128)(2,1)S(1)} %branch_0_fun.7), channel_id=1, replica_groups=mesh['y'=8,'zl'=4,'k'=2,'zh'=2,'x'=4] {'y'}, dimensions={0} | all-to-all | bytes 1114112 | tf_op jit(solution)/shard_map/cond/branch_0_fun/all_to_all | solution.py:418
  90.2 0.1 branch_0_fun.8
  90.3 22.9 %all_to_all.47.recv_h = bf16[8,37,16,128]{3,2,1,0:T(8,128)(2,1)} all-to-all(bf16[8,37,16,128]{3,2,1,0:T(8,128)(2,1)S(1)} %branch_0_fun.8), channel_id=1, replica_groups=mesh['y'=8,'zl'=4,'k'=2,'zh'=2,'x'=4] {'zh','zl'}, dimensions={0} | all-to-all | bytes 2424832 | tf_op jit(solution)/shard_map/cond/branch_0_fun/all_to_all | solution.py:418
  113.2 1.7 %branch_0_fun.9 = (bf16[16,80,128]{2,1,0:T(8,128)(2,1)}, bf16[16,128]{1,0:T(8,128)(2,1)S(1)}) custom-call(bf16[8,37,16,128]{3,2,1,0:T(8,128)(2,1)} %all_to_all.47.recv_h, bf16[8,16,128]{2,1,0:T(8,128)(2,1)S(1)} %get-tuple-element.27.dx), custom_call_target="tpu_custom_call" | custom-call | tf_op jit(solution)/shard_map/cond/branch_0_fun/pallas_call | solution.py:478
  114.9 0.0 copy-start.6
  114.9 3.8 %all-to-all-start.9 = ((bf16[16,80,128]{2,1,0:T(8,128)(2,1)}), bf16[16,80,128]{2,1,0:T(8,128)(2,1)S(1)}, u32[]{:S(2)}, u32[]{:S(2)}) async-start(bf16[16,80,128]{2,1,0:T(8,128)(2,1)} %get-tuple-element.57), calls=%async_computation.9 | async-start | bytes 655360 | tf_op jit(solution)/shard_map/all_to_all | solution.py:418
  118.8 2.1 %shard_map.140 = (bf16[64,16,128]{2,1,0:T(8,128)(2,1)S(1)}, bf16[65,16,128]{2,1,0:T(8,128)(2,1)S(1)}) custom-call(s32[64]{0:T(128)S(1)} %copy-done.5, s32[1]{0:T(128)S(6)} %copy.23.count_h.count, s32[1,128]{1,0:T(1,128)S(1)} %get-tuple-element.59.dest_other, bf16[296,16,128]{2,1,0:T(8,128)(2,1)} %get-tuple-element.60.recv, ...), custom_call_target="tpu_custom_call" | custom-call | bytes 7200000 | tf_op jit(solution)/shard_map/pallas_call | solution.py:492
  120.9 2.1 %collective-permute-start.1 = (bf16[65,16,128]{2,1,0:T(8,128)(2,1)S(1)}, bf16[65,16,128]{2,1,0:T(8,128)(2,1)S(1)}, u32[]{:S(2)}, u32[]{:S(2)}) collective-permute-start(bf16[65,16,128]{2,1,0:T(8,128)(2,1)S(1)} %get-tuple-element.61), channel_id=1, source_target_pairs={{0,8},{8,0},{1,9},{9,1},{2,10},{10,2},{3,11},{11,3},{4,12},{12,4},... | collective-permute-start | bytes 798728 | tf_op jit(solution)/shard_map/ppermute | solution.py:498
  123.0 1.3 %collective-permute-done.1.given = bf16[65,16,128]{2,1,0:T(8,128)(2,1)S(1)} collective-permute-done((bf16[65,16,128]{2,1,0:T(8,128)(2,1)S(1)}, bf16[65,16,128]{2,1,0:T(8,128)(2,1)S(1)}, u32[]{:S(2)}, u32[]{:S(2)}) %collective-permute-start.1) | collective-permute-done | bytes 266272 | tf_op jit(solution)/shard_map/ppermute | solution.py:498
  124.3 0.0 copy-done
  124.3 0.0 copy-done.6
  124.3 1.6 %shard_map.141.dx_neigh = f32[8,16,128]{2,1,0:T(8,128)S(1)} custom-call(s32[64]{0:T(128)S(1)} %copy-done.6, bf16[64,16,128]{2,1,0:T(8,128)(2,1)S(1)} %get-tuple-element.62.own, bf16[65,16,128]{2,1,0:T(8,128)(2,1)S(1)} %collective-permute-done.1.given, bf16[64,128,128]{2,1,0:T(8,128)(2,1)S(1)} %copy-done), custom_call_target="tpu_custom_call" | custom-call | bytes 7920000 | tf_op jit(solution)/shard_map/pallas_call | solution.py:350
  125.9 5.4 %all-to-all-done.9.x = bf16[16,80,128]{2,1,0:T(8,128)(2,1)S(1)} async-done(((bf16[16,80,128]{2,1,0:T(8,128)(2,1)}), bf16[16,80,128]{2,1,0:T(8,128)(2,1)S(1)}, u32[]{:S(2)}, u32[]{:S(2)}) %all-to-all-start.9) | async-done | bytes 327712 | tf_op jit(solution)/shard_map/all_to_all | solution.py:418
  131.3 0.9 shard_map.142
  (1 shorter events, 0.0 us)
Async XLA Ops:
  0.6 14.3 %copy-start.8 = (bf16[16,1024]{1,0:T(8,128)(2,1)S(1)}, bf16[16,1024]{1,0:T(8,128)(2,1)}, u32[]{:S(2)}) copy-start(bf16[16,1024]{1,0:T(8,128)(2,1)} %feats.1) | copy-start | bytes 98308
  0.6 14.3 %copy-start.5 = (s32[64]{0:T(128)S(1)}, s32[64]{0:T(128)}, u32[]{:S(2)}) copy-start(s32[64]{0:T(128)} %dest_own.3) | copy-start | bytes 772
  1.3 17.0 %copy-start.9 = (s32[1024]{0:T(1024)S(1)}, s32[1024]{0:T(1024)}, u32[]{:S(2)}) copy-start(s32[1024]{0:T(1024)} %param.19) | copy-start | bytes 12292
  4.8 10.2 %collective-permute-start = (bf16[65,16,128]{2,1,0:T(8,128)(2,1)}, bf16[65,16,128]{2,1,0:T(8,128)(2,1)S(1)}, u32[]{:S(2)}, u32[]{:S(2)}) collective-permute-start(bf16[65,16,128]{2,1,0:T(8,128)(2,1)} %shard_map.137.own), channel_id=1, source_target_pairs={{0,8},{8,0},{1,9},{9,1},{2,10},{10,2},{3,11},{11,3},{4,12},{12,4},... | collective-permute-start | bytes 798728 | tf_op jit(solution)/shard_map/ppermute | solution.py:403
  14.9 1.0 copy-start.1
  18.3 46.5 %copy-start.2 = (bf16[128,256]{1,0:T(8,128)(2,1)S(1)}, bf16[128,256]{1,0:T(8,128)(2,1)}, u32[]{:S(2)}) copy-start(bf16[128,256]{1,0:T(8,128)(2,1)} %w_self.1) | copy-start | bytes 196612
  18.3 46.5 %copy-start.3 = (bf16[128,256]{1,0:T(8,128)(2,1)S(1)}, bf16[128,256]{1,0:T(8,128)(2,1)}, u32[]{:S(2)}) copy-start(bf16[128,256]{1,0:T(8,128)(2,1)} %w_neigh.1) | copy-start | bytes 196612
  18.3 46.5 %copy-start.4 = (bf16[256,128]{1,0:T(8,128)(2,1)S(1)}, bf16[256,128]{1,0:T(8,128)(2,1)}, u32[]{:S(2)}) copy-start(bf16[256,128]{1,0:T(8,128)(2,1)} %cot.1) | copy-start | bytes 196612
  18.3 46.5 %copy-start.7 = (f32[256]{0:T(256)S(1)}, f32[256]{0:T(256)}, u32[]{:S(2)}) copy-start(f32[256]{0:T(256)} %param.22) | copy-start | bytes 3076
  66.0 8.4 %all-to-all-start.8 = ((bf16[4,11,16,128]{3,2,1,0:T(8,128)(2,1)}), bf16[4,11,16,128]{3,2,1,0:T(8,128)(2,1)S(1)}, u32[]{:S(2)}, u32[]{:S(2)}) async-start(bf16[4,11,16,128]{3,2,1,0:T(8,128)(2,1)} %get-tuple-element.55), calls=%async_computation.8 | async-start | bytes 360448 | tf_op jit(solution)/shard_map/all_to_all | solution.py:418
  74.4 49.9 %copy-start = (bf16[64,128,128]{2,1,0:T(8,128)(2,1)S(1)}, bf16[64,128,128]{2,1,0:T(8,128)(2,1)}, u32[]{:S(2)}) copy-start(bf16[64,128,128]{2,1,0:T(8,128)(2,1)} %vals.1) | copy-start | bytes 6291460
  114.9 9.4 %copy-start.6 = (s32[64]{0:T(128)S(1)}, s32[64]{0:T(128)}, u32[]{:S(2)}) copy-start(s32[64]{0:T(128)} %src.1) | copy-start | bytes 772
  114.9 16.4 %all-to-all-start.9 = ((bf16[16,80,128]{2,1,0:T(8,128)(2,1)}), bf16[16,80,128]{2,1,0:T(8,128)(2,1)S(1)}, u32[]{:S(2)}, u32[]{:S(2)}) async-start(bf16[16,80,128]{2,1,0:T(8,128)(2,1)} %get-tuple-element.57), calls=%async_computation.9 | async-start | bytes 655360 | tf_op jit(solution)/shard_map/all_to_all | solution.py:418
  120.9 3.4 %collective-permute-start.1 = (bf16[65,16,128]{2,1,0:T(8,128)(2,1)S(1)}, bf16[65,16,128]{2,1,0:T(8,128)(2,1)S(1)}, u32[]{:S(2)}, u32[]{:S(2)}) collective-permute-start(bf16[65,16,128]{2,1,0:T(8,128)(2,1)S(1)} %get-tuple-element.61), channel_id=1, source_target_pairs={{0,8},{8,0},{1,9},{9,1},{2,10},{10,2},{3,11},{11,3},{4,12},{12,4},... | collective-permute-start | bytes 798728 | tf_op jit(solution)/shard_map/ppermute | solution.py:498

commit v6 on v5

--- a/solution.py
+++ b/solution.py
@@ -28,7 +28,6 @@
 VMEM = pl.BlockSpec(memory_space=pltpu.VMEM)
 SMEM = pl.BlockSpec(memory_space=pltpu.SMEM)
 HBM = pl.BlockSpec(memory_space=pltpu.HBM)
-ANY = pl.BlockSpec(memory_space=pl.ANY)
 PARAMS = pltpu.CompilerParams(vmem_limit_bytes=32 * 1024 * 1024)
 FULL_PARAMS = pltpu.CompilerParams(vmem_limit_bytes=59 * 1024 * 1024)
 
@@ -82,13 +81,26 @@
     out[TILES_DEV] = coded.astype(F32).astype(BF)
     for g in range(parts):
         large[g].wait()
-        for t in range(g * STEP, (g + 1) * STEP):
-            start = pl.multiple_of(src[t] * TB, TB)
-            block = feats[:, pl.ds(start, TB)]
+        for t in range(g * STEP, (g + 1) * STEP, 2):
+            one, two = (
+                feats[:, pl.ds(pl.multiple_of(src[n] * TB, TB), TB)] for n in (t, t + 1)
+            )
+            zero = jnp.zeros_like(one)
+            pair = jnp.concatenate(
+                [
+                    jnp.concatenate([one, zero], axis=1),
+                    jnp.concatenate([zero, two], axis=1),
+                ],
+                axis=0,
+            )
             term = lax.dot_general(
-                block, vals[t], (((1,), (1,)), ((), ())), preferred_element_type=F32
-            )
-            out[t] = term.astype(BF)
+                pair,
+                jnp.concatenate([vals[t], vals[t + 1]], axis=1),
+                (((1,), (1,)), ((), ())),
+                preferred_element_type=F32,
+            ).astype(BF)
+            out[t] = term[0:F_LOC]
+            out[t + 1] = term[F_LOC:]
 
 
 def tile_terms(src, dest, count, feats, vals):
@@ -110,48 +122,56 @@
     )(src, dest, count, feats, vals)
 
 
-def dense_kernel(ny, nz, dest_own, count, own, other, feats, out, dest_other, acc, coded, sem):
+def add_terms(ny, nz, dest_of, terms, acc):
     k = lax.axis_index("k")
+    dump = acc.shape[0] - 1
     size = ny * NX + NX
-    of_y = jnp.where(k == 1, NX, 2 * nz * size // ny)
-    of_z = jnp.where(k == 1, size, RB)
+    of_y = jnp.where(k == 1, NX, nz * RB)
+    of_zl = jnp.where(k == 1, size, RB)
     of_zh = jnp.where(k == 1, nz * size, NX)
     bits = nz.bit_length() - 1
-    dump = acc.shape[0] - 1
+
+    def add(s, carry):
+        d, used = dest_of(s)
+        mine = jnp.logical_and(used, ((d >> 3) & 1) == k)
+        at = (d >> (4 + bits)) * of_y + ((d >> 4) & (nz - 1)) * of_zl
+        at = at + ((d >> 2) & 1) * of_zh + (d & (NX - 1))
+        at = jnp.where(mine, at, dump)
+        acc[at] = acc[at] + terms[s].astype(F32)
+        return carry
+
+    lax.fori_loop(0, TILES_DEV, add, 0, unroll=8)
+
+
+def own_kernel(ny, nz, dest_own, count, own, acc):
+    acc[...] = jnp.zeros_like(acc)
+    add_terms(ny, nz, lambda s: (dest_own[s], s < count[0]), own, acc)
+
+
+def both_kernel(ny, nz, first, other, feats, out_y, out_z, dest_other, acc, coded, sem):
     given = other[TILES_DEV].astype(F32)
     coded[...] = (given[0:1] * 8.0 + given[1:2]).astype(jnp.int32)
     copy = pltpu.make_async_copy(coded, dest_other, sem)
     copy.start()
-    acc[...] = jnp.zeros_like(acc)
-
-    def add_to(d, used, term):
-        mine = jnp.logical_and(used, ((d >> 3) & 1) == k)
-        at = (d >> (4 + bits)) * of_y + ((d >> 4) & (nz - 1)) * of_z
-        at = at + ((d >> 2) & 1) * of_zh + (d & (NX - 1))
-        at = jnp.where(mine, at, dump)
-        acc[at] = acc[at] + term.astype(F32)
-
-    def add_own(s, carry):
-        add_to(dest_own[s], s < count[0], own[s])
-        return carry
-
-    lax.fori_loop(0, TILES_DEV, add_own, 0, unroll=8)
+    acc[...] = first[...]
     copy.wait()
-
-    def add_other(s, carry):
-        d = dest_other[0, s]
-        add_to(d, d >= 0, other[s])
-        return carry
-
-    lax.fori_loop(0, TILES_DEV, add_other, 0, unroll=8)
-    out[...] = acc[0:dump].astype(BF)
+    add_terms(ny, nz, lambda s: (dest_other[0, s], dest_other[0, s] >= 0), other, acc)
+    k = lax.axis_index("k")
+
+    @pl.when(k == 0)
+    def _():
+        last = out_y.shape[0]
+        out_y[...] = acc[0:last].astype(BF)
 
     @pl.when(k == 1)
     def _():
+        last = out_z.shape[0]
+        out_z[...] = acc[0:last].astype(BF)
         for m in range(2 * nz):
             for x in range(NX):
                 b = (m // nz) * NX + x
-                out[m * size + ny * NX + x] = feats[:, b * TB : (b + 1) * TB]
+                at = m * (ny * NX + NX) + ny * NX + x
+                out_z[at] = feats[:, b * TB : (b + 1) * TB]
 
 
 def middle_z_kernel(nz, recv, out):
@@ -268,6 +288,7 @@
 
 def second_step_kernel(z_first, recv, out):
     came, places = recv.shape[0], out.shape[0]
+    sums_at = out.shape[1] - EXTRA
     bias = parted(added(recv, recv.shape[1] - 1))
     if z_first:
         nz = came // 2
@@ -277,8 +298,8 @@
                 at = (q % nz) * RB + (q // nz) * NX
                 out[p, at : at + NX] = recv[q, 0:NX]
             for n in range(4):
-                out[p, nz * RB + n] = sums[n]
-            out[p, nz * RB + 4] = bias
+                out[p, sums_at + n] = sums[n]
+            out[p, sums_at + 4] = bias
     else:
         for h in range(2):
             sums = [added(recv, 2 * NX + 4 * h + n).astype(BF) for n in range(4)]
@@ -286,26 +307,28 @@
                 for q in range(came):
                     out[p, q * NX : (q + 1) * NX] = recv[q, h * NX : (h + 1) * NX]
                 for n in range(4):
-                    out[p, came * NX + n] = sums[n]
-                out[p, came * NX + 4] = bias
-
-
-def share_kernel(first, recv_h, dx, out, bias_out, recv, sems):
-    copies = [
-        pltpu.make_async_copy(recv_h.at[p, pl.ds(first, EXTRA)], recv.at[p], sems.at[p])
-        for p in range(recv.shape[0])
-    ]
-    for copy in copies:
-        copy.start()
-    for copy in copies:
-        copy.wait()
-    sums = [jnp.sum(recv[:, n].astype(F32), axis=0) for n in range(EXTRA)]
-    rows = [x.astype(BF) for x in sums[:4]]
-    for p in range(out.shape[0]):
-        for n in range(4):
-            out[p, n * F_LOC : (n + 1) * F_LOC] = rows[n]
-        out[p, 4 * F_LOC : 5 * F_LOC] = dx[p % RB]
-    bias_out[...] = parted(sums[4])
+                    out[p, sums_at + n] = sums[n]
+                out[p, sums_at + 4] = bias
+
+
+def share_kernel(sizes, recv, dx, out, bias_out):
+    def run(size):
+        sums = []
+        for n in range(EXTRA):
+            at = range(size - EXTRA + n, recv.shape[0], size)
+            sums.append(sum(recv[m].astype(F32) for m in at))
+        rows = [x.astype(BF) for x in sums[:4]]
+        for p in range(out.shape[0]):
+            for n in range(4):
+                out[p, n * F_LOC : (n + 1) * F_LOC] = rows[n]
+            out[p, 4 * F_LOC : 5 * F_LOC] = dx[p % RB]
+        bias_out[...] = parted(sums[4])
+
+    if sizes[0] == sizes[1]:
+        run(sizes[0])
+    else:
+        for k in range(2):
+            pl.when(lax.axis_index("k") == k)(functools.partial(run, sizes[k]))
 
 
 def pick_kernel(nz, size_0, size_1, dest_own, count, dest_other, recv, bias_sum, own, other):
@@ -402,23 +425,33 @@
     )
     terms_other = lax.ppermute(terms, "k", swap)
     sent = 2 * nz * (ny + 1) * NX
-    dense, dest_other = whole(
-        functools.partial(dense_kernel, ny, nz),
-        (sds((sent, F_LOC, TB), BF), sds((1, TB), jnp.int32)),
-        [SMEM, SMEM, VMEM, VMEM, VMEM],
+    first = whole(
+        functools.partial(own_kernel, ny, nz),
+        sds((sent + 1, F_LOC, TB), F32),
+        [SMEM, SMEM, VMEM],
+        cost=lasting(1.2),
+    )(tile_dest, tile_count, terms)
+    dense_y, dense_z, dest_other = whole(
+        functools.partial(both_kernel, ny, nz),
+        (
+            sds((ny * nz * RB, F_LOC, TB), BF),
+            sds((sent, F_LOC, TB), BF),
+            sds((1, TB), jnp.int32),
+        ),
+        [VMEM] * 3,
         [
             pltpu.VMEM((sent + 1, F_LOC, TB), F32),
             pltpu.VMEM((1, TB), jnp.int32),
             pltpu.SemaphoreType.DMA,
         ],
-        [VMEM, SMEM],
-    )(tile_dest, tile_count, terms, terms_other, features)
+        [VMEM, VMEM, SMEM],
+    )(first, terms_other, features)
 
     def exchange(array, axes):
         return lax.all_to_all(array, axes, split_axis=0, concat_axis=0, tiled=True)
 
-    def z_collect(dense, features, degree2):
-        one = exchange(dense.reshape(2 * nz, (ny + 1) * NX, F_LOC, TB), ("zh", "zl"))
+    def z_collect(dense_y, dense_z, features, degree2):
+        one = exchange(dense_z.reshape(2 * nz, (ny + 1) * NX, F_LOC, TB), ("zh", "zl"))
         two = whole(
             functools.partial(middle_z_kernel, nz),
             sds((ny * NX, 4 * F_LOC, TB), BF),
@@ -429,8 +462,8 @@
             functools.partial(agg_kernel, True), sds((RB, 2 * F_LOC, TB), BF), [VMEM] * 2
         )(two, degree2)
 
-    def y_collect(dense, features, degree2):
-        one = exchange(dense.reshape(ny, sent // ny, F_LOC, TB), "y")
+    def y_collect(dense_y, dense_z, features, degree2):
+        one = exchange(dense_y.reshape(ny, nz * RB, F_LOC, TB), "y")
         two = whole(middle_y_kernel, sds((nz * RB, 2 * F_LOC, TB), BF), [VMEM] * 2)(
             one, features
         )
@@ -440,7 +473,7 @@
         )(two, degree2)
 
     full = lax.cond(
-        lax.axis_index("k") == 1, z_collect, y_collect, dense, features, degree2
+        lax.axis_index("k") == 1, z_collect, y_collect, dense_y, dense_z, features, degree2
     )
     hidden, back, dx_self = whole(
         dense_layer_kernel,
@@ -460,9 +493,8 @@
         first, second = (zs, "y") if z_first else ("y", zs)
         n1, n2 = lax.axis_size(first), lax.axis_size(second)
         width = NX + EXTRA if z_first else 2 * NX + 4 + EXTRA
-        sums_at = nz * RB if z_first else ny * NX
-
-        def run(back, dx_self):
+
+        def run(back):
             one = whole(
                 functools.partial(first_step_kernel, z_first),
                 sds((n1, width, F_LOC, TB), BF),
@@ -475,19 +507,16 @@
                 [VMEM],
             )(one)
             two = exchange(two, second)
-            share, bias_sum = whole(
-                functools.partial(share_kernel, sums_at),
-                (sds((2 * RB, 5 * F_LOC, TB), BF), sds((F_LOC, TB), BF)),
-                [ANY, VMEM],
-                [pltpu.VMEM((n2, EXTRA, F_LOC, TB), BF), pltpu.SemaphoreType.DMA((n2,))],
-            )(two, dx_self)
-            return two.reshape(tiles, F_LOC, TB), share, bias_sum
+            return two.reshape(tiles, F_LOC, TB)
 
         return run
 
-    portion, share, bias_sum = lax.cond(
-        lax.axis_index("k") == 0, in_two_steps(True), in_two_steps(False), back, dx_self
-    )
+    portion = lax.cond(lax.axis_index("k") == 0, in_two_steps(True), in_two_steps(False), back)
+    share, bias_sum = whole(
+        functools.partial(share_kernel, (tiles // ny, tiles // (2 * nz))),
+        (sds((2 * RB, 5 * F_LOC, TB), BF), sds((F_LOC, TB), BF)),
+        [VMEM] * 2,
+    )(portion, dx_self)
     chunks = exchange(share, ("k",) + COL)
     own, other = whole(
         functools.partial(pick_kernel, nz, tiles // ny, tiles // (2 * nz)),

time: 134 us -> 131 us (0.978)
  blocking collectives: 84.8 us -> 83.3 us
    all_to_all x4, blocking collectives: 84.8 us -> 83.3 us  [exchange(): return lax.all_to_all(array, axes, split_axis=0, concat_axis=0, tiled=True)]
    ppermute x1, waiting for transfers between devices: 1.35 us -> 0.01 us  [local(): terms_other = lax.ppermute(terms, 'k', swap)]
    pallas_call x2 -> x3, Pallas kernels: 4.06 us -> 4.06 us  [the longest x1 2.19 us: local(): whole(functools.partial(both_kernel, ny, nz), (sds((ny * nz * RB, F_LOC,...]
  transfers between devices with their start and end apart: 4 -> 4, of which waited for: 4 -> 3; matrix products, arithmetic and copies ran while one was open for 0% -> 0% of each run, Pallas kernels for 3% -> 4%
where the time goes in v6:
time: 131 us; the launch traced here: 129 us
  blocking collectives  83.3 us (64%)
  starting transfers between devices  17.6 us (13%)
  Pallas kernels  13.3 us (10%)
  waiting for transfers between devices  11.9 us (9%)
  between operations  1.48 us (1%)
  local copies, waits for them, and re-layouts  1.41 us (1%)
    all_to_all x4, blocking collectives, exchange(): return lax.all_to_all(array, axes, split_axis=0, concat_axis=0, tiled=True)  83.3 us
    all_to_all x2, waiting for transfers between devices, exchange(): return lax.all_to_all(array, axes, split_axis=0, concat_axis=0, tiled=True)  10.4 us
    ppermute x1, starting transfers between devices, local(): terms_other = lax.ppermute(terms, 'k', swap)  8.78 us
    all_to_all x2, starting transfers between devices, exchange(): return lax.all_to_all(array, axes, split_axis=0, concat_axis=0, tiled=True)  6.92 us
    pallas_call x1, Pallas kernels, tile_terms(): pl.pallas_call(terms_kernel, out_shape=sds((TILES_DEV + 1, F_LOC, TB), BF...  3 us
  transfers between devices with their start and end apart: 4, of which 3 were waited for; matrix products, arithmetic and copies ran while one was open for 0% of the time, Pallas kernels for 4%

profile of v6, /device:TPU:1, one launch (start us, length us, event | category | flops | bytes accessed | tf_op | source)
XLA Modules:
  0.0 129.0 jit_solution(13006820148525374001)
XLA Ops:
  0.6 0.0 copy-start.5
  1.3 3.0 %shard_map.137.own = bf16[65,16,128]{2,1,0:T(8,128)(2,1)} custom-call(s32[64]{0:T(128)} %src.1, s32[1,64]{1,0:T(1,128)} %bitcast.8, s32[1]{0:T(128)S(6)} %copy.19.count_h.count, bf16[16,1024]{1,0:T(8,128)(2,1)} %feats.1, bf16[64,128,128]{2,1,0:T(8,128)(2,1)} %vals.1), custom_call_target="tpu_custom_call" | custom-call | tf_op jit(solution)/shard_map/pallas_call | solution.py:107
  4.3 8.8 %collective-permute-start = (bf16[65,16,128]{2,1,0:T(8,128)(2,1)}, bf16[65,16,128]{2,1,0:T(8,128)(2,1)S(1)}, u32[]{:S(2)}, u32[]{:S(2)}) collective-permute-start(bf16[65,16,128]{2,1,0:T(8,128)(2,1)} %shard_map.137.own), channel_id=1, source_target_pairs={{0,8},{8,0},{1,9},{9,1},{2,10},{10,2},{3,11},{11,3},{4,12},{12,4},... | collective-permute-start | bytes 798728 | tf_op jit(solution)/shard_map/ppermute | solution.py:426
  13.1 0.0 copy-done.5
  13.1 0.0 copy-start.1
  13.1 0.9 copy-done.1
  14.1 0.0 copy-start.9
  14.1 1.1 shard_map.138.first
  15.2 0.0 copy-start.10
  15.2 0.0 collective-permute-done.other
  15.2 0.0 copy-done.9
  15.2 2.2 %shard_map.139 = (bf16[256,16,128]{2,1,0:T(8,128)(2,1)S(1)}, bf16[288,16,128]{2,1,0:T(8,128)(2,1)}, s32[1,128]{1,0:T(1,128)S(1)}) custom-call(f32[289,16,128]{2,1,0:T(8,128)S(1)} %shard_map.138.first, bf16[65,16,128]{2,1,0:T(8,128)(2,1)S(1)} %collective-permute-done.other, bf16[16,1024]{1,0:T(8,128)(2,1)S(1)} %copy-done.9), custom_call_target="tpu_custom_call" | custom-call | tf_op jit(solution)/shard_map/pallas_call | solution.py:434
  17.4 0.0 copy-done.10
  17.4 0.0 copy-start.2
  17.4 0.0 copy-start.3
  17.5 0.0 copy-start.4
  17.5 0.0 copy-start.7
  17.5 46.7 %conditional.2 = (bf16[8,32,128]{2,1,0:T(8,128)(2,1)S(1)}) conditional(s32[]{:T(128)} %convert_element_type.6, (bf16[256,16,128]{2,1,0:T(8,128)(2,1)S(1)}, bf16[16,1024]{1,0:T(8,128)(2,1)S(1)}, s32[8,128]{1,0:T(8,128)S(1)}) %tuple.28, (bf16[288,16,128]{2,1,0:T(8,128)(2,1)}, s32[8,128]{1,0:T(8,128)S(1)}) %tuple.29), branch_computations={%region_0.0_spmd, %region_1.0_spmd} | conditional | bytes 3407880 | solution.py:475
  17.5 24.0 %all_to_all.50.recv = bf16[8,36,16,128]{3,2,1,0:T(8,128)(2,1)S(1)} all-to-all(bf16[8,36,16,128]{3,2,1,0:T(8,128)(2,1)} %bitcast.12), channel_id=1, replica_groups=mesh['y'=8,'zl'=4,'k'=2,'zh'=2,'x'=4] {'zh','zl'}, dimensions={0} | all-to-all | bytes 2359296 | tf_op jit(solution)/shard_map/cond/branch_1_fun/all_to_all | solution.py:451
  41.5 0.1 branch_1_fun.4
  41.6 22.5 %all_to_all.51.recv = bf16[32,64,128]{2,1,0:T(8,128)(2,1)S(1)} all-to-all(bf16[32,64,128]{2,1,0:T(8,128)(2,1)S(1)} %branch_1_fun.4), channel_id=1, replica_groups=mesh['y'=8,'zl'=4,'k'=2,'zh'=2,'x'=4] {'y','x'}, dimensions={0} | all-to-all | bytes 1048576 | tf_op jit(solution)/shard_map/cond/branch_1_fun/all_to_all | solution.py:451
  64.2 0.0 copy-done.2
  64.2 0.0 copy-done.3
  64.2 0.0 copy-done.4
  64.2 0.0 copy-done.7
  64.2 1.2 shard_map.140
  65.4 3.4 %all-to-all-start.8 = ((bf16[4,11,16,128]{3,2,1,0:T(8,128)(2,1)}), bf16[4,11,16,128]{3,2,1,0:T(8,128)(2,1)S(1)}, u32[]{:S(2)}, u32[]{:S(2)}) async-start(bf16[4,11,16,128]{3,2,1,0:T(8,128)(2,1)} %get-tuple-element.45), calls=%async_computation.8 | async-start | bytes 360448 | tf_op jit(solution)/shard_map/all_to_all | solution.py:451
  68.8 5.3 %all-to-all-done.8 = bf16[4,11,16,128]{3,2,1,0:T(8,128)(2,1)S(1)} async-done(((bf16[4,11,16,128]{3,2,1,0:T(8,128)(2,1)}), bf16[4,11,16,128]{3,2,1,0:T(8,128)(2,1)S(1)}, u32[]{:S(2)}, u32[]{:S(2)}) %all-to-all-start.8) | async-done | bytes 180256 | tf_op jit(solution)/shard_map/all_to_all | solution.py:451
  74.0 37.0 %conditional.3 = (bf16[296,16,128]{2,1,0:T(8,128)(2,1)S(1)}) conditional(s32[]{:T(128)} %convert_element_type.7, bf16[4,11,16,128]{3,2,1,0:T(8,128)(2,1)S(1)} %all-to-all-done.8, bf16[4,11,16,128]{3,2,1,0:T(8,128)(2,1)S(1)} %all-to-all-done.8), branch_computations={%region_2.0_spmd, %region_3.0_spmd} | conditional | bytes 3538952 | solution.py:514
  74.0 0.1 branch_0_fun.6
  74.1 14.9 %all_to_all.52.recv = bf16[8,17,16,128]{3,2,1,0:T(8,128)(2,1)S(1)} all-to-all(bf16[8,17,16,128]{3,2,1,0:T(8,128)(2,1)S(1)} %branch_0_fun.6), channel_id=1, replica_groups=mesh['y'=8,'zl'=4,'k'=2,'zh'=2,'x'=4] {'y'}, dimensions={0} | all-to-all | bytes 1114112 | tf_op jit(solution)/shard_map/cond/branch_0_fun/all_to_all | solution.py:451
  89.0 0.1 branch_0_fun.7
  89.1 21.9 %all_to_all.53 = bf16[8,37,16,128]{3,2,1,0:T(8,128)(2,1)S(1)} all-to-all(bf16[8,37,16,128]{3,2,1,0:T(8,128)(2,1)S(1)} %branch_0_fun.7), channel_id=1, replica_groups=mesh['y'=8,'zl'=4,'k'=2,'zh'=2,'x'=4] {'zh','zl'}, dimensions={0} | all-to-all | bytes 2424832 | tf_op jit(solution)/shard_map/cond/branch_0_fun/all_to_all | solution.py:451
  111.0 0.0 copy-start.8
  111.0 0.0 copy-start
  111.0 0.7 shard_map.141
  111.8 0.0 copy-start.6
  111.8 0.4 copy-done.8
  112.2 3.6 %all-to-all-start.9 = ((bf16[16,80,128]{2,1,0:T(8,128)(2,1)}), bf16[16,80,128]{2,1,0:T(8,128)(2,1)S(1)}, u32[]{:S(2)}, u32[]{:S(2)}) async-start(bf16[16,80,128]{2,1,0:T(8,128)(2,1)} %get-tuple-element.47), calls=%async_computation.9 | async-start | bytes 655360 | tf_op jit(solution)/shard_map/all_to_all | solution.py:451
  115.8 2.1 %shard_map.142 = (bf16[64,16,128]{2,1,0:T(8,128)(2,1)S(1)}, bf16[65,16,128]{2,1,0:T(8,128)(2,1)S(1)}) custom-call(s32[64]{0:T(128)S(1)} %copy-done.5, s32[1]{0:T(128)S(6)} %copy.19.count_h.count, s32[1,128]{1,0:T(1,128)S(1)} %get-tuple-element.49.dest_other, bf16[296,16,128]{2,1,0:T(8,128)(2,1)} %copy-done.8, bf16[16,128]{1,0:T(8,128)(2,1)S(1)} %get-tuple-element.48.bias_sum), custom_call_target="tpu_custom_call" | custom-call | bytes 7200000 | tf_op jit(solution)/shard_map/pallas_call | solution.py:521
  117.9 1.9 %collective-permute-start.1 = (bf16[65,16,128]{2,1,0:T(8,128)(2,1)S(1)}, bf16[65,16,128]{2,1,0:T(8,128)(2,1)S(1)}, u32[]{:S(2)}, u32[]{:S(2)}) collective-permute-start(bf16[65,16,128]{2,1,0:T(8,128)(2,1)S(1)} %get-tuple-element.50), channel_id=1, source_target_pairs={{0,8},{8,0},{1,9},{9,1},{2,10},{10,2},{3,11},{11,3},{4,12},{12,4},... | collective-permute-start | bytes 798728 | tf_op jit(solution)/shard_map/ppermute | solution.py:527
  119.8 1.5 %collective-permute-done.1.given = bf16[65,16,128]{2,1,0:T(8,128)(2,1)S(1)} collective-permute-done((bf16[65,16,128]{2,1,0:T(8,128)(2,1)S(1)}, bf16[65,16,128]{2,1,0:T(8,128)(2,1)S(1)}, u32[]{:S(2)}, u32[]{:S(2)}) %collective-permute-start.1) | collective-permute-done | bytes 266272 | tf_op jit(solution)/shard_map/ppermute | solution.py:527
  121.4 0.0 copy-done
  121.4 0.0 copy-done.6
  121.4 1.6 %shard_map.143.dx_neigh = f32[8,16,128]{2,1,0:T(8,128)S(1)} custom-call(s32[64]{0:T(128)S(1)} %copy-done.6, bf16[64,16,128]{2,1,0:T(8,128)(2,1)S(1)} %get-tuple-element.51.own, bf16[65,16,128]{2,1,0:T(8,128)(2,1)S(1)} %collective-permute-done.1.given, bf16[64,128,128]{2,1,0:T(8,128)(2,1)S(1)} %copy-done), custom_call_target="tpu_custom_call" | custom-call | bytes 7920000 | tf_op jit(solution)/shard_map/pallas_call | solution.py:373
  123.0 5.1 %all-to-all-done.9.x = bf16[16,80,128]{2,1,0:T(8,128)(2,1)S(1)} async-done(((bf16[16,80,128]{2,1,0:T(8,128)(2,1)}), bf16[16,80,128]{2,1,0:T(8,128)(2,1)S(1)}, u32[]{:S(2)}, u32[]{:S(2)}) %all-to-all-start.9) | async-done | bytes 327712 | tf_op jit(solution)/shard_map/all_to_all | solution.py:451
  128.1 0.9 shard_map.144
  (1 shorter events, 0.0 us)
Async XLA Ops:
  0.6 12.5 %copy-start.5 = (s32[64]{0:T(128)S(1)}, s32[64]{0:T(128)}, u32[]{:S(2)}) copy-start(s32[64]{0:T(128)} %dest_own.3) | copy-start | bytes 772
  4.3 10.9 %collective-permute-start = (bf16[65,16,128]{2,1,0:T(8,128)(2,1)}, bf16[65,16,128]{2,1,0:T(8,128)(2,1)S(1)}, u32[]{:S(2)}, u32[]{:S(2)}) collective-permute-start(bf16[65,16,128]{2,1,0:T(8,128)(2,1)} %shard_map.137.own), channel_id=1, source_target_pairs={{0,8},{8,0},{1,9},{9,1},{2,10},{10,2},{3,11},{11,3},{4,12},{12,4},... | collective-permute-start | bytes 798728 | tf_op jit(solution)/shard_map/ppermute | solution.py:426
  13.1 1.0 copy-start.1
  14.1 1.1 copy-start.9
  15.2 2.2 %copy-start.10 = (s32[1024]{0:T(1024)S(1)}, s32[1024]{0:T(1024)}, u32[]{:S(2)}) copy-start(s32[1024]{0:T(1024)} %param.19) | copy-start | bytes 12292
  17.4 46.7 %copy-start.2 = (bf16[128,256]{1,0:T(8,128)(2,1)S(1)}, bf16[128,256]{1,0:T(8,128)(2,1)}, u32[]{:S(2)}) copy-start(bf16[128,256]{1,0:T(8,128)(2,1)} %w_self.1) | copy-start | bytes 196612
  17.4 46.7 %copy-start.3 = (bf16[128,256]{1,0:T(8,128)(2,1)S(1)}, bf16[128,256]{1,0:T(8,128)(2,1)}, u32[]{:S(2)}) copy-start(bf16[128,256]{1,0:T(8,128)(2,1)} %w_neigh.1) | copy-start | bytes 196612
  17.5 46.7 %copy-start.4 = (bf16[256,128]{1,0:T(8,128)(2,1)S(1)}, bf16[256,128]{1,0:T(8,128)(2,1)}, u32[]{:S(2)}) copy-start(bf16[256,128]{1,0:T(8,128)(2,1)} %cot.1) | copy-start | bytes 196612
  17.5 46.7 %copy-start.7 = (f32[256]{0:T(256)S(1)}, f32[256]{0:T(256)}, u32[]{:S(2)}) copy-start(f32[256]{0:T(256)} %param.22) | copy-start | bytes 3076
  65.4 8.6 %all-to-all-start.8 = ((bf16[4,11,16,128]{3,2,1,0:T(8,128)(2,1)}), bf16[4,11,16,128]{3,2,1,0:T(8,128)(2,1)S(1)}, u32[]{:S(2)}, u32[]{:S(2)}) async-start(bf16[4,11,16,128]{3,2,1,0:T(8,128)(2,1)} %get-tuple-element.45), calls=%async_computation.8 | async-start | bytes 360448 | tf_op jit(solution)/shard_map/all_to_all | solution.py:451
  111.0 1.2 copy-start.8
  111.0 10.3 %copy-start = (bf16[64,128,128]{2,1,0:T(8,128)(2,1)S(1)}, bf16[64,128,128]{2,1,0:T(8,128)(2,1)}, u32[]{:S(2)}) copy-start(bf16[64,128,128]{2,1,0:T(8,128)(2,1)} %vals.1) | copy-start | bytes 6291460
  111.8 9.6 %copy-start.6 = (s32[64]{0:T(128)S(1)}, s32[64]{0:T(128)}, u32[]{:S(2)}) copy-start(s32[64]{0:T(128)} %src.1) | copy-start | bytes 772
  112.2 15.9 %all-to-all-start.9 = ((bf16[16,80,128]{2,1,0:T(8,128)(2,1)}), bf16[16,80,128]{2,1,0:T(8,128)(2,1)S(1)}, u32[]{:S(2)}, u32[]{:S(2)}) async-start(bf16[16,80,128]{2,1,0:T(8,128)(2,1)} %get-tuple-element.47), calls=%async_computation.9 | async-start | bytes 655360 | tf_op jit(solution)/shard_map/all_to_all | solution.py:451
  117.9 3.4 %collective-permute-start.1 = (bf16[65,16,128]{2,1,0:T(8,128)(2,1)S(1)}, bf16[65,16,128]{2,1,0:T(8,128)(2,1)S(1)}, u32[]{:S(2)}, u32[]{:S(2)}) collective-permute-start(bf16[65,16,128]{2,1,0:T(8,128)(2,1)S(1)} %get-tuple-element.50), channel_id=1, source_target_pairs={{0,8},{8,0},{1,9},{9,1},{2,10},{10,2},{3,11},{11,3},{4,12},{12,4},... | collective-permute-start | bytes 798728 | tf_op jit(solution)/shard_map/ppermute | solution.py:527

commit v7 on v6

--- a/solution.py
+++ b/solution.py
@@ -418,6 +418,7 @@
 ):
     ny, nz = lax.axis_size("y"), lax.axis_size("zl")
     swap = [(0, 1), (1, 0)]
+    is_first = lax.axis_index("k") == 0
     degree2 = degree.reshape(RB, TB)
 
     terms = tile_terms(
@@ -473,7 +474,7 @@
         )(two, degree2)
 
     full = lax.cond(
-        lax.axis_index("k") == 1, z_collect, y_collect, dense_y, dense_z, features, degree2
+        is_first, y_collect, z_collect, dense_y, dense_z, features, degree2
     )
     hidden, back, dx_self = whole(
         dense_layer_kernel,
@@ -511,7 +512,7 @@
 
         return run
 
-    portion = lax.cond(lax.axis_index("k") == 0, in_two_steps(True), in_two_steps(False), back)
+    portion = lax.cond(is_first, in_two_steps(True), in_two_steps(False), back)
     share, bias_sum = whole(
         functools.partial(share_kernel, (tiles // ny, tiles // (2 * nz))),
         (sds((2 * RB, 5 * F_LOC, TB), BF), sds((F_LOC, TB), BF)),

time: 131 us -> 129 us (0.985)
  blocking collectives: 83.3 us -> 91.1 us
  waiting for transfers between devices: 11.9 us -> 6.71 us
  starting transfers between devices: 17.6 us -> 14.3 us
    all_to_all x4 -> x5, blocking collectives: 83.3 us -> 91.1 us  [exchange(): return lax.all_to_all(array, axes, split_axis=0, concat_axis=0, tiled=True)]
    all_to_all x2 -> x1, waiting for transfers between devices: 10.4 us -> 5.23 us  [exchange(): return lax.all_to_all(array, axes, split_axis=0, concat_axis=0, tiled=True)]
    all_to_all x2 -> x1, starting transfers between devices: 6.92 us -> 3.57 us  [exchange(): return lax.all_to_all(array, axes, split_axis=0, concat_axis=0, tiled=True)]
  transfers between devices with their start and end apart: 4 -> 3, of which waited for: 3 -> 2; matrix products, arithmetic and copies ran while one was open for 0% -> 0% of each run, Pallas kernels for 4% -> 4%
where the time goes in v7:
time: 129 us; the launch traced here: 128 us
  blocking collectives  91.1 us (71%)
  starting transfers between devices  14.3 us (11%)
  Pallas kernels  13 us (10%)
  waiting for transfers between devices  6.71 us (5%)
  between operations  1.47 us (1%)
  local copies, waits for them, and re-layouts  1.39 us (1%)
    all_to_all x5, blocking collectives, exchange(): return lax.all_to_all(array, axes, split_axis=0, concat_axis=0, tiled=True)  91.1 us
    ppermute x1, starting transfers between devices, local(): terms_other = lax.ppermute(terms, 'k', swap)  8.79 us
    all_to_all x1, waiting for transfers between devices, exchange(): return lax.all_to_all(array, axes, split_axis=0, concat_axis=0, tiled=True)  5.23 us
    all_to_all x1, starting transfers between devices, exchange(): return lax.all_to_all(array, axes, split_axis=0, concat_axis=0, tiled=True)  3.57 us
    pallas_call x1, Pallas kernels, tile_terms(): pl.pallas_call(terms_kernel, out_shape=sds((TILES_DEV + 1, F_LOC, TB), BF...  3 us
  transfers between devices with their start and end apart: 3, of which 2 were waited for; matrix products, arithmetic and copies ran while one was open for 0% of the time, Pallas kernels for 4%

profile of v7, /device:TPU:1, one launch (start us, length us, event | category | flops | bytes accessed | tf_op | source)
XLA Modules:
  0.0 128.1 jit_solution(12557832896629635479)
XLA Ops:
  0.6 0.0 copy-start.5
  1.3 3.0 %shard_map.137.own = bf16[65,16,128]{2,1,0:T(8,128)(2,1)} custom-call(s32[64]{0:T(128)} %src.1, s32[1,64]{1,0:T(1,128)} %bitcast.8, s32[1]{0:T(128)S(6)} %copy.19.count_h.count, bf16[16,1024]{1,0:T(8,128)(2,1)} %feats.1, bf16[64,128,128]{2,1,0:T(8,128)(2,1)} %vals.1), custom_call_target="tpu_custom_call" | custom-call | tf_op jit(solution)/shard_map/pallas_call | solution.py:107
  4.3 8.8 %collective-permute-start = (bf16[65,16,128]{2,1,0:T(8,128)(2,1)}, bf16[65,16,128]{2,1,0:T(8,128)(2,1)S(1)}, u32[]{:S(2)}, u32[]{:S(2)}) collective-permute-start(bf16[65,16,128]{2,1,0:T(8,128)(2,1)} %shard_map.137.own), channel_id=1, source_target_pairs={{0,8},{8,0},{1,9},{9,1},{2,10},{10,2},{3,11},{11,3},{4,12},{12,4},... | collective-permute-start | bytes 798728 | tf_op jit(solution)/shard_map/ppermute | solution.py:427
  13.1 0.0 copy-done.5
  13.1 0.0 copy-start.1
  13.1 0.9 copy-done.1
  14.1 0.0 copy-start.9
  14.1 1.1 shard_map.138.first
  15.2 0.0 copy-start.10
  15.2 0.0 collective-permute-done.other
  15.2 0.0 copy-done.9
  15.2 2.1 %shard_map.139 = (bf16[256,16,128]{2,1,0:T(8,128)(2,1)}, bf16[288,16,128]{2,1,0:T(8,128)(2,1)S(1)}, s32[1,128]{1,0:T(1,128)S(1)}) custom-call(f32[289,16,128]{2,1,0:T(8,128)S(1)} %shard_map.138.first, bf16[65,16,128]{2,1,0:T(8,128)(2,1)S(1)} %collective-permute-done.other, bf16[16,1024]{1,0:T(8,128)(2,1)S(1)} %copy-done.9), custom_call_target="tpu_custom_call" | custom-call | tf_op jit(solution)/shard_map/pallas_call | solution.py:435
  17.4 0.0 copy-done.10
  17.4 0.0 copy-start.2
  17.4 0.0 copy-start.3
  17.4 0.0 copy-start.4
  17.4 0.0 copy-start.7
  17.4 46.1 %conditional.2 = (bf16[8,32,128]{2,1,0:T(8,128)(2,1)S(1)}) conditional(s32[]{:T(128)} %convert_element_type.4, (bf16[288,16,128]{2,1,0:T(8,128)(2,1)S(1)}, s32[8,128]{1,0:T(8,128)S(1)}) %tuple.28, (bf16[256,16,128]{2,1,0:T(8,128)(2,1)}, bf16[16,1024]{1,0:T(8,128)(2,1)S(1)}, s32[8,128]{1,0:T(8,128)S(1)}) %tuple.29), branch_computations={%region_0.0_spmd, %region_1.0_spmd} | conditional | bytes 3407880 | solution.py:476
  17.4 23.8 %all_to_all.48.recv = bf16[8,36,16,128]{3,2,1,0:T(8,128)(2,1)S(1)} all-to-all(bf16[8,36,16,128]{3,2,1,0:T(8,128)(2,1)S(1)} %bitcast.12), channel_id=1, replica_groups=mesh['y'=8,'zl'=4,'k'=2,'zh'=2,'x'=4] {'zh','zl'}, dimensions={0} | all-to-all | bytes 2359296 | tf_op jit(solution)/shard_map/cond/branch_0_fun/all_to_all | solution.py:452
  41.2 0.1 branch_0_fun.4
  41.4 22.1 %all_to_all.49.recv = bf16[32,64,128]{2,1,0:T(8,128)(2,1)S(1)} all-to-all(bf16[32,64,128]{2,1,0:T(8,128)(2,1)S(1)} %branch_0_fun.4), channel_id=1, replica_groups=mesh['y'=8,'zl'=4,'k'=2,'zh'=2,'x'=4] {'y','x'}, dimensions={0} | all-to-all | bytes 1048576 | tf_op jit(solution)/shard_map/cond/branch_0_fun/all_to_all | solution.py:452
  63.5 0.0 copy-done.2
  63.6 0.0 copy-done.3
  63.6 0.0 copy-done.4
  63.6 0.0 copy-done.7
  63.6 1.0 shard_map.140
  64.6 8.4 %all_to_all.56 = bf16[4,11,16,128]{3,2,1,0:T(8,128)(2,1)S(1)} all-to-all(bf16[4,11,16,128]{3,2,1,0:T(8,128)(2,1)S(1)} %get-tuple-element.45), channel_id=1, replica_groups=mesh['y'=8,'zl'=4,'k'=2,'zh'=2,'x'=4] {'x'}, dimensions={0} | all-to-all | bytes 360448 | tf_op jit(solution)/shard_map/all_to_all | solution.py:452
  73.0 37.0 %conditional.3 = (bf16[296,16,128]{2,1,0:T(8,128)(2,1)S(1)}) conditional(s32[]{:T(128)} %convert_element_type.4, bf16[4,11,16,128]{3,2,1,0:T(8,128)(2,1)S(1)} %all_to_all.56, bf16[4,11,16,128]{3,2,1,0:T(8,128)(2,1)S(1)} %all_to_all.56), branch_computations={%region_2.0_spmd, %region_3.0_spmd} | conditional | bytes 3538952 | solution.py:515
  73.0 0.1 branch_0_fun.6
  73.1 14.9 %all_to_all.52.recv = bf16[8,17,16,128]{3,2,1,0:T(8,128)(2,1)S(1)} all-to-all(bf16[8,17,16,128]{3,2,1,0:T(8,128)(2,1)S(1)} %branch_0_fun.6), channel_id=1, replica_groups=mesh['y'=8,'zl'=4,'k'=2,'zh'=2,'x'=4] {'y'}, dimensions={0} | all-to-all | bytes 1114112 | tf_op jit(solution)/shard_map/cond/branch_0_fun/all_to_all | solution.py:452
  87.9 0.1 branch_0_fun.7
  88.1 21.9 %all_to_all.53 = bf16[8,37,16,128]{3,2,1,0:T(8,128)(2,1)S(1)} all-to-all(bf16[8,37,16,128]{3,2,1,0:T(8,128)(2,1)S(1)} %branch_0_fun.7), channel_id=1, replica_groups=mesh['y'=8,'zl'=4,'k'=2,'zh'=2,'x'=4] {'zh','zl'}, dimensions={0} | all-to-all | bytes 2424832 | tf_op jit(solution)/shard_map/cond/branch_0_fun/all_to_all | solution.py:452
  110.0 0.0 copy-start.8
  110.0 0.0 copy-start
  110.0 0.7 shard_map.141
  110.7 0.0 copy-start.6
  110.7 0.4 copy-done.8
  111.1 3.6 %all-to-all-start.9 = ((bf16[16,80,128]{2,1,0:T(8,128)(2,1)}), bf16[16,80,128]{2,1,0:T(8,128)(2,1)S(1)}, u32[]{:S(2)}, u32[]{:S(2)}) async-start(bf16[16,80,128]{2,1,0:T(8,128)(2,1)} %get-tuple-element.47), calls=%async_computation.9 | async-start | bytes 655360 | tf_op jit(solution)/shard_map/all_to_all | solution.py:452
  114.7 2.1 %shard_map.142 = (bf16[64,16,128]{2,1,0:T(8,128)(2,1)S(1)}, bf16[65,16,128]{2,1,0:T(8,128)(2,1)S(1)}) custom-call(s32[64]{0:T(128)S(1)} %copy-done.5, s32[1]{0:T(128)S(6)} %copy.19.count_h.count, s32[1,128]{1,0:T(1,128)S(1)} %get-tuple-element.49.dest_other, bf16[296,16,128]{2,1,0:T(8,128)(2,1)} %copy-done.8, bf16[16,128]{1,0:T(8,128)(2,1)S(1)} %get-tuple-element.48.bias_sum), custom_call_target="tpu_custom_call" | custom-call | bytes 7200000 | tf_op jit(solution)/shard_map/pallas_call | solution.py:522
  116.9 2.0 %collective-permute-start.1 = (bf16[65,16,128]{2,1,0:T(8,128)(2,1)S(1)}, bf16[65,16,128]{2,1,0:T(8,128)(2,1)S(1)}, u32[]{:S(2)}, u32[]{:S(2)}) collective-permute-start(bf16[65,16,128]{2,1,0:T(8,128)(2,1)S(1)} %get-tuple-element.50), channel_id=1, source_target_pairs={{0,8},{8,0},{1,9},{9,1},{2,10},{10,2},{3,11},{11,3},{4,12},{12,4},... | collective-permute-start | bytes 798728 | tf_op jit(solution)/shard_map/ppermute | solution.py:528
  118.8 1.5 %collective-permute-done.1.given = bf16[65,16,128]{2,1,0:T(8,128)(2,1)S(1)} collective-permute-done((bf16[65,16,128]{2,1,0:T(8,128)(2,1)S(1)}, bf16[65,16,128]{2,1,0:T(8,128)(2,1)S(1)}, u32[]{:S(2)}, u32[]{:S(2)}) %collective-permute-start.1) | collective-permute-done | bytes 266272 | tf_op jit(solution)/shard_map/ppermute | solution.py:528
  120.3 0.0 copy-done
  120.3 0.0 copy-done.6
  120.3 1.6 %shard_map.143.dx_neigh = f32[8,16,128]{2,1,0:T(8,128)S(1)} custom-call(s32[64]{0:T(128)S(1)} %copy-done.6, bf16[64,16,128]{2,1,0:T(8,128)(2,1)S(1)} %get-tuple-element.51.own, bf16[65,16,128]{2,1,0:T(8,128)(2,1)S(1)} %collective-permute-done.1.given, bf16[64,128,128]{2,1,0:T(8,128)(2,1)S(1)} %copy-done), custom_call_target="tpu_custom_call" | custom-call | bytes 7920000 | tf_op jit(solution)/shard_map/pallas_call | solution.py:373
  121.9 5.2 %all-to-all-done.9.x = bf16[16,80,128]{2,1,0:T(8,128)(2,1)S(1)} async-done(((bf16[16,80,128]{2,1,0:T(8,128)(2,1)}), bf16[16,80,128]{2,1,0:T(8,128)(2,1)S(1)}, u32[]{:S(2)}, u32[]{:S(2)}) %all-to-all-start.9) | async-done | bytes 327712 | tf_op jit(solution)/shard_map/all_to_all | solution.py:452
  127.1 0.9 shard_map.144
  (1 shorter events, 0.0 us)
Async XLA Ops:
  0.6 12.5 %copy-start.5 = (s32[64]{0:T(128)S(1)}, s32[64]{0:T(128)}, u32[]{:S(2)}) copy-start(s32[64]{0:T(128)} %dest_own.3) | copy-start | bytes 772
  4.3 10.9 %collective-permute-start = (bf16[65,16,128]{2,1,0:T(8,128)(2,1)}, bf16[65,16,128]{2,1,0:T(8,128)(2,1)S(1)}, u32[]{:S(2)}, u32[]{:S(2)}) collective-permute-start(bf16[65,16,128]{2,1,0:T(8,128)(2,1)} %shard_map.137.own), channel_id=1, source_target_pairs={{0,8},{8,0},{1,9},{9,1},{2,10},{10,2},{3,11},{11,3},{4,12},{12,4},... | collective-permute-start | bytes 798728 | tf_op jit(solution)/shard_map/ppermute | solution.py:427
  13.1 1.0 copy-start.1
  14.1 1.2 copy-start.9
  15.2 2.2 %copy-start.10 = (s32[1024]{0:T(1024)S(1)}, s32[1024]{0:T(1024)}, u32[]{:S(2)}) copy-start(s32[1024]{0:T(1024)} %param.19) | copy-start | bytes 12292
  17.4 46.2 %copy-start.2 = (bf16[128,256]{1,0:T(8,128)(2,1)S(1)}, bf16[128,256]{1,0:T(8,128)(2,1)}, u32[]{:S(2)}) copy-start(bf16[128,256]{1,0:T(8,128)(2,1)} %w_self.1) | copy-start | bytes 196612
  17.4 46.2 %copy-start.3 = (bf16[128,256]{1,0:T(8,128)(2,1)S(1)}, bf16[128,256]{1,0:T(8,128)(2,1)}, u32[]{:S(2)}) copy-start(bf16[128,256]{1,0:T(8,128)(2,1)} %w_neigh.1) | copy-start | bytes 196612
  17.4 46.2 %copy-start.4 = (bf16[256,128]{1,0:T(8,128)(2,1)S(1)}, bf16[256,128]{1,0:T(8,128)(2,1)}, u32[]{:S(2)}) copy-start(bf16[256,128]{1,0:T(8,128)(2,1)} %cot.1) | copy-start | bytes 196612
  17.4 46.2 %copy-start.7 = (f32[256]{0:T(256)S(1)}, f32[256]{0:T(256)}, u32[]{:S(2)}) copy-start(f32[256]{0:T(256)} %param.22) | copy-start | bytes 3076
  110.0 1.2 copy-start.8
  110.0 10.3 %copy-start = (bf16[64,128,128]{2,1,0:T(8,128)(2,1)S(1)}, bf16[64,128,128]{2,1,0:T(8,128)(2,1)}, u32[]{:S(2)}) copy-start(bf16[64,128,128]{2,1,0:T(8,128)(2,1)} %vals.1) | copy-start | bytes 6291460
  110.7 9.6 %copy-start.6 = (s32[64]{0:T(128)S(1)}, s32[64]{0:T(128)}, u32[]{:S(2)}) copy-start(s32[64]{0:T(128)} %src.1) | copy-start | bytes 772
  111.1 16.0 %all-to-all-start.9 = ((bf16[16,80,128]{2,1,0:T(8,128)(2,1)}), bf16[16,80,128]{2,1,0:T(8,128)(2,1)S(1)}, u32[]{:S(2)}, u32[]{:S(2)}) async-start(bf16[16,80,128]{2,1,0:T(8,128)(2,1)} %get-tuple-element.47), calls=%async_computation.9 | async-start | bytes 655360 | tf_op jit(solution)/shard_map/all_to_all | solution.py:452
  116.9 3.4 %collective-permute-start.1 = (bf16[65,16,128]{2,1,0:T(8,128)(2,1)S(1)}, bf16[65,16,128]{2,1,0:T(8,128)(2,1)S(1)}, u32[]{:S(2)}, u32[]{:S(2)}) collective-permute-start(bf16[65,16,128]{2,1,0:T(8,128)(2,1)S(1)} %get-tuple-element.50), channel_id=1, source_target_pairs={{0,8},{8,0},{1,9},{9,1},{2,10},{10,2},{3,11},{11,3},{4,12},{12,4},... | collective-permute-start | bytes 798728 | tf_op jit(solution)/shard_map/ppermute | solution.py:528

commit v8 on v7

--- a/solution.py
+++ b/solution.py
@@ -15,7 +15,7 @@
 Y = 8
 NX = 4
 STEP = 16
-EXTRA = 5
+EXTRA = 3
 
 EPS = 1e-06
 BF = jnp.bfloat16
@@ -245,14 +245,13 @@
         rows = slice(c * F_LOC, (c + 1) * F_LOC)
         h, x = c // NX, c % NX
         dx_out[c] = dx_self[rows]
-        out[x, h] = dsum[rows]
-        first = 2 + 4 * h
-        out[x, first] = part_self[rows, 0:TB].astype(BF)
-        out[x, first + 1] = part_self[rows, TB:].astype(BF)
-        out[x, first + 2] = part_neigh[rows, 0:TB].astype(BF)
-        out[x, first + 3] = part_neigh[rows, TB:].astype(BF)
-    for x in range(NX):
-        out[x, 10] = tail
+        for k, part in enumerate((part_self, part_neigh)):
+            at = k * NX + x
+            out[at, h] = dsum[rows]
+            out[at, 2 + 2 * h] = part[rows, 0:TB].astype(BF)
+            out[at, 3 + 2 * h] = part[rows, TB:].astype(BF)
+    for at in range(2 * NX):
+        out[at, 6] = tail
 
 
 def parted(tail):
@@ -270,17 +269,18 @@
 
 def first_step_kernel(z_first, recv, out):
     places = out.shape[0]
-    bias = parted(added(recv, 10))
+    mine = 0 if z_first else NX
+    bias = parted(added(recv, 6))
     for h in range(2):
-        sums = [added(recv, 2 + 4 * h + n).astype(BF) for n in range(4)]
+        sums = [added(recv, 2 + 2 * h + n).astype(BF) for n in range(2)]
         at = 0 if z_first else NX * h
-        sums_at = NX if z_first else 2 * NX + 4 * h
+        sums_at = NX if z_first else 2 * NX + 2 * h
         for p in range(places):
             if z_first and p // (places // 2) != h:
                 continue
             for x in range(NX):
-                out[p, at + x] = recv[x, h]
-            for n in range(4):
+                out[p, at + x] = recv[mine + x, h]
+            for n in range(2):
                 out[p, sums_at + n] = sums[n]
     for p in range(places):
         out[p, out.shape[1] - 1] = bias
@@ -292,23 +292,23 @@
     bias = parted(added(recv, recv.shape[1] - 1))
     if z_first:
         nz = came // 2
-        sums = [added(recv, NX + n).astype(BF) for n in range(4)]
+        sums = [added(recv, NX + n).astype(BF) for n in range(2)]
         for p in range(places):
             for q in range(came):
                 at = (q % nz) * RB + (q // nz) * NX
                 out[p, at : at + NX] = recv[q, 0:NX]
-            for n in range(4):
+            for n in range(2):
                 out[p, sums_at + n] = sums[n]
-            out[p, sums_at + 4] = bias
+            out[p, sums_at + 2] = bias
     else:
         for h in range(2):
-            sums = [added(recv, 2 * NX + 4 * h + n).astype(BF) for n in range(4)]
+            sums = [added(recv, 2 * NX + 2 * h + n).astype(BF) for n in range(2)]
             for p in range(places // 2 * h, places // 2 * (h + 1)):
                 for q in range(came):
                     out[p, q * NX : (q + 1) * NX] = recv[q, h * NX : (h + 1) * NX]
-                for n in range(4):
+                for n in range(2):
                     out[p, sums_at + n] = sums[n]
-                out[p, sums_at + 4] = bias
+                out[p, sums_at + 2] = bias
 
 
 def share_kernel(sizes, recv, dx, out, bias_out):
@@ -317,12 +317,12 @@
         for n in range(EXTRA):
             at = range(size - EXTRA + n, recv.shape[0], size)
             sums.append(sum(recv[m].astype(F32) for m in at))
-        rows = [x.astype(BF) for x in sums[:4]]
+        rows = [x.astype(BF) for x in sums[:2]]
         for p in range(out.shape[0]):
-            for n in range(4):
+            for n in range(2):
                 out[p, n * F_LOC : (n + 1) * F_LOC] = rows[n]
-            out[p, 4 * F_LOC : 5 * F_LOC] = dx[p % RB]
-        bias_out[...] = parted(sums[4])
+            out[p, 2 * F_LOC : 3 * F_LOC] = dx[p % RB]
+        bias_out[...] = parted(sums[2])
 
     if sizes[0] == sizes[1]:
         run(sizes[0])
@@ -385,22 +385,20 @@
 
 
 def last_kernel(x, bias_sum, given, dx_neigh, grad_x, grad_self, grad_neigh, grad_bias):
-    for first, out in ((0, grad_self), (32, grad_neigh)):
-        rows = slice(first, first + 32)
-        part = x[0:RB, rows].astype(F32) + x[RB : 2 * RB, rows].astype(F32)
+    for k, out in enumerate((grad_self, grad_neigh)):
+        part = x[k * RB : (k + 1) * RB, 0 : 2 * F_LOC].astype(F32)
         scale = jnp.sqrt(jnp.sum(part * part) / (RB * 32 * TB) + EPS)
         scaled = part / scale
         for c in range(RB):
             at = slice(c * F_LOC, (c + 1) * F_LOC)
             out[at, 0:TB] = scaled[c, 0:16]
             out[at, TB:] = scaled[c, 16:32]
-    mine = bias_sum[...].astype(F32)
-    theirs = given[TILES_DEV].astype(F32)
-    two = (mine[0:2] + mine[2:4]) + (theirs[0:2] + theirs[2:4])
+    k = lax.axis_index("k")
+    tail = jnp.where(k == 0, bias_sum[...], given[TILES_DEV]).astype(F32)
+    two = tail[0:2] + tail[2:4]
     grad_bias[...] = two / jnp.sqrt(jnp.mean(two * two) + EPS)
-    here = lax.axis_index("k") * RB
     for b in range(RB):
-        dx_self = x[here + b, 4 * F_LOC : 5 * F_LOC].astype(F32)
+        dx_self = x[k * RB + b, 2 * F_LOC : 3 * F_LOC].astype(F32)
         grad_x[:, b * TB : (b + 1) * TB] = (dx_self + dx_neigh[b]).astype(BF)
 
 
@@ -480,12 +478,12 @@
         dense_layer_kernel,
         (
             sds(cotangent.shape, BF),
-            sds((NX, 11, F_LOC, TB), BF),
+            sds((2 * NX, 7, F_LOC, TB), BF),
             sds((RB, F_LOC, TB), BF),
         ),
         [VMEM] * 6,
     )(full, w_self, w_neigh, bias.reshape(1, -1), cotangent, degree2)
-    back = exchange(back, "x")
+    back = exchange(back, ("k", "x"))
 
     tiles = max(ny * (nz * RB + EXTRA), 2 * nz * (ny * NX + EXTRA))
 
@@ -493,7 +491,7 @@
         zs = ("zh", "zl")
         first, second = (zs, "y") if z_first else ("y", zs)
         n1, n2 = lax.axis_size(first), lax.axis_size(second)
-        width = NX + EXTRA if z_first else 2 * NX + 4 + EXTRA
+        width = NX + EXTRA if z_first else 2 * NX + 2 + EXTRA
 
         def run(back):
             one = whole(
@@ -515,7 +513,7 @@
     portion = lax.cond(is_first, in_two_steps(True), in_two_steps(False), back)
     share, bias_sum = whole(
         functools.partial(share_kernel, (tiles // ny, tiles // (2 * nz))),
-        (sds((2 * RB, 5 * F_LOC, TB), BF), sds((F_LOC, TB), BF)),
+        (sds((2 * RB, 3 * F_LOC, TB), BF), sds((F_LOC, TB), BF)),
         [VMEM] * 2,
     )(portion, dx_self)
     chunks = exchange(share, ("k",) + COL)

time: 129 us -> 127 us (0.984)
  transfers between devices with their start and end apart: 3 -> 3, of which waited for: 2 -> 2; matrix products, arithmetic and copies ran while one was open for 0% -> 0% of each run, Pallas kernels for 4% -> 3%
where the time goes in v8:
time: 127 us; the launch traced here: 126 us
  blocking collectives  90.2 us (71%)
  starting transfers between devices  14.8 us (12%)
  Pallas kernels  12.4 us (10%)
  waiting for transfers between devices  6.05 us (5%)
  between operations  1.46 us (1%)
    all_to_all x5, blocking collectives, exchange(): return lax.all_to_all(array, axes, split_axis=0, concat_axis=0, tiled=True)  90.2 us
    ppermute x1, starting transfers between devices, local(): terms_other = lax.ppermute(terms, 'k', swap)  8.79 us
    all_to_all x1, waiting for transfers between devices, exchange(): return lax.all_to_all(array, axes, split_axis=0, concat_axis=0, tiled=True)  4.71 us
    all_to_all x1, starting transfers between devices, exchange(): return lax.all_to_all(array, axes, split_axis=0, concat_axis=0, tiled=True)  3.88 us
    pallas_call x1, Pallas kernels, tile_terms(): pl.pallas_call(terms_kernel, out_shape=sds((TILES_DEV + 1, F_LOC, TB), BF...  3.28 us
  transfers between devices with their start and end apart: 3, of which 2 were waited for; matrix products, arithmetic and copies ran while one was open for 0% of the time, Pallas kernels for 3%

profile of v8, /device:TPU:1, one launch (start us, length us, event | category | flops | bytes accessed | tf_op | source)
XLA Modules:
  0.0 126.0 jit_solution(5485740129103966452)
XLA Ops:
  1.3 0.0 copy-start.5
  1.3 3.3 %shard_map.137.own = bf16[65,16,128]{2,1,0:T(8,128)(2,1)} custom-call(s32[64]{0:T(128)} %src.1, s32[1,64]{1,0:T(1,128)} %bitcast.8, s32[1]{0:T(128)S(6)} %copy.19.count_h.count, bf16[16,1024]{1,0:T(8,128)(2,1)} %feats.1, bf16[64,128,128]{2,1,0:T(8,128)(2,1)} %vals.1), custom_call_target="tpu_custom_call" | custom-call | tf_op jit(solution)/shard_map/pallas_call | solution.py:107
  4.6 8.8 %collective-permute-start = (bf16[65,16,128]{2,1,0:T(8,128)(2,1)}, bf16[65,16,128]{2,1,0:T(8,128)(2,1)S(1)}, u32[]{:S(2)}, u32[]{:S(2)}) collective-permute-start(bf16[65,16,128]{2,1,0:T(8,128)(2,1)} %shard_map.137.own), channel_id=1, source_target_pairs={{0,8},{8,0},{1,9},{9,1},{2,10},{10,2},{3,11},{11,3},{4,12},{12,4},... | collective-permute-start | bytes 798728 | tf_op jit(solution)/shard_map/ppermute | solution.py:425
  13.4 0.0 copy-done.5
  13.4 0.0 copy-start.1
  13.4 0.9 copy-done.1
  14.3 0.0 copy-start.8
  14.3 1.1 shard_map.138.first
  15.5 0.0 copy-start.9
  15.5 0.0 collective-permute-done.other
  15.5 0.0 copy-done.8
  15.5 2.2 %shard_map.139 = (bf16[256,16,128]{2,1,0:T(8,128)(2,1)}, bf16[288,16,128]{2,1,0:T(8,128)(2,1)S(1)}, s32[1,128]{1,0:T(1,128)S(1)}) custom-call(f32[289,16,128]{2,1,0:T(8,128)S(1)} %shard_map.138.first, bf16[65,16,128]{2,1,0:T(8,128)(2,1)S(1)} %collective-permute-done.other, bf16[16,1024]{1,0:T(8,128)(2,1)S(1)} %copy-done.8), custom_call_target="tpu_custom_call" | custom-call | tf_op jit(solution)/shard_map/pallas_call | solution.py:433
  17.7 0.0 copy-done.9
  17.7 0.0 copy-start.2
  17.7 0.0 copy-start.3
  17.7 0.0 copy-start.4
  17.7 0.0 copy-start.7
  17.7 46.1 %conditional.2 = (bf16[8,32,128]{2,1,0:T(8,128)(2,1)S(1)}) conditional(s32[]{:T(128)} %convert_element_type.4, (bf16[288,16,128]{2,1,0:T(8,128)(2,1)S(1)}, s32[8,128]{1,0:T(8,128)S(1)}) %tuple.28, (bf16[256,16,128]{2,1,0:T(8,128)(2,1)}, bf16[16,1024]{1,0:T(8,128)(2,1)S(1)}, s32[8,128]{1,0:T(8,128)S(1)}) %tuple.29), branch_computations={%region_0.0_spmd, %region_1.0_spmd} | conditional | bytes 3407880 | solution.py:474
  17.7 23.8 %all_to_all.48.recv = bf16[8,36,16,128]{3,2,1,0:T(8,128)(2,1)S(1)} all-to-all(bf16[8,36,16,128]{3,2,1,0:T(8,128)(2,1)S(1)} %bitcast.12), channel_id=1, replica_groups=mesh['y'=8,'zl'=4,'k'=2,'zh'=2,'x'=4] {'zh','zl'}, dimensions={0} | all-to-all | bytes 2359296 | tf_op jit(solution)/shard_map/cond/branch_0_fun/all_to_all | solution.py:450
  41.5 0.1 branch_0_fun.4
  41.6 22.2 %all_to_all.49.recv = bf16[32,64,128]{2,1,0:T(8,128)(2,1)S(1)} all-to-all(bf16[32,64,128]{2,1,0:T(8,128)(2,1)S(1)} %branch_0_fun.4), channel_id=1, replica_groups=mesh['y'=8,'zl'=4,'k'=2,'zh'=2,'x'=4] {'y','x'}, dimensions={0} | all-to-all | bytes 1048576 | tf_op jit(solution)/shard_map/cond/branch_0_fun/all_to_all | solution.py:450
  63.8 0.0 copy-done.2
  63.8 0.0 copy-done.3
  63.9 0.0 copy-done.4
  63.9 0.0 copy-done.7
  63.9 0.9 shard_map.140
  64.8 9.5 %all_to_all.56 = bf16[8,7,16,128]{3,2,1,0:T(8,128)(2,1)S(1)} all-to-all(bf16[8,7,16,128]{3,2,1,0:T(8,128)(2,1)S(1)} %get-tuple-element.45), channel_id=1, replica_groups=mesh['y'=8,'zl'=4,'k'=2,'zh'=2,'x'=4] {'k','x'}, dimensions={0} | all-to-all | bytes 458752 | tf_op jit(solution)/shard_map/all_to_all | solution.py:450
  74.3 35.1 %conditional.3 = (bf16[280,16,128]{2,1,0:T(8,128)(2,1)S(1)}) conditional(s32[]{:T(128)} %convert_element_type.4, bf16[8,7,16,128]{3,2,1,0:T(8,128)(2,1)S(1)} %all_to_all.56, bf16[8,7,16,128]{3,2,1,0:T(8,128)(2,1)S(1)} %all_to_all.56), branch_computations={%region_2.0_spmd, %region_3.0_spmd} | conditional | bytes 3145736 | solution.py:513
  74.3 0.1 branch_0_fun.6
  74.3 13.5 %all_to_all.52.recv = bf16[8,13,16,128]{3,2,1,0:T(8,128)(2,1)S(1)} all-to-all(bf16[8,13,16,128]{3,2,1,0:T(8,128)(2,1)S(1)} %branch_0_fun.6), channel_id=1, replica_groups=mesh['y'=8,'zl'=4,'k'=2,'zh'=2,'x'=4] {'y'}, dimensions={0} | all-to-all | bytes 851968 | tf_op jit(solution)/shard_map/cond/branch_0_fun/all_to_all | solution.py:450
  87.8 0.1 branch_0_fun.7
  87.9 21.4 %all_to_all.53 = bf16[8,35,16,128]{3,2,1,0:T(8,128)(2,1)S(1)} all-to-all(bf16[8,35,16,128]{3,2,1,0:T(8,128)(2,1)S(1)} %branch_0_fun.7), channel_id=1, replica_groups=mesh['y'=8,'zl'=4,'k'=2,'zh'=2,'x'=4] {'zh','zl'}, dimensions={0} | all-to-all | bytes 2293760 | tf_op jit(solution)/shard_map/cond/branch_0_fun/all_to_all | solution.py:450
  109.3 0.0 copy-start
  109.3 0.0 copy-start.6
  109.3 0.7 shard_map.141
  110.0 3.9 %all-to-all-start.9 = ((bf16[16,48,128]{2,1,0:T(8,128)(2,1)}), bf16[16,48,128]{2,1,0:T(8,128)(2,1)S(1)}, u32[]{:S(2)}, u32[]{:S(2)}) async-start(bf16[16,48,128]{2,1,0:T(8,128)(2,1)} %get-tuple-element.47), calls=%async_computation.9 | async-start | bytes 393216 | tf_op jit(solution)/shard_map/all_to_all | solution.py:450
  113.9 1.4 %shard_map.142 = (bf16[64,16,128]{2,1,0:T(8,128)(2,1)S(1)}, bf16[65,16,128]{2,1,0:T(8,128)(2,1)S(1)}) custom-call(s32[64]{0:T(128)S(1)} %copy-done.5, s32[1]{0:T(128)S(6)} %copy.19.count_h.count, s32[1,128]{1,0:T(1,128)S(1)} %get-tuple-element.49.dest_other, bf16[280,16,128]{2,1,0:T(8,128)(2,1)S(1)} %get-tuple-element.57.recv, ...), custom_call_target="tpu_custom_call" | custom-call | bytes 7200000 | tf_op jit(solution)/shard_map/pallas_call | solution.py:520
  115.3 2.1 %collective-permute-start.1 = (bf16[65,16,128]{2,1,0:T(8,128)(2,1)S(1)}, bf16[65,16,128]{2,1,0:T(8,128)(2,1)S(1)}, u32[]{:S(2)}, u32[]{:S(2)}) collective-permute-start(bf16[65,16,128]{2,1,0:T(8,128)(2,1)S(1)} %get-tuple-element.50), channel_id=1, source_target_pairs={{0,8},{8,0},{1,9},{9,1},{2,10},{10,2},{3,11},{11,3},{4,12},{12,4},... | collective-permute-start | bytes 798728 | tf_op jit(solution)/shard_map/ppermute | solution.py:526
  117.4 1.3 %collective-permute-done.1.given = bf16[65,16,128]{2,1,0:T(8,128)(2,1)S(1)} collective-permute-done((bf16[65,16,128]{2,1,0:T(8,128)(2,1)S(1)}, bf16[65,16,128]{2,1,0:T(8,128)(2,1)S(1)}, u32[]{:S(2)}, u32[]{:S(2)}) %collective-permute-start.1) | collective-permute-done | bytes 266272 | tf_op jit(solution)/shard_map/ppermute | solution.py:526
  118.7 0.0 copy-done
  118.7 0.0 copy-done.6
  118.7 1.6 %shard_map.143.dx_neigh = f32[8,16,128]{2,1,0:T(8,128)S(1)} custom-call(s32[64]{0:T(128)S(1)} %copy-done.6, bf16[64,16,128]{2,1,0:T(8,128)(2,1)S(1)} %get-tuple-element.51.own, bf16[65,16,128]{2,1,0:T(8,128)(2,1)S(1)} %collective-permute-done.1.given, bf16[64,128,128]{2,1,0:T(8,128)(2,1)S(1)} %copy-done), custom_call_target="tpu_custom_call" | custom-call | bytes 7920000 | tf_op jit(solution)/shard_map/pallas_call | solution.py:373
  120.3 4.7 %all-to-all-done.9.x = bf16[16,48,128]{2,1,0:T(8,128)(2,1)S(1)} async-done(((bf16[16,48,128]{2,1,0:T(8,128)(2,1)}), bf16[16,48,128]{2,1,0:T(8,128)(2,1)S(1)}, u32[]{:S(2)}, u32[]{:S(2)}) %all-to-all-start.9) | async-done | bytes 196640 | tf_op jit(solution)/shard_map/all_to_all | solution.py:450
  125.0 0.9 shard_map.144
  (1 shorter events, 0.0 us)
Async XLA Ops:
  1.3 12.1 %copy-start.5 = (s32[64]{0:T(128)S(1)}, s32[64]{0:T(128)}, u32[]{:S(2)}) copy-start(s32[64]{0:T(128)} %dest_own.3) | copy-start | bytes 772
  4.6 10.9 %collective-permute-start = (bf16[65,16,128]{2,1,0:T(8,128)(2,1)}, bf16[65,16,128]{2,1,0:T(8,128)(2,1)S(1)}, u32[]{:S(2)}, u32[]{:S(2)}) collective-permute-start(bf16[65,16,128]{2,1,0:T(8,128)(2,1)} %shard_map.137.own), channel_id=1, source_target_pairs={{0,8},{8,0},{1,9},{9,1},{2,10},{10,2},{3,11},{11,3},{4,12},{12,4},... | collective-permute-start | bytes 798728 | tf_op jit(solution)/shard_map/ppermute | solution.py:425
  13.4 1.0 copy-start.1
  14.3 1.2 copy-start.8
  15.5 2.2 %copy-start.9 = (s32[1024]{0:T(1024)S(1)}, s32[1024]{0:T(1024)}, u32[]{:S(2)}) copy-start(s32[1024]{0:T(1024)} %param.19) | copy-start | bytes 12292
  17.7 46.2 %copy-start.2 = (bf16[128,256]{1,0:T(8,128)(2,1)S(1)}, bf16[128,256]{1,0:T(8,128)(2,1)}, u32[]{:S(2)}) copy-start(bf16[128,256]{1,0:T(8,128)(2,1)} %w_self.1) | copy-start | bytes 196612
  17.7 46.2 %copy-start.3 = (bf16[128,256]{1,0:T(8,128)(2,1)S(1)}, bf16[128,256]{1,0:T(8,128)(2,1)}, u32[]{:S(2)}) copy-start(bf16[128,256]{1,0:T(8,128)(2,1)} %w_neigh.1) | copy-start | bytes 196612
  17.7 46.2 %copy-start.4 = (bf16[256,128]{1,0:T(8,128)(2,1)S(1)}, bf16[256,128]{1,0:T(8,128)(2,1)}, u32[]{:S(2)}) copy-start(bf16[256,128]{1,0:T(8,128)(2,1)} %cot.1) | copy-start | bytes 196612
  17.7 46.2 %copy-start.7 = (f32[256]{0:T(256)S(1)}, f32[256]{0:T(256)}, u32[]{:S(2)}) copy-start(f32[256]{0:T(256)} %param.22) | copy-start | bytes 3076
  109.3 9.4 %copy-start = (bf16[64,128,128]{2,1,0:T(8,128)(2,1)S(1)}, bf16[64,128,128]{2,1,0:T(8,128)(2,1)}, u32[]{:S(2)}) copy-start(bf16[64,128,128]{2,1,0:T(8,128)(2,1)} %vals.1) | copy-start | bytes 6291460
  109.3 9.4 %copy-start.6 = (s32[64]{0:T(128)S(1)}, s32[64]{0:T(128)}, u32[]{:S(2)}) copy-start(s32[64]{0:T(128)} %src.1) | copy-start | bytes 772
  110.0 15.0 %all-to-all-start.9 = ((bf16[16,48,128]{2,1,0:T(8,128)(2,1)}), bf16[16,48,128]{2,1,0:T(8,128)(2,1)S(1)}, u32[]{:S(2)}, u32[]{:S(2)}) async-start(bf16[16,48,128]{2,1,0:T(8,128)(2,1)} %get-tuple-element.47), calls=%async_computation.9 | async-start | bytes 393216 | tf_op jit(solution)/shard_map/all_to_all | solution.py:450
  115.3 3.4 %collective-permute-start.1 = (bf16[65,16,128]{2,1,0:T(8,128)(2,1)S(1)}, bf16[65,16,128]{2,1,0:T(8,128)(2,1)S(1)}, u32[]{:S(2)}, u32[]{:S(2)}) collective-permute-start(bf16[65,16,128]{2,1,0:T(8,128)(2,1)S(1)} %get-tuple-element.50), channel_id=1, source_target_pairs={{0,8},{8,0},{1,9},{9,1},{2,10},{10,2},{3,11},{11,3},{4,12},{12,4},... | collective-permute-start | bytes 798728 | tf_op jit(solution)/shard_map/ppermute | solution.py:526

commit v9 on v8

--- a/solution.py
+++ b/solution.py
@@ -241,17 +241,19 @@
     two = jnp.concatenate([part_bias[:, 0:TB], part_bias[:, TB:]], axis=0)
     high = two.astype(BF).astype(F32)
     tail = jnp.concatenate([high, two - high, jnp.zeros((12, TB), F32)], axis=0).astype(BF)
+    here = lax.axis_index("k") * NX
     for c in range(RB):
         rows = slice(c * F_LOC, (c + 1) * F_LOC)
         h, x = c // NX, c % NX
         dx_out[c] = dx_self[rows]
+        out[here + x, h] = dsum[rows]
         for k, part in enumerate((part_self, part_neigh)):
             at = k * NX + x
-            out[at, h] = dsum[rows]
             out[at, 2 + 2 * h] = part[rows, 0:TB].astype(BF)
             out[at, 3 + 2 * h] = part[rows, TB:].astype(BF)
-    for at in range(2 * NX):
-        out[at, 6] = tail
+    for x in range(NX):
+        out[NX - here + x, 0] = tail
+        out[NX - here + x, 1] = tail
 
 
 def parted(tail):
@@ -270,7 +272,7 @@
 def first_step_kernel(z_first, recv, out):
     places = out.shape[0]
     mine = 0 if z_first else NX
-    bias = parted(added(recv, 6))
+    bias = parted(sum(recv[NX - mine + x, 0].astype(F32) for x in range(NX)))
     for h in range(2):
         sums = [added(recv, 2 + 2 * h + n).astype(BF) for n in range(2)]
         at = 0 if z_first else NX * h
@@ -394,8 +396,9 @@
             out[at, 0:TB] = scaled[c, 0:16]
             out[at, TB:] = scaled[c, 16:32]
     k = lax.axis_index("k")
-    tail = jnp.where(k == 0, bias_sum[...], given[TILES_DEV]).astype(F32)
-    two = tail[0:2] + tail[2:4]
+    mine = bias_sum[...].astype(F32)
+    theirs = given[TILES_DEV].astype(F32)
+    two = (mine[0:2] + mine[2:4]) + (theirs[0:2] + theirs[2:4])
     grad_bias[...] = two / jnp.sqrt(jnp.mean(two * two) + EPS)
     for b in range(RB):
         dx_self = x[k * RB + b, 2 * F_LOC : 3 * F_LOC].astype(F32)
@@ -478,7 +481,7 @@
         dense_layer_kernel,
         (
             sds(cotangent.shape, BF),
-            sds((2 * NX, 7, F_LOC, TB), BF),
+            sds((2 * NX, 6, F_LOC, TB), BF),
             sds((RB, F_LOC, TB), BF),
         ),
         [VMEM] * 6,

time: 127 us -> 126 us (level)
  no operation moved by 1% of the time
where the time goes in v9:
time: 126 us
  blocking collectives  89.9 us (71%)
  starting transfers between devices  14.8 us (12%)
  Pallas kernels  12.4 us (10%)
  waiting for transfers between devices  6.04 us (5%)
  between operations  1.47 us (1%)
    all_to_all x5, blocking collectives, exchange(): return lax.all_to_all(array, axes, split_axis=0, concat_axis=0, tiled=True)  89.9 us
    ppermute x1, starting transfers between devices, local(): terms_other = lax.ppermute(terms, 'k', swap)  8.79 us
    all_to_all x1, waiting for transfers between devices, exchange(): return lax.all_to_all(array, axes, split_axis=0, concat_axis=0, tiled=True)  4.7 us
    all_to_all x1, starting transfers between devices, exchange(): return lax.all_to_all(array, axes, split_axis=0, concat_axis=0, tiled=True)  3.88 us
    pallas_call x1, Pallas kernels, tile_terms(): pl.pallas_call(terms_kernel, out_shape=sds((TILES_DEV + 1, F_LOC, TB), BF...  3.28 us
  transfers between devices with their start and end apart: 3, of which 2 were waited for; matrix products, arithmetic and copies ran while one was open for 0% of the time, Pallas kernels for 3%

profile of v9, /device:TPU:1, one launch (start us, length us, event | category | flops | bytes accessed | tf_op | source)
XLA Modules:
  0.0 125.7 jit_solution(17823500515923695142)
XLA Ops:
  1.3 0.0 copy-start.5
  1.3 3.3 %shard_map.137.own = bf16[65,16,128]{2,1,0:T(8,128)(2,1)} custom-call(s32[64]{0:T(128)} %src.1, s32[1,64]{1,0:T(1,128)} %bitcast.8, s32[1]{0:T(128)S(6)} %copy.19.count_h.count, bf16[16,1024]{1,0:T(8,128)(2,1)} %feats.1, bf16[64,128,128]{2,1,0:T(8,128)(2,1)} %vals.1), custom_call_target="tpu_custom_call" | custom-call | tf_op jit(solution)/shard_map/pallas_call | solution.py:107
  4.6 8.8 %collective-permute-start = (bf16[65,16,128]{2,1,0:T(8,128)(2,1)}, bf16[65,16,128]{2,1,0:T(8,128)(2,1)S(1)}, u32[]{:S(2)}, u32[]{:S(2)}) collective-permute-start(bf16[65,16,128]{2,1,0:T(8,128)(2,1)} %shard_map.137.own), channel_id=1, source_target_pairs={{0,8},{8,0},{1,9},{9,1},{2,10},{10,2},{3,11},{11,3},{4,12},{12,4},... | collective-permute-start | bytes 798728 | tf_op jit(solution)/shard_map/ppermute | solution.py:428
  13.4 0.0 copy-done.5
  13.4 0.0 copy-start.1
  13.4 0.9 copy-done.1
  14.3 0.0 copy-start.8
  14.3 1.1 shard_map.138.first
  15.5 0.0 copy-start.9
  15.5 0.0 collective-permute-done.other
  15.5 0.0 copy-done.8
  15.5 2.1 %shard_map.139 = (bf16[256,16,128]{2,1,0:T(8,128)(2,1)}, bf16[288,16,128]{2,1,0:T(8,128)(2,1)S(1)}, s32[1,128]{1,0:T(1,128)S(1)}) custom-call(f32[289,16,128]{2,1,0:T(8,128)S(1)} %shard_map.138.first, bf16[65,16,128]{2,1,0:T(8,128)(2,1)S(1)} %collective-permute-done.other, bf16[16,1024]{1,0:T(8,128)(2,1)S(1)} %copy-done.8), custom_call_target="tpu_custom_call" | custom-call | tf_op jit(solution)/shard_map/pallas_call | solution.py:436
  17.7 0.0 copy-done.9
  17.7 0.0 copy-start.2
  17.7 0.0 copy-start.3
  17.7 0.0 copy-start.4
  17.7 0.0 copy-start.7
  17.7 46.1 %conditional.2 = (bf16[8,32,128]{2,1,0:T(8,128)(2,1)S(1)}) conditional(s32[]{:T(128)} %convert_element_type.4, (bf16[288,16,128]{2,1,0:T(8,128)(2,1)S(1)}, s32[8,128]{1,0:T(8,128)S(1)}) %tuple.28, (bf16[256,16,128]{2,1,0:T(8,128)(2,1)}, bf16[16,1024]{1,0:T(8,128)(2,1)S(1)}, s32[8,128]{1,0:T(8,128)S(1)}) %tuple.29), branch_computations={%region_0.0_spmd, %region_1.0_spmd} | conditional | bytes 3407880 | solution.py:477
  17.7 23.8 %all_to_all.48.recv = bf16[8,36,16,128]{3,2,1,0:T(8,128)(2,1)S(1)} all-to-all(bf16[8,36,16,128]{3,2,1,0:T(8,128)(2,1)S(1)} %bitcast.12), channel_id=1, replica_groups=mesh['y'=8,'zl'=4,'k'=2,'zh'=2,'x'=4] {'zh','zl'}, dimensions={0} | all-to-all | bytes 2359296 | tf_op jit(solution)/shard_map/cond/branch_0_fun/all_to_all | solution.py:453
  41.5 0.1 branch_0_fun.4
  41.6 22.1 %all_to_all.49.recv = bf16[32,64,128]{2,1,0:T(8,128)(2,1)S(1)} all-to-all(bf16[32,64,128]{2,1,0:T(8,128)(2,1)S(1)} %branch_0_fun.4), channel_id=1, replica_groups=mesh['y'=8,'zl'=4,'k'=2,'zh'=2,'x'=4] {'y','x'}, dimensions={0} | all-to-all | bytes 1048576 | tf_op jit(solution)/shard_map/cond/branch_0_fun/all_to_all | solution.py:453
  63.8 0.0 copy-done.2
  63.8 0.0 copy-done.3
  63.9 0.0 copy-done.4
  63.9 0.0 copy-done.7
  63.9 0.9 shard_map.140
  64.8 9.2 %all_to_all.56 = bf16[8,6,16,128]{3,2,1,0:T(8,128)(2,1)S(1)} all-to-all(bf16[8,6,16,128]{3,2,1,0:T(8,128)(2,1)S(1)} %get-tuple-element.45), channel_id=1, replica_groups=mesh['y'=8,'zl'=4,'k'=2,'zh'=2,'x'=4] {'k','x'}, dimensions={0} | all-to-all | bytes 393216 | tf_op jit(solution)/shard_map/all_to_all | solution.py:453
  73.9 35.1 %conditional.3 = (bf16[280,16,128]{2,1,0:T(8,128)(2,1)S(1)}) conditional(s32[]{:T(128)} %convert_element_type.4, bf16[8,6,16,128]{3,2,1,0:T(8,128)(2,1)S(1)} %all_to_all.56, bf16[8,6,16,128]{3,2,1,0:T(8,128)(2,1)S(1)} %all_to_all.56), branch_computations={%region_2.0_spmd, %region_3.0_spmd} | conditional | bytes 3145736 | solution.py:516
  73.9 0.1 branch_0_fun.6
  74.0 13.5 %all_to_all.52.recv = bf16[8,13,16,128]{3,2,1,0:T(8,128)(2,1)S(1)} all-to-all(bf16[8,13,16,128]{3,2,1,0:T(8,128)(2,1)S(1)} %branch_0_fun.6), channel_id=1, replica_groups=mesh['y'=8,'zl'=4,'k'=2,'zh'=2,'x'=4] {'y'}, dimensions={0} | all-to-all | bytes 851968 | tf_op jit(solution)/shard_map/cond/branch_0_fun/all_to_all | solution.py:453
  87.5 0.1 branch_0_fun.7
  87.6 21.4 %all_to_all.53 = bf16[8,35,16,128]{3,2,1,0:T(8,128)(2,1)S(1)} all-to-all(bf16[8,35,16,128]{3,2,1,0:T(8,128)(2,1)S(1)} %branch_0_fun.7), channel_id=1, replica_groups=mesh['y'=8,'zl'=4,'k'=2,'zh'=2,'x'=4] {'zh','zl'}, dimensions={0} | all-to-all | bytes 2293760 | tf_op jit(solution)/shard_map/cond/branch_0_fun/all_to_all | solution.py:453
  109.0 0.0 copy-start
  109.0 0.0 copy-start.6
  109.0 0.7 shard_map.141
  109.7 3.9 %all-to-all-start.9 = ((bf16[16,48,128]{2,1,0:T(8,128)(2,1)}), bf16[16,48,128]{2,1,0:T(8,128)(2,1)S(1)}, u32[]{:S(2)}, u32[]{:S(2)}) async-start(bf16[16,48,128]{2,1,0:T(8,128)(2,1)} %get-tuple-element.47), calls=%async_computation.9 | async-start | bytes 393216 | tf_op jit(solution)/shard_map/all_to_all | solution.py:453
  113.6 1.4 %shard_map.142 = (bf16[64,16,128]{2,1,0:T(8,128)(2,1)S(1)}, bf16[65,16,128]{2,1,0:T(8,128)(2,1)S(1)}) custom-call(s32[64]{0:T(128)S(1)} %copy-done.5, s32[1]{0:T(128)S(6)} %copy.19.count_h.count, s32[1,128]{1,0:T(1,128)S(1)} %get-tuple-element.49.dest_other, bf16[280,16,128]{2,1,0:T(8,128)(2,1)S(1)} %get-tuple-element.57.recv, ...), custom_call_target="tpu_custom_call" | custom-call | bytes 7200000 | tf_op jit(solution)/shard_map/pallas_call | solution.py:523
  115.0 2.1 %collective-permute-start.1 = (bf16[65,16,128]{2,1,0:T(8,128)(2,1)S(1)}, bf16[65,16,128]{2,1,0:T(8,128)(2,1)S(1)}, u32[]{:S(2)}, u32[]{:S(2)}) collective-permute-start(bf16[65,16,128]{2,1,0:T(8,128)(2,1)S(1)} %get-tuple-element.50), channel_id=1, source_target_pairs={{0,8},{8,0},{1,9},{9,1},{2,10},{10,2},{3,11},{11,3},{4,12},{12,4},... | collective-permute-start | bytes 798728 | tf_op jit(solution)/shard_map/ppermute | solution.py:529
  117.1 1.3 %collective-permute-done.1.given = bf16[65,16,128]{2,1,0:T(8,128)(2,1)S(1)} collective-permute-done((bf16[65,16,128]{2,1,0:T(8,128)(2,1)S(1)}, bf16[65,16,128]{2,1,0:T(8,128)(2,1)S(1)}, u32[]{:S(2)}, u32[]{:S(2)}) %collective-permute-start.1) | collective-permute-done | bytes 266272 | tf_op jit(solution)/shard_map/ppermute | solution.py:529
  118.4 0.0 copy-done
  118.4 0.0 copy-done.6
  118.4 1.6 %shard_map.143.dx_neigh = f32[8,16,128]{2,1,0:T(8,128)S(1)} custom-call(s32[64]{0:T(128)S(1)} %copy-done.6, bf16[64,16,128]{2,1,0:T(8,128)(2,1)S(1)} %get-tuple-element.51.own, bf16[65,16,128]{2,1,0:T(8,128)(2,1)S(1)} %collective-permute-done.1.given, bf16[64,128,128]{2,1,0:T(8,128)(2,1)S(1)} %copy-done), custom_call_target="tpu_custom_call" | custom-call | bytes 7920000 | tf_op jit(solution)/shard_map/pallas_call | solution.py:375
  120.0 4.7 %all-to-all-done.9.x = bf16[16,48,128]{2,1,0:T(8,128)(2,1)S(1)} async-done(((bf16[16,48,128]{2,1,0:T(8,128)(2,1)}), bf16[16,48,128]{2,1,0:T(8,128)(2,1)S(1)}, u32[]{:S(2)}, u32[]{:S(2)}) %all-to-all-start.9) | async-done | bytes 196640 | tf_op jit(solution)/shard_map/all_to_all | solution.py:453
  124.7 0.9 shard_map.144
  (1 shorter events, 0.0 us)
Async XLA Ops:
  1.3 12.1 %copy-start.5 = (s32[64]{0:T(128)S(1)}, s32[64]{0:T(128)}, u32[]{:S(2)}) copy-start(s32[64]{0:T(128)} %dest_own.3) | copy-start | bytes 772
  4.6 10.9 %collective-permute-start = (bf16[65,16,128]{2,1,0:T(8,128)(2,1)}, bf16[65,16,128]{2,1,0:T(8,128)(2,1)S(1)}, u32[]{:S(2)}, u32[]{:S(2)}) collective-permute-start(bf16[65,16,128]{2,1,0:T(8,128)(2,1)} %shard_map.137.own), channel_id=1, source_target_pairs={{0,8},{8,0},{1,9},{9,1},{2,10},{10,2},{3,11},{11,3},{4,12},{12,4},... | collective-permute-start | bytes 798728 | tf_op jit(solution)/shard_map/ppermute | solution.py:428
  13.4 1.0 copy-start.1
  14.3 1.2 copy-start.8
  15.5 2.2 %copy-start.9 = (s32[1024]{0:T(1024)S(1)}, s32[1024]{0:T(1024)}, u32[]{:S(2)}) copy-start(s32[1024]{0:T(1024)} %param.19) | copy-start | bytes 12292
  17.7 46.2 %copy-start.2 = (bf16[128,256]{1,0:T(8,128)(2,1)S(1)}, bf16[128,256]{1,0:T(8,128)(2,1)}, u32[]{:S(2)}) copy-start(bf16[128,256]{1,0:T(8,128)(2,1)} %w_self.1) | copy-start | bytes 196612
  17.7 46.2 %copy-start.3 = (bf16[128,256]{1,0:T(8,128)(2,1)S(1)}, bf16[128,256]{1,0:T(8,128)(2,1)}, u32[]{:S(2)}) copy-start(bf16[128,256]{1,0:T(8,128)(2,1)} %w_neigh.1) | copy-start | bytes 196612
  17.7 46.2 %copy-start.4 = (bf16[256,128]{1,0:T(8,128)(2,1)S(1)}, bf16[256,128]{1,0:T(8,128)(2,1)}, u32[]{:S(2)}) copy-start(bf16[256,128]{1,0:T(8,128)(2,1)} %cot.1) | copy-start | bytes 196612
  17.7 46.2 %copy-start.7 = (f32[256]{0:T(256)S(1)}, f32[256]{0:T(256)}, u32[]{:S(2)}) copy-start(f32[256]{0:T(256)} %param.22) | copy-start | bytes 3076
  109.0 9.4 %copy-start = (bf16[64,128,128]{2,1,0:T(8,128)(2,1)S(1)}, bf16[64,128,128]{2,1,0:T(8,128)(2,1)}, u32[]{:S(2)}) copy-start(bf16[64,128,128]{2,1,0:T(8,128)(2,1)} %vals.1) | copy-start | bytes 6291460
  109.0 9.4 %copy-start.6 = (s32[64]{0:T(128)S(1)}, s32[64]{0:T(128)}, u32[]{:S(2)}) copy-start(s32[64]{0:T(128)} %src.1) | copy-start | bytes 772
  109.7 15.0 %all-to-all-start.9 = ((bf16[16,48,128]{2,1,0:T(8,128)(2,1)}), bf16[16,48,128]{2,1,0:T(8,128)(2,1)S(1)}, u32[]{:S(2)}, u32[]{:S(2)}) async-start(bf16[16,48,128]{2,1,0:T(8,128)(2,1)} %get-tuple-element.47), calls=%async_computation.9 | async-start | bytes 393216 | tf_op jit(solution)/shard_map/all_to_all | solution.py:453
  115.0 3.4 %collective-permute-start.1 = (bf16[65,16,128]{2,1,0:T(8,128)(2,1)S(1)}, bf16[65,16,128]{2,1,0:T(8,128)(2,1)S(1)}, u32[]{:S(2)}, u32[]{:S(2)}) collective-permute-start(bf16[65,16,128]{2,1,0:T(8,128)(2,1)S(1)} %get-tuple-element.50), channel_id=1, source_target_pairs={{0,8},{8,0},{1,9},{9,1},{2,10},{10,2},{3,11},{11,3},{4,12},{12,4},... | collective-permute-start | bytes 798728 | tf_op jit(solution)/shard_map/ppermute | solution.py:529

commit v10 on v9

--- a/solution.py
+++ b/solution.py
@@ -14,7 +14,7 @@
 F_LOC = 16
 Y = 8
 NX = 4
-STEP = 16
+STEP = 32
 EXTRA = 3
 
 EPS = 1e-06

time: 126 us -> 126 us (level)
  no operation moved by 1% of the time
where the time goes in v10:
time: 126 us; the launch traced here: 125 us
  blocking collectives  89.9 us (71%)
  starting transfers between devices  14.8 us (12%)
  Pallas kernels  11.8 us (9%)
  waiting for transfers between devices  6.29 us (5%)
  between operations  1.47 us (1%)
    all_to_all x5, blocking collectives, exchange(): return lax.all_to_all(array, axes, split_axis=0, concat_axis=0, tiled=True)  89.9 us
    ppermute x1, starting transfers between devices, local(): terms_other = lax.ppermute(terms, 'k', swap)  8.78 us
    all_to_all x1, waiting for transfers between devices, exchange(): return lax.all_to_all(array, axes, split_axis=0, concat_axis=0, tiled=True)  4.95 us
    all_to_all x1, starting transfers between devices, exchange(): return lax.all_to_all(array, axes, split_axis=0, concat_axis=0, tiled=True)  3.88 us
    pallas_call x1, Pallas kernels, tile_terms(): pl.pallas_call(terms_kernel, out_shape=sds((TILES_DEV + 1, F_LOC, TB), BF...  2.94 us
  transfers between devices with their start and end apart: 3, of which 2 were waited for; matrix products, arithmetic and copies ran while one was open for 0% of the time, Pallas kernels for 3%

profile of v10, /device:TPU:1, one launch (start us, length us, event | category | flops | bytes accessed | tf_op | source)
XLA Modules:
  0.0 125.3 jit_solution(5953390793149661305)
XLA Ops:
  1.3 0.0 copy-start.5
  1.3 2.9 %shard_map.137.own = bf16[65,16,128]{2,1,0:T(8,128)(2,1)} custom-call(s32[64]{0:T(128)} %src.1, s32[1,64]{1,0:T(1,128)} %bitcast.8, s32[1]{0:T(128)S(6)} %copy.19.count_h.count, bf16[16,1024]{1,0:T(8,128)(2,1)} %feats.1, bf16[64,128,128]{2,1,0:T(8,128)(2,1)} %vals.1), custom_call_target="tpu_custom_call" | custom-call | tf_op jit(solution)/shard_map/pallas_call | solution.py:107
  4.2 8.8 %collective-permute-start = (bf16[65,16,128]{2,1,0:T(8,128)(2,1)}, bf16[65,16,128]{2,1,0:T(8,128)(2,1)S(1)}, u32[]{:S(2)}, u32[]{:S(2)}) collective-permute-start(bf16[65,16,128]{2,1,0:T(8,128)(2,1)} %shard_map.137.own), channel_id=1, source_target_pairs={{0,8},{8,0},{1,9},{9,1},{2,10},{10,2},{3,11},{11,3},{4,12},{12,4},... | collective-permute-start | bytes 798728 | tf_op jit(solution)/shard_map/ppermute | solution.py:428
  13.0 0.0 copy-done.5
  13.0 0.0 copy-start.1
  13.1 0.9 copy-done.1
  14.0 0.0 copy-start.8
  14.0 1.1 shard_map.138.first
  15.1 0.0 copy-start.9
  15.1 0.0 collective-permute-done.other
  15.1 0.0 copy-done.8
  15.2 2.2 %shard_map.139 = (bf16[256,16,128]{2,1,0:T(8,128)(2,1)}, bf16[288,16,128]{2,1,0:T(8,128)(2,1)S(1)}, s32[1,128]{1,0:T(1,128)S(1)}) custom-call(f32[289,16,128]{2,1,0:T(8,128)S(1)} %shard_map.138.first, bf16[65,16,128]{2,1,0:T(8,128)(2,1)S(1)} %collective-permute-done.other, bf16[16,1024]{1,0:T(8,128)(2,1)S(1)} %copy-done.8), custom_call_target="tpu_custom_call" | custom-call | tf_op jit(solution)/shard_map/pallas_call | solution.py:436
  17.3 0.0 copy-done.9
  17.3 0.0 copy-start.2
  17.3 0.0 copy-start.3
  17.3 0.0 copy-start.4
  17.4 0.0 copy-start.7
  17.4 46.1 %conditional.2 = (bf16[8,32,128]{2,1,0:T(8,128)(2,1)S(1)}) conditional(s32[]{:T(128)} %convert_element_type.4, (bf16[288,16,128]{2,1,0:T(8,128)(2,1)S(1)}, s32[8,128]{1,0:T(8,128)S(1)}) %tuple.28, (bf16[256,16,128]{2,1,0:T(8,128)(2,1)}, bf16[16,1024]{1,0:T(8,128)(2,1)S(1)}, s32[8,128]{1,0:T(8,128)S(1)}) %tuple.29), branch_computations={%region_0.0_spmd, %region_1.0_spmd} | conditional | bytes 3407880 | solution.py:477
  17.4 23.8 %all_to_all.48.recv = bf16[8,36,16,128]{3,2,1,0:T(8,128)(2,1)S(1)} all-to-all(bf16[8,36,16,128]{3,2,1,0:T(8,128)(2,1)S(1)} %bitcast.12), channel_id=1, replica_groups=mesh['y'=8,'zl'=4,'k'=2,'zh'=2,'x'=4] {'zh','zl'}, dimensions={0} | all-to-all | bytes 2359296 | tf_op jit(solution)/shard_map/cond/branch_0_fun/all_to_all | solution.py:453
  41.1 0.1 branch_0_fun.4
  41.3 22.1 %all_to_all.49.recv = bf16[32,64,128]{2,1,0:T(8,128)(2,1)S(1)} all-to-all(bf16[32,64,128]{2,1,0:T(8,128)(2,1)S(1)} %branch_0_fun.4), channel_id=1, replica_groups=mesh['y'=8,'zl'=4,'k'=2,'zh'=2,'x'=4] {'y','x'}, dimensions={0} | all-to-all | bytes 1048576 | tf_op jit(solution)/shard_map/cond/branch_0_fun/all_to_all | solution.py:453
  63.5 0.0 copy-done.2
  63.5 0.0 copy-done.3
  63.5 0.0 copy-done.4
  63.5 0.0 copy-done.7
  63.5 0.9 shard_map.140
  64.4 9.2 %all_to_all.56 = bf16[8,6,16,128]{3,2,1,0:T(8,128)(2,1)S(1)} all-to-all(bf16[8,6,16,128]{3,2,1,0:T(8,128)(2,1)S(1)} %get-tuple-element.45), channel_id=1, replica_groups=mesh['y'=8,'zl'=4,'k'=2,'zh'=2,'x'=4] {'k','x'}, dimensions={0} | all-to-all | bytes 393216 | tf_op jit(solution)/shard_map/all_to_all | solution.py:453
  73.6 35.1 %conditional.3 = (bf16[280,16,128]{2,1,0:T(8,128)(2,1)S(1)}) conditional(s32[]{:T(128)} %convert_element_type.4, bf16[8,6,16,128]{3,2,1,0:T(8,128)(2,1)S(1)} %all_to_all.56, bf16[8,6,16,128]{3,2,1,0:T(8,128)(2,1)S(1)} %all_to_all.56), branch_computations={%region_2.0_spmd, %region_3.0_spmd} | conditional | bytes 3145736 | solution.py:516
  73.6 0.1 branch_0_fun.6
  73.6 13.5 %all_to_all.52.recv = bf16[8,13,16,128]{3,2,1,0:T(8,128)(2,1)S(1)} all-to-all(bf16[8,13,16,128]{3,2,1,0:T(8,128)(2,1)S(1)} %branch_0_fun.6), channel_id=1, replica_groups=mesh['y'=8,'zl'=4,'k'=2,'zh'=2,'x'=4] {'y'}, dimensions={0} | all-to-all | bytes 851968 | tf_op jit(solution)/shard_map/cond/branch_0_fun/all_to_all | solution.py:453
  87.1 0.1 branch_0_fun.7
  87.3 21.4 %all_to_all.53 = bf16[8,35,16,128]{3,2,1,0:T(8,128)(2,1)S(1)} all-to-all(bf16[8,35,16,128]{3,2,1,0:T(8,128)(2,1)S(1)} %branch_0_fun.7), channel_id=1, replica_groups=mesh['y'=8,'zl'=4,'k'=2,'zh'=2,'x'=4] {'zh','zl'}, dimensions={0} | all-to-all | bytes 2293760 | tf_op jit(solution)/shard_map/cond/branch_0_fun/all_to_all | solution.py:453
  108.7 0.0 copy-start
  108.7 0.0 copy-start.6
  108.7 0.7 shard_map.141
  109.4 3.9 %all-to-all-start.9 = ((bf16[16,48,128]{2,1,0:T(8,128)(2,1)}), bf16[16,48,128]{2,1,0:T(8,128)(2,1)S(1)}, u32[]{:S(2)}, u32[]{:S(2)}) async-start(bf16[16,48,128]{2,1,0:T(8,128)(2,1)} %get-tuple-element.47), calls=%async_computation.9 | async-start | bytes 393216 | tf_op jit(solution)/shard_map/all_to_all | solution.py:453
  113.2 1.4 %shard_map.142 = (bf16[64,16,128]{2,1,0:T(8,128)(2,1)S(1)}, bf16[65,16,128]{2,1,0:T(8,128)(2,1)S(1)}) custom-call(s32[64]{0:T(128)S(1)} %copy-done.5, s32[1]{0:T(128)S(6)} %copy.19.count_h.count, s32[1,128]{1,0:T(1,128)S(1)} %get-tuple-element.49.dest_other, bf16[280,16,128]{2,1,0:T(8,128)(2,1)S(1)} %get-tuple-element.57.recv, ...), custom_call_target="tpu_custom_call" | custom-call | bytes 7200000 | tf_op jit(solution)/shard_map/pallas_call | solution.py:523
  114.6 2.1 %collective-permute-start.1 = (bf16[65,16,128]{2,1,0:T(8,128)(2,1)S(1)}, bf16[65,16,128]{2,1,0:T(8,128)(2,1)S(1)}, u32[]{:S(2)}, u32[]{:S(2)}) collective-permute-start(bf16[65,16,128]{2,1,0:T(8,128)(2,1)S(1)} %get-tuple-element.50), channel_id=1, source_target_pairs={{0,8},{8,0},{1,9},{9,1},{2,10},{10,2},{3,11},{11,3},{4,12},{12,4},... | collective-permute-start | bytes 798728 | tf_op jit(solution)/shard_map/ppermute | solution.py:529
  116.7 1.3 %collective-permute-done.1.given = bf16[65,16,128]{2,1,0:T(8,128)(2,1)S(1)} collective-permute-done((bf16[65,16,128]{2,1,0:T(8,128)(2,1)S(1)}, bf16[65,16,128]{2,1,0:T(8,128)(2,1)S(1)}, u32[]{:S(2)}, u32[]{:S(2)}) %collective-permute-start.1) | collective-permute-done | bytes 266272 | tf_op jit(solution)/shard_map/ppermute | solution.py:529
  118.1 0.0 copy-done
  118.1 0.0 copy-done.6
  118.1 1.4 %shard_map.143.dx_neigh = f32[8,16,128]{2,1,0:T(8,128)S(1)} custom-call(s32[64]{0:T(128)S(1)} %copy-done.6, bf16[64,16,128]{2,1,0:T(8,128)(2,1)S(1)} %get-tuple-element.51.own, bf16[65,16,128]{2,1,0:T(8,128)(2,1)S(1)} %collective-permute-done.1.given, bf16[64,128,128]{2,1,0:T(8,128)(2,1)S(1)} %copy-done), custom_call_target="tpu_custom_call" | custom-call | bytes 7920000 | tf_op jit(solution)/shard_map/pallas_call | solution.py:375
  119.4 4.9 %all-to-all-done.9.x = bf16[16,48,128]{2,1,0:T(8,128)(2,1)S(1)} async-done(((bf16[16,48,128]{2,1,0:T(8,128)(2,1)}), bf16[16,48,128]{2,1,0:T(8,128)(2,1)S(1)}, u32[]{:S(2)}, u32[]{:S(2)}) %all-to-all-start.9) | async-done | bytes 196640 | tf_op jit(solution)/shard_map/all_to_all | solution.py:453
  124.4 0.9 shard_map.144
  (1 shorter events, 0.0 us)
Async XLA Ops:
  1.3 11.8 %copy-start.5 = (s32[64]{0:T(128)S(1)}, s32[64]{0:T(128)}, u32[]{:S(2)}) copy-start(s32[64]{0:T(128)} %dest_own.3) | copy-start | bytes 772
  4.2 10.9 %collective-permute-start = (bf16[65,16,128]{2,1,0:T(8,128)(2,1)}, bf16[65,16,128]{2,1,0:T(8,128)(2,1)S(1)}, u32[]{:S(2)}, u32[]{:S(2)}) collective-permute-start(bf16[65,16,128]{2,1,0:T(8,128)(2,1)} %shard_map.137.own), channel_id=1, source_target_pairs={{0,8},{8,0},{1,9},{9,1},{2,10},{10,2},{3,11},{11,3},{4,12},{12,4},... | collective-permute-start | bytes 798728 | tf_op jit(solution)/shard_map/ppermute | solution.py:428
  13.0 1.0 copy-start.1
  14.0 1.2 copy-start.8
  15.1 2.2 %copy-start.9 = (s32[1024]{0:T(1024)S(1)}, s32[1024]{0:T(1024)}, u32[]{:S(2)}) copy-start(s32[1024]{0:T(1024)} %param.19) | copy-start | bytes 12292
  17.3 46.2 %copy-start.2 = (bf16[128,256]{1,0:T(8,128)(2,1)S(1)}, bf16[128,256]{1,0:T(8,128)(2,1)}, u32[]{:S(2)}) copy-start(bf16[128,256]{1,0:T(8,128)(2,1)} %w_self.1) | copy-start | bytes 196612
  17.3 46.2 %copy-start.3 = (bf16[128,256]{1,0:T(8,128)(2,1)S(1)}, bf16[128,256]{1,0:T(8,128)(2,1)}, u32[]{:S(2)}) copy-start(bf16[128,256]{1,0:T(8,128)(2,1)} %w_neigh.1) | copy-start | bytes 196612
  17.3 46.2 %copy-start.4 = (bf16[256,128]{1,0:T(8,128)(2,1)S(1)}, bf16[256,128]{1,0:T(8,128)(2,1)}, u32[]{:S(2)}) copy-start(bf16[256,128]{1,0:T(8,128)(2,1)} %cot.1) | copy-start | bytes 196612
  17.4 46.2 %copy-start.7 = (f32[256]{0:T(256)S(1)}, f32[256]{0:T(256)}, u32[]{:S(2)}) copy-start(f32[256]{0:T(256)} %param.22) | copy-start | bytes 3076
  108.7 9.4 %copy-start = (bf16[64,128,128]{2,1,0:T(8,128)(2,1)S(1)}, bf16[64,128,128]{2,1,0:T(8,128)(2,1)}, u32[]{:S(2)}) copy-start(bf16[64,128,128]{2,1,0:T(8,128)(2,1)} %vals.1) | copy-start | bytes 6291460
  108.7 9.4 %copy-start.6 = (s32[64]{0:T(128)S(1)}, s32[64]{0:T(128)}, u32[]{:S(2)}) copy-start(s32[64]{0:T(128)} %src.1) | copy-start | bytes 772
  109.4 15.0 %all-to-all-start.9 = ((bf16[16,48,128]{2,1,0:T(8,128)(2,1)}), bf16[16,48,128]{2,1,0:T(8,128)(2,1)S(1)}, u32[]{:S(2)}, u32[]{:S(2)}) async-start(bf16[16,48,128]{2,1,0:T(8,128)(2,1)} %get-tuple-element.47), calls=%async_computation.9 | async-start | bytes 393216 | tf_op jit(solution)/shard_map/all_to_all | solution.py:453
  114.6 3.4 %collective-permute-start.1 = (bf16[65,16,128]{2,1,0:T(8,128)(2,1)S(1)}, bf16[65,16,128]{2,1,0:T(8,128)(2,1)S(1)}, u32[]{:S(2)}, u32[]{:S(2)}) collective-permute-start(bf16[65,16,128]{2,1,0:T(8,128)(2,1)S(1)} %get-tuple-element.50), channel_id=1, source_target_pairs={{0,8},{8,0},{1,9},{9,1},{2,10},{10,2},{3,11},{11,3},{4,12},{12,4},... | collective-permute-start | bytes 798728 | tf_op jit(solution)/shard_map/ppermute | solution.py:529
